TPU v7x, 32 devices: a whole 2x2x4 slice. The times are simulated.
32 devices in a mesh: dp: 8 (over y, x, core), mp: 4 (over z).
Axes of the slice: x: 2, y: 2, z: 4, core: 2. Of those that a mesh axis runs over, the one named last changes fastest.
Arguments:
- tokens: bfloat16 [96, 160, 768], P('dp', 'mp'), may hold values from -6 to 6
- word_len: int32 [96], P('dp'), may hold values from 1 to 60, as said below
- region_count: int32 [96], P('dp'), may hold values from 10 to 100, as said below
- w_qkv: bfloat16 [3, 768, 768], P(None, None, 'mp'), may hold values from -0.3125 to 0.3125
- qv_bias: bfloat16 [2, 768], P(None, 'mp'), may hold values from -3 to 3
- w_out: bfloat16 [768, 768], P('mp'), may hold values from -0.625 to 0.625
- out_bias: bfloat16 [768], replicated, may hold values from -3 to 3
- norm1_gain: bfloat16 [768], replicated, may hold values from 0.5 to 1.5
- norm1_bias: bfloat16 [768], replicated, may hold values from -3 to 3
- w_in: bfloat16 [768, 3072], P(None, 'mp'), may hold values from -0.21875 to 0.21875
- in_bias: bfloat16 [3072], P('mp'), may hold values from -3 to 3
- w_down: bfloat16 [3072, 768], P('mp'), may hold values from -0.15625 to 0.15625
- down_bias: bfloat16 [768], replicated, may hold values from -3 to 3
- norm2_gain: bfloat16 [768], replicated, may hold values from 0.5 to 1.5
- norm2_bias: bfloat16 [768], replicated, may hold values from -3 to 3
- cotangent: bfloat16 [96, 160, 768], P('dp', 'mp'), may hold values from -6 to 6
Outputs:
- layer_out: bfloat16 [96, 160, 768], P('dp', 'mp')
- grad_input: float32 [96, 160, 768], P('dp', 'mp')
- grad_qkv: float32 [3, 768, 768], P(None, None, 'mp')
- grad_qv_bias: float32 [2, 768], P(None, 'mp')
- grad_out: float32 [768, 768], P('mp')
- grad_out_bias: float32 [768], replicated
- grad_norm1_gain: float32 [768], replicated
- grad_norm1_bias: float32 [768], replicated
- grad_in: float32 [768, 3072], P(None, 'mp')
- grad_in_bias: float32 [3072], P('mp')
- grad_down: float32 [3072, 768], P('mp')
- grad_down_bias: float32 [768], replicated
- grad_norm2_gain: float32 [768], replicated
- grad_norm2_bias: float32 [768], replicated
Inputs may be any that keep to these rules, and one draw needn't show every extreme that they name: `word_len`: words of a pair; in each aligned block of 12 pairs one pair, chosen at random, has 60 words and 100 regions. `region_count`: regions of a pair.
All inputs are finite; a program needn't handle non-finite values.
Results may differ from a plain program's by a relative error of at most 0.014.
The roundings to bfloat16 on the way count: a program that leaves them out, or rounds other values in their place, can miss the bound.
Values may be sent and summed in bfloat16 or wider, within the bound.
No kernel may reach another device: no remote copies, remote signals or barrier semaphores. Data moves between devices by JAX's collectives and lax.ppermute only.
A program may use at most 128 MiB of HBM per device.

v0:
```python
from functools import partial

import jax
import jax.numpy as jnp
from jax import lax
from jax.experimental import pallas as pl
from jax.experimental.pallas import tpu as pltpu
from jax.sharding import PartitionSpec as P

HEAD = 64
WORDS = 60
EPSILON = 1e-05
SQRT_HALF = 0.7071067811865476
DENSITY = 0.3989422804014327
F32 = jnp.float32
BF16 = jnp.bfloat16
MIB = 1024 * 1024


def dot(one, two, one_axis, two_axis):
    return lax.dot_general(
        one, two, (((one_axis,), (two_axis,)), ((), ())), preferred_element_type=F32
    )


def normalize(total, gain, shift):
    centered = total - jnp.mean(total, axis=-1, keepdims=True)
    inv_scale = lax.rsqrt(jnp.mean(centered * centered, axis=-1, keepdims=True) + EPSILON)
    normed = centered * inv_scale
    return normed * gain + shift, normed, inv_scale


def normalize_back(upstream, normed, inv_scale, gain):
    scaled_up = upstream * gain
    mean_one = jnp.mean(scaled_up, axis=-1, keepdims=True)
    mean_two = jnp.mean(scaled_up * normed, axis=-1, keepdims=True)
    return inv_scale * (scaled_up - mean_one - normed * mean_two)


def column_sum(array):
    return jnp.sum(array, axis=0, keepdims=True)


def head_stack(array, heads):
    head = lax.broadcasted_iota(jnp.int32, array.shape, 1) // HEAD
    zero = jnp.zeros_like(array)
    return jnp.concatenate([jnp.where(head == h, array, zero) for h in range(heads)], axis=0)


def head_pick(stacked, heads):
    rows = stacked.shape[0] // heads
    head = lax.broadcasted_iota(jnp.int32, (rows, stacked.shape[1]), 1) // HEAD
    total = stacked[:rows]
    for h in range(1, heads):
        total = jnp.where(head == h, stacked[h * rows : (h + 1) * rows], total)
    return total


def head_weights(first, here_ref, own_ref, one_ref, two_ref):
    low = here_ref[0] == 0
    half = one_ref.shape[1]
    one, two = one_ref[0], two_ref[0]
    return (
        jnp.where(first, own_ref[:half], jnp.where(low, one, two)),
        jnp.where(first, own_ref[half:], jnp.where(low, two, one)),
    )


def attention_kernel(
    pairs, here_ref, x_ref, own_qk, qk_one, qk_two, own_vo, vo_one, vo_two, small_ref, valid_ref, vectors_ref,
    q_ref, k_ref, v_ref, weights_ref, context_ref, low_ref, normed_ref, scale_ref, total_ref,
):
    step = pl.program_id(0)
    cols = q_ref.shape[2]
    heads = cols // HEAD
    slots = x_ref.shape[0] // pairs
    x = x_ref[...]
    w_q, w_k = head_weights(step == 0, here_ref, own_qk, qk_one, qk_two)
    w_v, w_o = head_weights(step == 0, here_ref, own_vo, vo_one, vo_two)
    q_ref[0] = (dot(x, w_q, 1, 1) + small_ref[0, 0:1, :cols]).astype(BF16)
    k_ref[0] = dot(x, w_k, 1, 1).astype(BF16)
    v_ref[0] = (dot(x, w_v, 1, 1) + small_ref[0, 1:2, :cols]).astype(BF16)
    for p in range(pairs):
        rows = slice(p * slots, (p + 1) * slots)
        scores = dot(head_stack(q_ref[0, rows], heads), k_ref[0, rows], 1, 1) * HEAD ** (-0.5)
        scores = jnp.where(valid_ref[p] > 0.5, scores, -1e30)
        exp_scores = jnp.exp(scores - jnp.max(scores, axis=-1, keepdims=True))
        weights = exp_scores / jnp.sum(exp_scores, axis=-1, keepdims=True)
        weights_ref[0, p] = weights
        mixed = dot(weights.astype(BF16), v_ref[0, rows], 1, 0)
        context_ref[0, rows] = head_pick(mixed, heads).astype(BF16)
    branch = dot(context_ref[0], w_o, 1, 0)

    @pl.when(step == 0)
    def _():
        total_ref[...] = branch

    @pl.when(step > 0)
    def _():
        total_ref[...] += branch

    @pl.when(step == pl.num_programs(0) - 1)
    def _():
        first_sum = total_ref[...] + vectors_ref[0:1] + x.astype(F32)
        hidden, normed, scale = normalize(first_sum, vectors_ref[1:2], vectors_ref[2:3])
        low_ref[...] = hidden.astype(BF16)
        normed_ref[...] = normed
        scale_ref[...] = scale


def blocks_of(units):
    size = min(256, units)
    return [(start, min(start + size, units)) for start in range(0, units, size)]


class Copies:
    def __init__(self, sems):
        self.sems, self.used = sems, 0

    def start(self, *pairs):
        copies = []
        for source, target in pairs:
            copies.append(pltpu.make_async_copy(source, target, self.sems.at[self.used]))
            copies[-1].start()
            self.used += 1
        return copies


def wait_all(copies):
    for copy in copies:
        copy.wait()


def halves_of(half, start, stop):
    parts = []
    if start < half:
        parts.append((0, start, min(stop, half)))
    if stop > half:
        parts.append((1, max(start - half, 0), stop - half))
    return parts


def own_units(core, half, which, first, last):
    side = core if which == 0 else 1 - core
    return pl.ds(pl.multiple_of(side * half + first, 128), last - first)


def join_rows(refs):
    pairs = refs[0].shape[0]
    return jnp.concatenate([ref[p].astype(F32) for p in range(pairs) for ref in refs], axis=0)


def leave_rows(array, refs):
    pairs, rows = refs[0].shape[:2]
    for p in range(pairs):
        for j, ref in enumerate(refs):
            start = (p * len(refs) + j) * rows
            ref[p] = array[start : start + rows].astype(BF16)


def ffn_kernel(
    count, here_ref, low_hbm, normed_hbm, w_in_hbm, in_one, in_two, w_down_hbm, down_one, down_two, small_ref,
    vectors_ref, *refs,
):
    cot_hbm, out_refs = refs[:count], refs[count : 2 * count]
    (
        delta_hbm, pre_grad_hbm, in_keep_hbm, in_send_hbm, down_keep_hbm, down_send_hbm, sum_in_ref, sums_ref,
        low_ref, normed_ref, w_in_ref, w_down_ref, cot_ref, act_ref, slope_ref, total_ref, delta_ref, pre_grad_ref,
        in_keep_ref, in_send_ref, down_keep_ref, down_send_ref, ffn_low_ref, sems,
    ) = refs[2 * count :]
    core = here_ref[0]
    half = in_one.shape[1]
    copies_ = Copies(sems)
    start, wait = copies_.start, wait_all

    halves = partial(halves_of, half)
    own = partial(own_units, core, half)

    def down_rows(slot, first, start_, stop):
        if first:
            parts = [w_down_ref[own(w, a, b)] for w, a, b in halves(start_, stop)]
        else:
            parts = [(down_one, down_two)[w][slot - 1, a:b] for w, a, b in halves(start_, stop)]
        return jnp.concatenate(parts, axis=0)

    def forward(slot, mine):
        low = low_ref[...]
        branch = None
        for first, last in blocks_of(2 * half):
            parts = halves(first, last)
            if mine:
                w_in = jnp.concatenate([w_in_ref[:, own(*p)] for p in parts], axis=1)
                pre_act = dot(low, w_in, 1, 0)
            else:
                w_in = jnp.concatenate([(in_one, in_two)[w][slot - 1, a:b] for w, a, b in parts], axis=0)
                pre_act = dot(low, w_in, 1, 1)
            bias = jnp.concatenate([small_ref[slot, 2:3, own(*p)] for p in parts], axis=1)
            pre_act = pre_act + bias
            share = 0.5 * (1.0 + lax.erf(pre_act * SQRT_HALF))
            act = (pre_act * share).astype(BF16)
            act_ref[slot, :, first:last] = act
            slope_ref[slot, :, first:last] = share + pre_act * (DENSITY * jnp.exp(-0.5 * pre_act * pre_act))
            term = dot(act, down_rows(slot, mine, first, last), 1, 0)
            branch = term if branch is None else branch + term
        total_ref[...] += branch

    low_copies = start((low_hbm, low_ref))
    own_copies = start((w_in_hbm, w_in_ref), (w_down_hbm, w_down_ref))
    later_copies = start((normed_hbm, normed_ref), *[(cot_hbm[k], cot_ref.at[k]) for k in range(count)])
    total_ref[...] = jnp.zeros_like(total_ref)
    wait(low_copies)
    for slot in range(1, count):
        forward(slot, False)
    wait(own_copies)
    forward(0, True)
    wait(later_copies)

    hidden = normed_ref[...] * vectors_ref[1:2] + vectors_ref[2:3]
    second = total_ref[...] + vectors_ref[3:4] + hidden
    gain = vectors_ref[4:5]
    output, normed, scale = normalize(second, gain, vectors_ref[5:6])
    leave_rows(output, out_refs)
    upstream = join_rows([cot_ref.at[k] for k in range(count)])
    delta = normalize_back(upstream, normed, scale, gain)
    delta_ref[...] = delta
    leaving = start((delta_ref, delta_hbm))
    sums_ref[...] = jnp.zeros_like(sums_ref)
    sums_ref[0:1] = column_sum(upstream * normed)
    sums_ref[1:2] = column_sum(upstream)
    sums_ref[2:3] = column_sum(delta)
    ffn_low_ref[...] = delta.astype(BF16)
    leavers = (
        (pre_grad_ref, pre_grad_hbm),
        (down_send_ref, down_send_hbm),
        (down_keep_ref, down_keep_hbm),
        (in_send_ref, in_send_hbm),
        (in_keep_ref, in_keep_hbm),
    )
    base = copies_.used

    def leave(slot, i):
        source, target = leavers[i]
        return pltpu.make_async_copy(source.at[slot], target.at[slot], sems.at[base + len(leavers) * slot + i])

    def backward(slot, mine):
        ffn_low, low = ffn_low_ref[...], low_ref[...]
        for first, last in blocks_of(2 * half):
            act_grad = dot(ffn_low, down_rows(slot, mine, first, last), 1, 1)
            pre_grad_ref[slot, :, first:last] = (act_grad * slope_ref[slot, :, first:last]).astype(BF16)
        leave(slot, 0).start()
        down_send_ref[slot] = dot(act_ref[slot, :, half:], ffn_low, 0, 0).astype(BF16)
        leave(slot, 1).start()
        down_keep_ref[slot] = dot(act_ref[slot, :, :half], ffn_low, 0, 0).astype(BF16)
        leave(slot, 2).start()
        one, two = pre_grad_ref[slot, :, :half], pre_grad_ref[slot, :, half:]
        in_send_ref[slot] = dot(two, low, 0, 0).astype(BF16)
        leave(slot, 3).start()
        in_keep_ref[slot] = dot(one, low, 0, 0).astype(BF16)
        leave(slot, 4).start()
        natural = slot ^ here_ref[1]
        sum_in_ref[natural, :, own(0, 0, half)] = column_sum(one.astype(F32))
        sum_in_ref[natural, :, own(1, 0, half)] = column_sum(two.astype(F32))

    backward(0, True)
    lax.fori_loop(1, count, lambda slot, _: (backward(slot, False), 0)[1], 0)
    wait(leaving)
    for slot in range(count):
        for i in range(len(leavers)):
            leave(slot, i).wait()


def ffn_back_kernel(
    count, here_ref, pre_grad_hbm, w_in_hbm, in_one, in_two, delta_hbm, normed_hbm, scale_ref, vectors_ref,
    delta_attn_hbm, attn_low_ref, sums_ref, pre_grad_ref, w_in_ref, delta_ref, normed_ref, total_ref, sems,
):
    core = here_ref[0]
    half = in_one.shape[1]
    copies = Copies(sems)
    base = copies.used
    copies.used += count

    def load(slot):
        return pltpu.make_async_copy(pre_grad_hbm.at[slot], pre_grad_ref.at[slot], sems.at[base + slot])

    for slot in list(range(1, count)) + [0]:
        load(slot).start()
    w_copies = copies.start((w_in_hbm, w_in_ref))
    norm_copies = copies.start((delta_hbm, delta_ref), (normed_hbm, normed_ref))

    def add(slot, mine):
        load(slot).wait()
        branch = None
        for a, b in blocks_of(2 * half):
            pre_grad = pre_grad_ref[slot, :, a:b]
            parts = halves_of(half, a, b)
            if mine:
                w_in = jnp.concatenate([w_in_ref[:, own_units(core, half, *p)] for p in parts], axis=1)
                term = dot(pre_grad, w_in, 1, 1)
            else:
                w_in = jnp.concatenate([(in_one, in_two)[w][slot - 1, c:d] for w, c, d in parts], axis=0)
                term = dot(pre_grad, w_in, 1, 0)
            branch = term if branch is None else branch + term
        total_ref[...] += branch

    total_ref[...] = jnp.zeros_like(total_ref)
    lax.fori_loop(1, count, lambda slot, _: (add(slot, False), 0)[1], 0)
    wait_all(w_copies)
    add(0, True)
    wait_all(norm_copies)
    hidden_grad = total_ref[...] + delta_ref[...]
    normed = normed_ref[...]
    delta = normalize_back(hidden_grad, normed, scale_ref[...], vectors_ref[1:2])
    total_ref[...] = delta
    leaving = copies.start((total_ref, delta_attn_hbm))
    attn_low_ref[...] = delta.astype(BF16)
    sums_ref[...] = jnp.zeros_like(sums_ref)
    sums_ref[0:1] = column_sum(delta)
    sums_ref[1:2] = column_sum(hidden_grad * normed)
    sums_ref[2:3] = column_sum(hidden_grad)
    wait_all(leaving)


def attention_back_kernel(
    pairs, here_ref, x_ref, attn_low_ref, delta_ref, own_qk, qk_one, qk_two, own_vo, vo_one, vo_two, q_ref, k_ref,
    v_ref, weights_ref, context_ref, sums_one_ref, sums_two_ref, sum_in_ref,
    qk_keep_ref, vo_keep_ref, send_ref, sums_ref, *refs,
):
    step = pl.program_id(0)
    shards_ = pl.num_programs(0)
    out_refs = refs[:shards_]
    dq_ref, dk_ref, dv_ref, total_ref = refs[shards_:]

    @pl.when(step == 0)
    def _():
        total_ref[...] = delta_ref[...]
        sums_ref[...] = jnp.zeros_like(sums_ref)
        sums_ref[0:3] = sums_one_ref[0:3]
        sums_ref[3:6] = sums_two_ref[0:3]
        for j in range(shards_):
            sums_ref[6 + j : 7 + j] = sum_in_ref[j]

    core = here_ref[0]
    cols = q_ref.shape[2]
    heads = cols // HEAD
    slots = x_ref.shape[0] // pairs
    scale = HEAD ** (-0.5)
    x = x_ref[...]
    attn_low = attn_low_ref[...]
    w_q, w_k = head_weights(step == 0, here_ref, own_qk, qk_one, qk_two)
    w_v, w_o = head_weights(step == 0, here_ref, own_vo, vo_one, vo_two)
    context_grad = dot(attn_low, w_o, 1, 1).astype(BF16)
    grad_out = dot(context_ref[0], attn_low, 0, 0).astype(BF16)
    for p in range(pairs):
        rows = slice(p * slots, (p + 1) * slots)
        up = head_stack(context_grad[rows], heads)
        weights = weights_ref[0, p]
        prob_grad = dot(up, v_ref[0, rows], 1, 1)
        inner = jnp.sum(prob_grad * weights, axis=-1, keepdims=True)
        score_grad = (weights * (prob_grad - inner)).astype(BF16)
        dv_ref[rows] = dot(weights.astype(BF16), up, 0, 0).astype(BF16)
        query_grad = head_pick(dot(score_grad, k_ref[0, rows], 1, 0), heads)
        dq_ref[rows] = (query_grad * scale).astype(BF16)
        key_grad = dot(score_grad, head_stack(q_ref[0, rows], heads), 0, 0)
        dk_ref[rows] = (key_grad * scale).astype(BF16)
    dq, dk, dv = dq_ref[...], dk_ref[...], dv_ref[...]
    row = pl.ds(6 + shards_ + (step ^ here_ref[1]), 1)
    sums_ref[row, :cols] = column_sum(dq.astype(F32))
    sums_ref[row, 2 * cols : 3 * cols] = column_sum(dv.astype(F32))
    grad_q = dot(dq, x, 0, 0).astype(BF16)
    grad_k = dot(dk, x, 0, 0).astype(BF16)
    grad_v = dot(dv, x, 0, 0).astype(BF16)

    @pl.when(core == 0)
    def _():
        qk_keep_ref[0], send_ref[0, 0] = grad_q, grad_k
        vo_keep_ref[0], send_ref[1, 0] = grad_v, grad_out

    @pl.when(core != 0)
    def _():
        qk_keep_ref[0], send_ref[0, 0] = grad_k, grad_q
        vo_keep_ref[0], send_ref[1, 0] = grad_out, grad_v

    total_ref[...] += dot(dq, w_q, 1, 0) + dot(dk, w_k, 1, 0) + dot(dv, w_v, 1, 0)

    @pl.when(step == shards_ - 1)
    def _():
        leave_rows(total_ref[...], out_refs)


def place_kernel(pairs, here_ref, *refs):
    out_ref = refs[-1]
    for k, ref in enumerate(refs[:-1]):
        out_ref[pl.ds((here_ref[1] ^ k) * pairs, pairs)] = ref[...].astype(out_ref.dtype)


def head_grads_kernel(order, here_ref, mine_ref, other_ref, grad_qkv_ref, grad_out_ref):
    core = here_ref[0]
    part = grad_out_ref.shape[1]
    for side, ref in ((core, mine_ref), (1 - core, other_ref)):
        for k, index in enumerate(order):
            place = here_ref[2] ^ index
            piece = ref[k].astype(F32)
            grad_qkv_ref[side, place] = piece[:part]

            @pl.when(side == 0)
            def _():
                grad_qkv_ref[2, place] = piece[part:]

            @pl.when(side != 0)
            def _():
                grad_out_ref[place] = piece[part:]


def unit_grads_kernel(here_ref, in_ref, down_ref, in_other, down_other, grad_in_ref, grad_down_ref):
    half = in_ref.shape[1]
    mine = pl.multiple_of(here_ref[0] * half, half)
    other = pl.multiple_of((1 - here_ref[0]) * half, half)
    grad_in_ref[:, pl.ds(mine, half)] = in_ref[0].astype(F32).T
    grad_in_ref[:, pl.ds(other, half)] = in_other[0].astype(F32).T
    grad_down_ref[pl.ds(mine, half)] = down_ref[0].astype(F32)
    grad_down_ref[pl.ds(other, half)] = down_other[0].astype(F32)


def whole(array):
    return pl.BlockSpec(array.shape, lambda *_: (0,) * len(array.shape))


def per_step(array):
    return pl.BlockSpec((1,) + array.shape[1:], lambda s, *_: (s,) + (0,) * (len(array.shape) - 1))


def where_it_is(array):
    return pl.BlockSpec(memory_space=pl.ANY)


def in_vmem(array):
    return pl.BlockSpec(memory_space=pltpu.VMEM)


def call(kernel, steps, name, vmem, inputs, outputs, scratch, scalar, kept=()):
    spec = pltpu.PrefetchScalarGridSpec(
        num_scalar_prefetch=1,
        grid=(steps,),
        in_specs=[make if isinstance(make, pl.BlockSpec) else make(a) for make, a in inputs],
        out_specs=[make if isinstance(make, pl.BlockSpec) else make(a) for make, a in outputs],
        scratch_shapes=scratch,
    )
    return pl.pallas_call(
        kernel,
        grid_spec=spec,
        out_shape=[pltpu.HBM(a.shape, a.dtype) if i in kept else a for i, (_, a) in enumerate(outputs)],
        name=name,
        cost_estimate=pl.CostEstimate(flops=0, bytes_accessed=0, transcendentals=0),
        compiler_params=pltpu.CompilerParams(vmem_limit_bytes=vmem * MIB),
    )(scalar, *[a if make is in_vmem else in_place(a) for make, a in inputs])


def shape(dims, dtype):
    return jax.ShapeDtypeStruct(dims, dtype)


def in_place(array):
    if array.size * array.dtype.itemsize < MIB:
        return array
    return pltpu.with_memory_space_constraint(array, pltpu.HBM)


def add_kernel(counts, *refs):
    refs = refs[1:]
    out_refs = refs[sum(counts) :]
    for count, out_ref in zip(counts, out_refs):
        total = refs[0][...].astype(F32)
        for ref in refs[1:count]:
            total = total + ref[...].astype(F32)
        out_ref[...] = total.astype(BF16)
        refs = refs[count:]


def add_terms(sides, me):
    in_specs, out_specs, arrays, outs, lefts = [], [], [], [], []

    def place(own_bits, fixed, left):
        def index(g, me_ref):
            at = 0
            for b in own_bits:
                if b in fixed:
                    value = (me_ref[0] >> b) & 1
                    value = value if fixed[b] else 1 - value
                else:
                    value = (g >> (len(left) - 1 - left.index(b))) & 1
                at = at * 2 + value
            return (0, at, 0, 0)

        return index

    for terms, fixed in sides:
        first, bits = terms[0]
        left = [b for b in bits if b not in fixed]
        n, _, rows, cols = first.shape
        in_specs += [pl.BlockSpec((n, 1, rows, cols), place(b, fixed, left)) for _, b in terms]
        out_specs.append(pl.BlockSpec((n, 1, rows, cols), lambda g, _: (0, g, 0, 0)))
        arrays += [a for a, _ in terms]
        outs.append(shape((n, 1 << len(left), rows, cols), BF16))
        lefts.append(left)
    results = pl.pallas_call(
        partial(add_kernel, [len(terms) for terms, _ in sides]),
        grid_spec=pltpu.PrefetchScalarGridSpec(
            num_scalar_prefetch=1, grid=(1 << len(lefts[0]),), in_specs=in_specs, out_specs=out_specs
        ),
        out_shape=outs,
        name="add",
        cost_estimate=pl.CostEstimate(flops=0, bytes_accessed=0, transcendentals=0),
        compiler_params=pltpu.CompilerParams(vmem_limit_bytes=24 * MIB),
    )(me, *arrays)
    return results, lefts


def flip(array, axis, mask):
    size = lax.axis_size(axis)
    return lax.ppermute(array, axis, [(i, i ^ mask) for i in range(size)])


def tie(*arrays):
    return lax.optimization_barrier(arrays)


def pick(array, axis, index):
    return lax.dynamic_index_in_dim(array, index, axis, keepdims=False)


def outer_bits():
    bits = list(range(1, lax.axis_size("dp").bit_length() - 1))
    return bits, (bits, bits[::-1])


def share_of():
    me = lax.axis_index("dp")
    return (me & 1) * (lax.axis_size("dp") // 2) + (me >> 1)


class Gather:
    def __init__(self, pair):
        self.bits, self.orders = outer_bits()
        self.steps = len(self.bits)
        self.n, _, self.cols = pair[0].shape
        self.held = [
            a.reshape((self.n,) + (1,) * self.steps + a.shape[1:]) for a in pair
        ]

    def send(self, step):
        return [flip(h, "dp", 1 << order[step]) for h, order in zip(self.held, self.orders)]

    def merge(self, step, mine, theirs):
        me = lax.axis_index("dp")
        merged = []
        for one, two, order in zip(mine, theirs, self.orders):
            bit = order[step]
            low = ((me >> bit) & 1) == 0
            parts = [jnp.where(low, one, two), jnp.where(low, two, one)]
            merged.append(jnp.concatenate(parts, axis=1 + self.steps - bit))
        return merged

    def take(self, step, got):
        self.held = self.merge(step, self.held, got)

    def halves(self):
        return self.flat(self.held)

    def flat(self, arrays):
        return [a.reshape(self.n, -1, self.cols) for a in arrays]


class Reduce:
    def __init__(self, keeps, gots):
        self.bits, self.orders = outer_bits()
        self.steps = len(self.bits)
        self.me = lax.axis_index("dp").astype(jnp.int32).reshape(1)
        high_first = self.bits[::-1]
        n, rows, cols = keeps[0].shape
        form = (n, 1 << self.steps, rows >> self.steps, cols)
        self.terms = [
            [(k.reshape(form), high_first), (g.reshape(form), high_first)]
            for k, g in zip(keeps, gots)
        ]
        self.left = [None, None]

    def pack(self, step):
        sides = []
        for terms, order in zip(self.terms, self.orders):
            fixed = {b: True for b in order[:step]}
            fixed[order[step]] = False
            sides.append((terms, fixed))
        sends, self.left = add_terms(sides, self.me)
        return sends

    def send(self, step, packs):
        return [flip(p, "dp", 1 << order[step]) for p, order in zip(packs, self.orders)]

    def take(self, got):
        for side in range(2):
            self.terms[side].append((got[side], self.left[side]))

    def finish(self):
        fixed = {b: True for b in self.bits}
        sums, _ = add_terms([(t, fixed) for t in self.terms], self.me)
        return [a[:, 0] for a in sums]


def gather_stack(piece):
    bits, _ = outer_bits()
    order = list(range(1 << len(bits)))
    if len(order) <= 4:
        return [piece] + [flip(piece, "dp", 2 * k) for k in order[1:]], order
    held = piece[None]
    for bit in bits:
        held = jnp.concatenate([held, flip(held, "dp", 1 << bit)])
    return [held[k] for k in order], order


def add_parts(*parts):
    total = parts[0].astype(F32)
    for part in parts[1:]:
        total = total + part.astype(F32)
    return total.astype(BF16)


def shards(
    tokens,
    word_len,
    region_count,
    w_qkv,
    qv_bias,
    w_out,
    out_bias,
    norm1_gain,
    norm1_bias,
    w_in,
    in_bias,
    w_down,
    down_bias,
    norm2_gain,
    norm2_bias,
    cotangent,
):
    mp = lax.axis_size("mp")
    dp = lax.axis_size("dp")
    mi = lax.axis_index("mp")
    width = tokens.shape[2]
    rows_local = tokens.shape[1]
    slots = rows_local * mp
    pairs = tokens.shape[0] // mp
    rows = pairs * slots
    cols = w_qkv.shape[2]
    units = w_in.shape[1]
    half_units = units // 2
    order = jnp.arange(mp) ^ mi
    here = jnp.stack([lax.axis_index("dp") & 1, mi, lax.axis_index("dp") >> 1]).astype(jnp.int32)
    share = share_of()

    turned = w_qkv.transpose(0, 2, 1).reshape(3 * cols, width)
    own_qk = turned[: 2 * cols]
    own_vo = jnp.concatenate([turned[2 * cols :], w_out], axis=0)
    att_part, ffn_part = 2 * cols // dp, units // dp
    first = share * att_part
    rows_of = lambda array, start, size: lax.dynamic_slice_in_dim(array, start, size, 0)
    vo_piece = jnp.where(
        first < cols,
        rows_of(turned, 2 * cols + jnp.minimum(first, cols - att_part), att_part),
        rows_of(w_out, jnp.maximum(first - cols, 0), att_part),
    )

    def row_blocks(array):
        blocks = array.reshape((mp, pairs) + array.shape[1:])
        return [pick(blocks, 0, mi ^ k) for k in range(mp)]

    def join(blocks):
        return jnp.concatenate(blocks, axis=1).reshape(rows, width)

    fill = lambda v: jnp.pad(v, ((0, 0), (0, width - v.shape[1])))
    small = jnp.concatenate([fill(qv_bias), in_bias.reshape(1, units), jnp.zeros((5, width), BF16)])
    att_send = jnp.concatenate([rows_of(turned, first, att_part), vo_piece], axis=0)
    ffn_send = jnp.concatenate(
        [rows_of(w_in.T, share * ffn_part, ffn_part), rows_of(w_down, share * ffn_part, ffn_part), small],
        axis=0,
    )
    tok = row_blocks(tokens)
    cot = row_blocks(cotangent)
    vectors = jnp.stack(
        [out_bias, norm1_gain, norm1_bias, down_bias, norm2_gain, norm2_bias, out_bias, out_bias]
    ).astype(F32)
    words = lax.dynamic_slice_in_dim(word_len, mi * pairs, pairs, 0)
    regions = lax.dynamic_slice_in_dim(region_count, mi * pairs, pairs, 0)
    slot_index = (order[:, None] * rows_local + jnp.arange(rows_local)[None, :]).reshape(-1)
    key_valid = jnp.where(
        slot_index[None, :] < WORDS,
        slot_index[None, :] < words[:, None],
        slot_index[None, :] - WORDS < regions[:, None],
    ).astype(F32)[:, None, :]

    att_got = {k: flip(att_send, "mp", k) for k in (3, 2, 1)}
    att_got = [att_got[k] for k in (1, 2, 3)]
    att_got, ffn_send, tok, vectors, key_valid, here, own_qk, own_vo = tie(
        att_got, ffn_send, tok, vectors, key_valid, here, own_qk, own_vo
    )
    att = Gather(
        [
            jnp.stack([g[:att_part] for g in att_got]),
            jnp.stack([g[att_part:] for g in att_got]),
        ]
    )
    ffn_two = flip(ffn_send, "mp", 2)
    got = att.send(0)
    tok_one = flip(tok[1], "mp", 1)
    ffn_two, got, tok_one, ffn_send, tok = tie(ffn_two, got, tok_one, ffn_send, tok)
    for step in range(1, att.steps):
        att.take(step - 1, got)
        got = att.send(step)
        if step == 1:
            ffn_odd = flip(jnp.stack([ffn_send, ffn_two]), "mp", 1)
            tok_three = flip(tok[3], "mp", 3)
        got, ffn_odd, tok_three, tok = tie(got, ffn_odd, tok_three, tok)
    att.take(att.steps - 1, got)
    ffn_got = [ffn_odd[0], ffn_two, ffn_odd[1]]
    ffn = Gather(
        [
            jnp.stack([g[:ffn_part] for g in ffn_got]),
            jnp.stack([g[ffn_part : 2 * ffn_part] for g in ffn_got]),
        ]
    )
    got = ffn.send(0)
    qk_one, vo_one = att.halves()
    qk_two, vo_two = flip(qk_one, "dp", 1), flip(vo_one, "dp", 1)
    tok_two = flip(tok[2], "mp", 2)
    smalls = jnp.stack([small] + [g[2 * ffn_part :] for g in ffn_got]).astype(F32)
    got, qk_two, vo_two, tok_two, cot, smalls = tie(got, qk_two, vo_two, tok_two, cot, smalls)
    heads_low = shape((mp, rows, cols), BF16)
    low_shape = shape((rows, width), BF16)
    rows_shape = shape((rows, width), F32)
    sums_shape = shape((8, width), F32)
    block_shape = shape((pairs, rows_local, width), BF16)
    for step in range(1, ffn.steps):
        ffn.take(step - 1, got)
        got = ffn.send(step)
        if step < ffn.steps - 1:
            got = tie(*got)
    early = [flip(h, "dp", 1) for h in ffn.held]
    early, cot, x = tie(early, cot, join([tok[0], tok_one, tok_two, tok_three]))
    cot_blocks = [cot[0]] + [flip(cot[k], "mp", k) for k in range(1, mp)]
    later = lambda a: pl.BlockSpec((1,) + a.shape[1:], lambda s, h: (jnp.clip(s - 1, 0, mp - 2), 0, 0))
    head_args = [
        (whole, own_qk),
        (later, qk_one),
        (later, qk_two),
        (whole, own_vo),
        (later, vo_one),
        (later, vo_two),
    ]
    q, k, v, weights, context, hidden_low, normed_one, scale_one = call(
        partial(attention_kernel, pairs),
        mp,
        "attention",
        32,
        [
            (whole, x),
            *head_args,
            (per_step, smalls),
            (whole, key_valid),
            (whole, vectors),
        ],
        [
            (per_step, heads_low),
            (per_step, heads_low),
            (per_step, heads_low),
            (per_step, shape((mp, pairs, cols // HEAD * slots, slots), F32)),
            (per_step, heads_low),
            (whole, low_shape),
            (whole, rows_shape),
            (whole, shape((rows, 1), F32)),
        ],
        [pltpu.VMEM((rows, width), F32)],
        here,
        range(5),
    )
    got, early, hidden_low, cot_blocks = tie(got, early, hidden_low, cot_blocks)
    ffn.take(ffn.steps - 1, got)
    in_one, down_one = ffn.halves()
    late = [flip(g, "dp", 1) for g in got]
    late, hidden_low = tie(late, hidden_low)
    in_two, down_two = ffn.flat(ffn.merge(ffn.steps - 1, early, late))

    half = shape((mp, half_units, width), BF16)
    pre_shape = shape((mp, rows, units), BF16)
    vmem = lambda a: pltpu.VMEM(a.shape, a.dtype)
    results = call(
        partial(ffn_kernel, mp),
        1,
        "ffn",
        44,
        [
            (where_it_is, hidden_low),
            (where_it_is, normed_one),
            (where_it_is, w_in),
            (in_vmem, in_one),
            (in_vmem, in_two),
            (where_it_is, w_down),
            (in_vmem, down_one),
            (in_vmem, down_two),
            (whole, smalls),
            (whole, vectors),
            *[(where_it_is, c) for c in cot_blocks],
        ],
        [
            *[(whole, block_shape)] * mp,
            (where_it_is, rows_shape),
            (where_it_is, pre_shape),
            (where_it_is, half),
            (where_it_is, half),
            (where_it_is, half),
            (where_it_is, half),
            (whole, shape((mp, 1, units), F32)),
            (whole, sums_shape),
        ],
        [
            vmem(low_shape),
            vmem(rows_shape),
            pltpu.VMEM((width, units), BF16),
            pltpu.VMEM((units, width), BF16),
            pltpu.VMEM((mp,) + block_shape.shape, BF16),
            vmem(pre_shape),
            pltpu.VMEM(pre_shape.shape, F32),
            vmem(rows_shape),
            vmem(rows_shape),
            vmem(pre_shape),
            vmem(half),
            vmem(half),
            vmem(half),
            vmem(half),
            vmem(low_shape),
            pltpu.SemaphoreType.DMA((3 + 1 + mp + 1 + 5 * mp,)),
        ],
        here,
        range(mp + 6),
    )
    out_blocks = results[:mp]
    delta_ffn, pre_grad, in_keep, in_send, down_keep, down_send, sum_in, sums_two = results[mp:]
    in_got, down_got = flip(in_send, "dp", 1), flip(down_send, "dp", 1)
    delta_attn, attn_low, sums_one = call(
        partial(ffn_back_kernel, mp),
        1,
        "ffn_back",
        28,
        [
            (where_it_is, pre_grad),
            (where_it_is, w_in),
            (in_vmem, in_one),
            (in_vmem, in_two),
            (where_it_is, delta_ffn),
            (where_it_is, normed_one),
            (whole, scale_one),
            (whole, vectors),
        ],
        [(where_it_is, rows_shape), (whole, low_shape), (whole, sums_shape)],
        [
            vmem(pre_shape),
            pltpu.VMEM((width, units), BF16),
            vmem(rows_shape),
            vmem(rows_shape),
            vmem(rows_shape),
            pltpu.SemaphoreType.DMA((mp + 1 + 2 + 1,)),
        ],
        here,
        (0,),
    )
    in_got, down_got, out_blocks, attn_low = tie(in_got, down_got, out_blocks, attn_low)
    ffn = Reduce([in_keep, down_keep], [in_got, down_got])
    packs = ffn.pack(0)
    packs, attn_low, out_blocks = tie(packs, attn_low, out_blocks)
    got = ffn.send(0, packs)
    out_got = [out_blocks[0]] + [flip(out_blocks[k], "mp", k) for k in range(1, mp)]
    small_half = shape((mp, cols, width), BF16)
    results = call(
        partial(attention_back_kernel, pairs),
        mp,
        "attention_back",
        40,
        [
            (whole, x),
            (whole, attn_low),
            (whole, delta_attn),
            *head_args,
            (per_step, q),
            (per_step, k),
            (per_step, v),
            (per_step, weights),
            (per_step, context),
            (whole, sums_one),
            (whole, sums_two),
            (whole, sum_in),
        ],
        [
            (per_step, small_half),
            (per_step, small_half),
            (
                pl.BlockSpec((2, 1, cols, width), lambda s, h: (0, s, 0, 0)),
                shape((2, mp, cols, width), BF16),
            ),
            (whole, shape((-(-(6 + 2 * mp) // 8) * 8, width), F32)),
            *[(whole, block_shape)] * mp,
        ],
        [pltpu.VMEM((rows, cols), BF16)] * 3 + [pltpu.VMEM((rows, width), F32)],
        here,
        (0, 1, 2) + tuple(range(4, 4 + mp)),
    )
    qk_keep, vo_keep, att_send, sums = results[:4]
    row_sends = results[4:]
    got, out_got, att_send, row_sends, sums = tie(got, out_got, att_send, row_sends, sums)
    for step in range(1, ffn.steps):
        ffn.take(got)
        packs = ffn.pack(step)
        got = ffn.send(step, packs)
        if step == 1:
            att_got = flip(att_send, "dp", 1)
            row_three = flip(row_sends[3], "mp", 3)
            sums_got = flip(sums, "mp", 2)
        got, att_got, row_three, sums_got, row_sends = tie(got, att_got, row_three, sums_got, row_sends)
    sums = sums + sums_got
    place = lambda blocks, dtype: call(
        partial(place_kernel, pairs),
        1,
        "place",
        16,
        [(whole, b) for b in blocks],
        [(whole, shape((mp * pairs, rows_local, width), dtype))],
        [],
        here,
    )[0]
    layer_out = place(out_got, BF16)
    ffn.take(got)
    ffn_parts = ffn.finish()
    ffn_odd = jnp.concatenate([p[1::2] for p in ffn_parts], axis=1)
    ffn_even = jnp.concatenate([p[0::2] for p in ffn_parts], axis=1)
    att = Reduce([qk_keep, vo_keep], [att_got[0], att_got[1]])
    ffn_odd, ffn_even, sums = tie(ffn_odd, ffn_even, sums)
    got = att.send(0, att.pack(0))
    ffn_got = flip(ffn_odd, "mp", 1)
    sums_got = flip(sums, "dp", 2)
    row_two = flip(row_sends[2], "mp", 2)
    got, ffn_got, sums_got, row_two, row_sends, layer_out = tie(
        got, ffn_got, sums_got, row_two, row_sends, layer_out
    )
    sums = sums + sums_got
    for mask in [1 << b for b in range(2, dp.bit_length() - 2)]:
        sums = sums + flip(sums, "dp", mask)
    ffn_two = add_parts(ffn_even[1], ffn_got[1])
    for step in range(1, att.steps):
        att.take(got)
        packs = att.pack(step)
        got = att.send(step, packs)
        if step == 1:
            ffn_last = flip(ffn_two, "mp", 2)
            row_one = flip(row_sends[1], "mp", 1)
            sums_got = flip(sums, "dp", dp // 2)
        got, ffn_last, row_one, sums_got, row_sends = tie(got, ffn_last, row_one, sums_got, row_sends)
    att.take(got)
    sums = sums + sums_got
    att_parts = att.finish()
    att_odd = jnp.concatenate([p[1::2] for p in att_parts], axis=1)
    att_even = jnp.concatenate([p[0::2] for p in att_parts], axis=1)
    ffn_sum = add_parts(ffn_even[0], ffn_got[0], ffn_last)
    ffn = Gather([ffn_sum[None, :ffn_part], ffn_sum[None, ffn_part:]])
    ffn.held, att_odd, att_even, sums = tie(ffn.held, att_odd, att_even, sums)
    got = ffn.send(0)
    att_got = flip(att_odd, "mp", 1)
    sums_got = flip(sums, "dp", 1)
    got, att_got, sums_got, row_one = tie(got, att_got, sums_got, row_one)
    grad_input = place([row_sends[0], row_one, row_two, row_three], F32)
    sums = sums + sums_got
    att_two = add_parts(att_even[1], att_got[1])
    for step in range(1, ffn.steps):
        ffn.take(step - 1, got)
        got = ffn.send(step)
        if step == 1:
            att_last = flip(att_two, "mp", 2)
            sums_got = flip(sums, "mp", 1)
        got, att_last, sums_got, grad_input = tie(got, att_last, sums_got, grad_input)
    ffn.take(ffn.steps - 1, got)
    sums = sums + sums_got
    att_sum = add_parts(att_even[0], att_got[0], att_last)
    ffn_halves = ffn.halves()
    core_got = [flip(h, "dp", 1) for h in ffn_halves]
    att_mine, att_order = gather_stack(att_sum)
    grad_in, grad_down = call(
        unit_grads_kernel,
        1,
        "unit_grads",
        24,
        [(whole, a) for a in ffn_halves + core_got],
        [(whole, shape((width, units), F32)), (whole, shape((units, width), F32))],
        [],
        here,
    )
    att_mine, grad_in, grad_down, sums = tie(att_mine, grad_in, grad_down, sums)
    att_mine = jnp.stack(att_mine)
    att_other = flip(att_mine, "dp", 1)
    grad_qkv, grad_out = call(
        partial(head_grads_kernel, att_order),
        1,
        "head_grads",
        24,
        [(whole, att_mine), (whole, att_other)],
        [
            (whole, shape((3, cols // att_part, att_part, width), F32)),
            (whole, shape((cols // att_part, att_part, width), F32)),
        ],
        [],
        here,
    )
    sum_in_bias = lax.dynamic_index_in_dim(sums, 6 + mi, 0, keepdims=False)
    sum_qv = lax.dynamic_index_in_dim(sums, 6 + mp + mi, 0, keepdims=False)
    sum_qv = jnp.stack([sum_qv[:cols], sum_qv[2 * cols : 3 * cols]])
    return (
        layer_out,
        grad_input,
        grad_qkv.reshape(3, cols, width).transpose(0, 2, 1),
        sum_qv,
        grad_out.reshape(cols, width),
        sums[0],
        sums[1],
        sums[2],
        grad_in,
        sum_in_bias,
        grad_down,
        sums[5],
        sums[3],
        sums[4],
    )


def solution(mesh):
    in_specs = (
        P("dp", "mp", None),
        P("dp"),
        P("dp"),
        P(None, None, "mp"),
        P(None, "mp"),
        P("mp", None),
        P(),
        P(),
        P(),
        P(None, "mp"),
        P("mp"),
        P("mp", None),
        P(),
        P(),
        P(),
        P("dp", "mp", None),
    )
    out_specs = (
        P("dp", "mp", None),
        P("dp", "mp", None),
        P(None, None, "mp"),
        P(None, "mp"),
        P("mp", None),
        P(),
        P(),
        P(),
        P(None, "mp"),
        P("mp"),
        P("mp", None),
        P(),
        P(),
        P(),
    )
    return jax.shard_map(shards, mesh=mesh, in_specs=in_specs, out_specs=out_specs, check_vma=False)
```

profile of v0, /device:TPU:0, one launch (start us, length us, event | category | flops | bytes accessed | tf_op | source)
XLA Modules:
  0.0 243.3 jit_solution(5628604757045372254)
XLA Ops:
  1.8 3.1 %collective-permute-start = (bf16[96,768]{1,0:T(8,128)(2,1)S(1)}, bf16[96,768]{1,0:T(8,128)(2,1)S(1)}, u32[]{:S(2)}, u32[]{:S(2)}) collective-permute-start(bf16[96,768]{1,0:T(8,128)(2,1)S(1)} %pad_maximum_fusion.22), channel_id=1, source_target_pairs={{0,1},{1,0},{2,3},{3,2},{4,5},{5,4},{6,7},{7,6},{8,9},{9,8},{10,11... | collective-permute-start | bytes 442376 | tf_op jit(solution)/shard_map/ppermute | solution.py:520
  4.9 2.6 %collective-permute-start.1 = (bf16[96,768]{1,0:T(8,128)(2,1)S(1)}, bf16[96,768]{1,0:T(8,128)(2,1)}, u32[]{:S(2)}, u32[]{:S(2)}) collective-permute-start(bf16[96,768]{1,0:T(8,128)(2,1)S(1)} %pad_maximum_fusion.22), channel_id=1, source_target_pairs={{0,2},{1,3},{2,0},{3,1},{4,6},{5,7},{6,4},{7,5},{8,10},{9,11},{10,... | collective-permute-start | bytes 442376 | tf_op jit(solution)/shard_map/ppermute | solution.py:520
  14.2 4.8 %collective-permute-done.1 = bf16[96,768]{1,0:T(8,128)(2,1)} collective-permute-done((bf16[96,768]{1,0:T(8,128)(2,1)S(1)}, bf16[96,768]{1,0:T(8,128)(2,1)}, u32[]{:S(2)}, u32[]{:S(2)}) %collective-permute-start.1) | collective-permute-done | bytes 147488 | tf_op jit(solution)/shard_map/ppermute | solution.py:520
  20.1 1.6 collective-permute-start.5
  21.7 3.3 %collective-permute-start.3 = (bf16[200,768]{1,0:T(8,128)(2,1)S(1)}, bf16[200,768]{1,0:T(8,128)(2,1)S(1)}, u32[]{:S(2)}, u32[]{:S(2)}) collective-permute-start(bf16[200,768]{1,0:T(8,128)(2,1)S(1)} %concatenate.71), channel_id=1, source_target_pairs={{0,2},{1,3},{2,0},{3,1},{4,6},{5,7},{6,4},{7,5},{8,10},{9,11},{10,... | collective-permute-start | bytes 921608 | tf_op jit(solution)/shard_map/ppermute | solution.py:520
  25.0 1.6 collective-permute-start.4
  26.6 7.8 %collective-permute-done.6 = bf16[3,40,768]{2,1,0:T(8,128)(2,1)S(1)} collective-permute-done((bf16[3,40,768]{2,1,0:T(8,128)(2,1)}, bf16[3,40,768]{2,1,0:T(8,128)(2,1)S(1)}, u32[]{:S(2)}, u32[]{:S(2)}) %collective-permute-start.6) | collective-permute-done | bytes 184352 | tf_op jit(solution)/shard_map/ppermute | solution.py:520
  34.4 3.2 %collective-permute-done.3 = bf16[200,768]{1,0:T(8,128)(2,1)S(1)} collective-permute-done((bf16[200,768]{1,0:T(8,128)(2,1)S(1)}, bf16[200,768]{1,0:T(8,128)(2,1)S(1)}, u32[]{:S(2)}, u32[]{:S(2)}) %collective-permute-start.3) | collective-permute-done | bytes 307232 | tf_op jit(solution)/shard_map/ppermute | solution.py:520
  37.8 1.6 collective-permute-start.8
  41.4 14.2 %collective-permute-done.10 = bf16[3,40,768]{2,1,0:T(8,128)(2,1)S(1)} collective-permute-done((bf16[3,40,768]{2,1,0:T(8,128)(2,1)S(1)}, bf16[3,40,768]{2,1,0:T(8,128)(2,1)S(1)}, u32[]{:S(2)}, u32[]{:S(2)}) %collective-permute-start.10) | collective-permute-done | bytes 184352 | tf_op jit(solution)/shard_map/ppermute | solution.py:520
  58.3 1.6 collective-permute-start.11
  59.9 10.3 %collective-permute-done.15 = bf16[3,40,768]{2,1,0:T(8,128)(2,1)S(1)} collective-permute-done((bf16[3,40,768]{2,1,0:T(8,128)(2,1)S(1)}, bf16[3,40,768]{2,1,0:T(8,128)(2,1)S(1)}, u32[]{:S(2)}, u32[]{:S(2)}) %collective-permute-start.15) | collective-permute-done | bytes 184352 | tf_op jit(solution)/shard_map/ppermute | solution.py:520
  71.2 1.5 collective-permute-start.19
  72.7 1.5 collective-permute-start.18
  74.4 2.7 %collective-permute-start.21 = (bf16[3,40,768]{2,1,0:T(8,128)(2,1)S(1)}, bf16[3,40,768]{2,1,0:T(8,128)(2,1)S(1)}, u32[]{:S(2)}, u32[]{:S(2)}) collective-permute-start(bf16[3,40,768]{2,1,0:T(8,128)(2,1)S(1)} %get-tuple-element.233), channel_id=1, source_target_pairs={{0,2},{1,3},{2,0},{3,1},{4,6},{5,7},{6,4},{7,5},{8,10},{9,11},{10,... | collective-permute-start | bytes 552968 | tf_op jit(solution)/shard_map/ppermute | solution.py:520
  77.0 1.7 collective-permute-start.22
  78.8 12.0 %attention.1 = (bf16[4,480,192]{2,1,0:T(8,128)(2,1)}, bf16[4,480,192]{2,1,0:T(8,128)(2,1)}, bf16[4,480,192]{2,1,0:T(8,128)(2,1)}, f32[4,3,480,160]{3,2,1,0:T(8,1...) custom-call(s32[3]{0:T(128)S(1)} %pad_add_fusion.here_ref, ...), custom_call_target="tpu_custom_call" | custom-call | tf_op jit(solution)/shard_map/attention/pallas_call | solution.py:448
  90.7 2.1 collective-permute-done.19
  98.7 20.2 %ffn.1 = (bf16[3,40,768]{2,1,0:T(8,128)(2,1)}, bf16[3,40,768]{2,1,0:T(8,128)(2,1)}, bf16[3,40,768]{2,1,0:T(8,128)(2,1)}, bf16[3,40,768]{2,1,0:T(8,128)(2,1)}, f3...) custom-call(s32[3]{0:T(128)S(1)} %pad_add_fusion.here_ref, ...), custom_call_target="tpu_custom_call" | custom-call | tf_op jit(solution)/shard_map/ffn/pallas_call | solution.py:448
  119.5 7.2 %ffn_back.1 = (f32[480,768]{1,0:T(8,128)}, bf16[480,768]{1,0:T(8,128)(2,1)S(1)}, f32[8,768]{1,0:T(8,128)S(1)}) custom-call(s32[3]{0:T(128)S(1)} %pad_add_fusion.here_ref, bf16[4,480,768]{2,1,0:T(8,128)(2,1)} %get-tuple-element.255.pre_grad_hbm, bf16[768,768]{1,0:T(8,128)(2,1)} %w_in_hbm.3, bf16[3,384,768]{2,1,0:T(8,128)(2,1)S(1)} %bitcast.139, ...), custom_call_target="tpu_custom_call" | custom-call | tf_op jit(solution)/shard_map/ffn_back/pallas_call | solution.py:448
  127.2 1.9 add.189
  129.6 1.5 collective-permute-start.28
  132.1 1.6 collective-permute-start.30
  133.8 1.7 collective-permute-start.31
  135.5 19.1 %attention_back.1 = (bf16[4,192,768]{2,1,0:T(8,128)(2,1)}, bf16[4,192,768]{2,1,0:T(8,128)(2,1)}, bf16[2,4,192,768]{3,2,1,0:T(8,128)(2,1)}, f32[16,768]{1,0:T(8,1...) custom-call(s32[3]{0:T(128)S(1)} %pad_add_fusion.here_ref, ...), custom_call_target="tpu_custom_call" | custom-call | tf_op jit(solution)/shard_map/attention_back/pallas_call | solution.py:448
  154.6 2.6 %collective-permute-done.27.refs_3_ = bf16[4,2,96,768]{3,2,1,0:T(8,128)(2,1)S(1)} collective-permute-done((bf16[4,2,96,768]{3,2,1,0:T(8,128)(2,1)}, bf16[4,2,96,768]{3,2,1,0:T(8,128)(2,1)S(1)}, u32[]{:S(2)}, u32[]{:S(2)}) %collective-permute-start.27) | collective-permute-done | bytes 1179680 | tf_op jit(solution)/shard_map/ppermute | solution.py:520
  157.8 1.6 collective-permute-start.32
  159.4 1.5 collective-permute-start.33
  160.9 2.1 collective-permute-start.35
  163.0 10.0 %collective-permute-done.36 = f32[16,768]{1,0:T(8,128)S(1)} collective-permute-done((f32[16,768]{1,0:T(8,128)S(1)}, f32[16,768]{1,0:T(8,128)S(1)}, u32[]{:S(2)}, u32[]{:S(2)}) %collective-permute-start.36) | collective-permute-done | bytes 49184 | tf_op jit(solution)/shard_map/ppermute | solution.py:520
  178.3 1.5 collective-permute-start.37
  182.5 1.5 place.2
  184.0 10.1 %collective-permute-done.40 = f32[16,768]{1,0:T(8,128)S(1)} collective-permute-done((f32[16,768]{1,0:T(8,128)S(1)}, f32[16,768]{1,0:T(8,128)S(1)}, u32[]{:S(2)}, u32[]{:S(2)}) %collective-permute-start.40) | collective-permute-done | bytes 49184 | tf_op jit(solution)/shard_map/ppermute | solution.py:520
  194.5 2.0 collective-permute-start.44
  198.1 1.5 collective-permute-start.45
  201.0 3.9 %collective-permute-done.46 = f32[16,768]{1,0:T(8,128)S(1)} collective-permute-done((f32[16,768]{1,0:T(8,128)S(1)}, f32[16,768]{1,0:T(8,128)S(1)}, u32[]{:S(2)}, u32[]{:S(2)}) %collective-permute-start.46) | collective-permute-done | bytes 49184 | tf_op jit(solution)/shard_map/ppermute | solution.py:520
  205.5 3.6 %collective-permute-done.44 = bf16[192,768]{1,0:T(8,128)(2,1)S(1)} collective-permute-done((bf16[192,768]{1,0:T(8,128)(2,1)S(1)}, bf16[192,768]{1,0:T(8,128)(2,1)S(1)}, u32[]{:S(2)}, u32[]{:S(2)}) %collective-permute-start.44) | collective-permute-done | bytes 294944 | tf_op jit(solution)/shard_map/ppermute | solution.py:520
  209.8 1.6 collective-permute-start.47
  215.0 1.5 collective-permute-done.48
  217.7 2.1 collective-permute-start.52
  222.1 1.7 collective-permute-start.54
  223.8 1.7 place.3
  226.2 2.0 collective-permute-done.53
  229.4 1.5 collective-permute-start.56
  231.0 1.7 collective-permute-start.57
  232.6 3.1 %unit_grads.1 = (f32[768,768]{1,0:T(8,128)}, f32[768,768]{1,0:T(8,128)}) custom-call(s32[3]{0:T(128)S(1)} %pad_add_fusion.here_ref, bf16[1,384,768]{2,1,0:T(8,128)(2,1)S(1)} %bitcast.163, bf16[1,384,768]{2,1,0:T(8,128)(2,1)S(1)} %bitcast.161, bf16[1,384,768]{2,1,0:T(8,128)(2,1)S(1)} %collective-permute-done.58.in_other, ...), custom_call_target="tpu_custom_call" | custom-call | tf_op jit(solution)/shard_map/unit_grads/pallas_call | solution.py:448
  235.8 3.2 %collective-permute-done.57 = bf16[96,768]{1,0:T(8,128)(2,1)S(1)} collective-permute-done((bf16[96,768]{1,0:T(8,128)(2,1)S(1)}, bf16[96,768]{1,0:T(8,128)(2,1)S(1)}, u32[]{:S(2)}, u32[]{:S(2)}) %collective-permute-start.57) | collective-permute-done | bytes 147488 | tf_op jit(solution)/shard_map/ppermute | solution.py:520
  241.2 2.2 head_grads.1
  (256 shorter events, 47.3 us)
Async XLA Ops:
  1.8 12.4 %collective-permute-start = (bf16[96,768]{1,0:T(8,128)(2,1)S(1)}, bf16[96,768]{1,0:T(8,128)(2,1)S(1)}, u32[]{:S(2)}, u32[]{:S(2)}) collective-permute-start(bf16[96,768]{1,0:T(8,128)(2,1)S(1)} %pad_maximum_fusion.22), channel_id=1, source_target_pairs={{0,1},{1,0},{2,3},{3,2},{4,5},{5,4},{6,7},{7,6},{8,9},{9,8},{10,11... | collective-permute-start | bytes 442376 | tf_op jit(solution)/shard_map/ppermute | solution.py:520
  4.9 14.1 %collective-permute-start.1 = (bf16[96,768]{1,0:T(8,128)(2,1)S(1)}, bf16[96,768]{1,0:T(8,128)(2,1)}, u32[]{:S(2)}, u32[]{:S(2)}) collective-permute-start(bf16[96,768]{1,0:T(8,128)(2,1)S(1)} %pad_maximum_fusion.22), channel_id=1, source_target_pairs={{0,2},{1,3},{2,0},{3,1},{4,6},{5,7},{6,4},{7,5},{8,10},{9,11},{10,... | collective-permute-start | bytes 442376 | tf_op jit(solution)/shard_map/ppermute | solution.py:520
  7.5 11.5 %collective-permute-start.2 = (bf16[96,768]{1,0:T(8,128)(2,1)S(1)}, bf16[96,768]{1,0:T(8,128)(2,1)}, u32[]{:S(2)}, u32[]{:S(2)}) collective-permute-start(bf16[96,768]{1,0:T(8,128)(2,1)S(1)} %pad_maximum_fusion.22), channel_id=1, source_target_pairs={{0,3},{1,2},{2,1},{3,0},{4,7},{5,6},{6,5},{7,4},{8,11},{9,10},{10,... | collective-permute-start | bytes 442376 | tf_op jit(solution)/shard_map/ppermute | solution.py:520
  20.1 14.3 %collective-permute-start.5 = (bf16[3,1,1,48,768]{4,3,0,2,1:T(8,128)(2,1)S(1)}, bf16[3,1,1,48,768]{4,3,0,2,1:T(8,128)(2,1)S(1)}, u32[]{:S(2)}, u32[]{:S(2)}) collective-permute-start(bf16[3,1,1,48,768]{4,3,0,2,1:T(8,128)(2,1)S(1)} %maximum_bitcast_fusion.3), channel_id=1, source_target_pairs={{0,16},{4,20},{8,24},{12,28},{16,0},{20,4},{24,8},{28,12},{1,17},{... | collective-permute-start | bytes 663560 | tf_op jit(solution)/shard_map/ppermute | solution.py:520
  21.7 15.9 %collective-permute-start.3 = (bf16[200,768]{1,0:T(8,128)(2,1)S(1)}, bf16[200,768]{1,0:T(8,128)(2,1)S(1)}, u32[]{:S(2)}, u32[]{:S(2)}) collective-permute-start(bf16[200,768]{1,0:T(8,128)(2,1)S(1)} %concatenate.71), channel_id=1, source_target_pairs={{0,2},{1,3},{2,0},{3,1},{4,6},{5,7},{6,4},{7,5},{8,10},{9,11},{10,... | collective-permute-start | bytes 921608 | tf_op jit(solution)/shard_map/ppermute | solution.py:520
  25.0 9.4 %collective-permute-start.4 = (bf16[3,1,1,48,768]{4,3,0,2,1:T(8,128)(2,1)S(1)}, bf16[3,1,1,48,768]{4,3,0,2,1:T(8,128)(2,1)S(1)}, u32[]{:S(2)}, u32[]{:S(2)}) collective-permute-start(bf16[3,1,1,48,768]{4,3,0,2,1:T(8,128)(2,1)S(1)} %maximum_bitcast_fusion.2), channel_id=1, source_target_pairs={{0,8},{4,12},{8,0},{12,4},{16,24},{20,28},{24,16},{28,20},{1,9},{5... | collective-permute-start | bytes 663560 | tf_op jit(solution)/shard_map/ppermute | solution.py:520
  26.6 7.8 %collective-permute-start.6 = (bf16[3,40,768]{2,1,0:T(8,128)(2,1)}, bf16[3,40,768]{2,1,0:T(8,128)(2,1)S(1)}, u32[]{:S(2)}, u32[]{:S(2)}) collective-permute-start(bf16[3,40,768]{2,1,0:T(8,128)(2,1)} %get-tuple-element.195), channel_id=1, source_target_pairs={{0,1},{1,0},{2,3},{3,2},{4,5},{5,4},{6,7},{7,6},{8,9},{9,8},{10,11... | collective-permute-start | bytes 552968 | tf_op jit(solution)/shard_map/ppermute | solution.py:520
  37.7 18.8 %collective-permute-start.9 = (bf16[2,200,768]{2,1,0:T(8,128)(2,1)S(1)}, bf16[2,200,768]{2,1,0:T(8,128)(2,1)S(1)}, u32[]{:S(2)}, u32[]{:S(2)}) collective-permute-start(bf16[2,200,768]{2,1,0:T(8,128)(2,1)S(1)} %pad_maximum_fusion.9), channel_id=1, source_target_pairs={{0,1},{1,0},{2,3},{3,2},{4,5},{5,4},{6,7},{7,6},{8,9},{9,8},{10,11... | collective-permute-start | bytes 1843208 | tf_op jit(solution)/shard_map/ppermute | solution.py:520
  37.8 17.7 %collective-permute-start.8 = (bf16[3,2,1,48,768]{4,3,0,2,1:T(8,128)(2,1)S(1)}, bf16[3,2,1,48,768]{4,3,0,2,1:T(8,128)(2,1)S(1)}, u32[]{:S(2)}, u32[]{:S(2)}) collective-permute-start(bf16[3,2,1,48,768]{4,3,0,2,1:T(8,128)(2,1)S(1)} %pad_maximum_fusion.17), channel_id=1, source_target_pairs={{0,8},{4,12},{8,0},{12,4},{16,24},{20,28},{24,16},{28,20},{1,9},{5... | collective-permute-start | bytes 1327112 | tf_op jit(solution)/shard_map/ppermute | solution.py:520
  39.5 16.1 %collective-permute-start.7 = (bf16[3,1,2,48,768]{4,3,0,2,1:T(8,128)(2,1)S(1)}, bf16[3,1,2,48,768]{4,3,0,2,1:T(8,128)(2,1)S(1)}, u32[]{:S(2)}, u32[]{:S(2)}) collective-permute-start(bf16[3,1,2,48,768]{4,3,0,2,1:T(8,128)(2,1)S(1)} %pad_maximum_fusion.16), channel_id=1, source_target_pairs={{0,16},{4,20},{8,24},{12,28},{16,0},{20,4},{24,8},{28,12},{1,17},{... | collective-permute-start | bytes 1327112 | tf_op jit(solution)/shard_map/ppermute | solution.py:520
  40.2 15.4 %collective-permute-start.10 = (bf16[3,40,768]{2,1,0:T(8,128)(2,1)S(1)}, bf16[3,40,768]{2,1,0:T(8,128)(2,1)S(1)}, u32[]{:S(2)}, u32[]{:S(2)}) collective-permute-start(bf16[3,40,768]{2,1,0:T(8,128)(2,1)S(1)} %copy-done.18), channel_id=1, source_target_pairs={{0,3},{1,2},{2,1},{3,0},{4,7},{5,6},{6,5},{7,4},{8,11},{9,10},{10,... | collective-permute-start | bytes 552968 | tf_op jit(solution)/shard_map/ppermute | solution.py:520
  56.7 13.5 %collective-permute-start.14 = (bf16[3,192,768]{2,1,0:T(8,128)(2,1)S(1)}, bf16[3,192,768]{2,1,0:T(8,128)(2,1)S(1)}, u32[]{:S(2)}, u32[]{:S(2)}) collective-permute-start(bf16[3,192,768]{2,1,0:T(8,128)(2,1)S(1)} %bitcast.148), channel_id=1, source_target_pairs={{0,4},{4,0},{8,12},{12,8},{16,20},{20,16},{24,28},{28,24},{1,5},{5... | collective-permute-start | bytes 2654216 | tf_op jit(solution)/shard_map/ppermute | solution.py:520
  57.1 13.2 %collective-permute-start.13 = (bf16[3,192,768]{2,1,0:T(8,128)(2,1)S(1)}, bf16[3,192,768]{2,1,0:T(8,128)(2,1)S(1)}, u32[]{:S(2)}, u32[]{:S(2)}) collective-permute-start(bf16[3,192,768]{2,1,0:T(8,128)(2,1)S(1)} %bitcast.151), channel_id=1, source_target_pairs={{0,4},{4,0},{8,12},{12,8},{16,20},{20,16},{24,28},{28,24},{1,5},{5... | collective-permute-start | bytes 2654216 | tf_op jit(solution)/shard_map/ppermute | solution.py:520
  57.7 12.5 %collective-permute-start.12 = (bf16[3,1,1,96,768]{4,3,0,2,1:T(8,128)(2,1)S(1)}, bf16[3,1,1,96,768]{4,3,0,2,1:T(8,128)(2,1)S(1)}, u32[]{:S(2)}, u32[]{:S(2)}) collective-permute-start(bf16[3,1,1,96,768]{4,3,0,2,1:T(8,128)(2,1)S(1)} %maximum_bitcast_fusion.1), channel_id=1, source_target_pairs={{0,16},{4,20},{8,24},{12,28},{16,0},{20,4},{24,8},{28,12},{1,17},{... | collective-permute-start | bytes 1327112 | tf_op jit(solution)/shard_map/ppermute | solution.py:520
  58.3 11.9 %collective-permute-start.11 = (bf16[3,1,1,96,768]{4,3,0,2,1:T(8,128)(2,1)S(1)}, bf16[3,1,1,96,768]{4,3,0,2,1:T(8,128)(2,1)S(1)}, u32[]{:S(2)}, u32[]{:S(2)}) collective-permute-start(bf16[3,1,1,96,768]{4,3,0,2,1:T(8,128)(2,1)S(1)} %maximum_bitcast_fusion), channel_id=1, source_target_pairs={{0,8},{4,12},{8,0},{12,4},{16,24},{20,28},{24,16},{28,20},{1,9},{5... | collective-permute-start | bytes 1327112 | tf_op jit(solution)/shard_map/ppermute | solution.py:520
  59.9 10.3 %collective-permute-start.15 = (bf16[3,40,768]{2,1,0:T(8,128)(2,1)S(1)}, bf16[3,40,768]{2,1,0:T(8,128)(2,1)S(1)}, u32[]{:S(2)}, u32[]{:S(2)}) collective-permute-start(bf16[3,40,768]{2,1,0:T(8,128)(2,1)S(1)} %copy-done.17), channel_id=1, source_target_pairs={{0,2},{1,3},{2,0},{3,1},{4,6},{5,7},{6,4},{7,5},{8,10},{9,11},{10,... | collective-permute-start | bytes 552968 | tf_op jit(solution)/shard_map/ppermute | solution.py:520
  71.2 21.6 %collective-permute-start.19 = (bf16[3,2,1,96,768]{4,3,0,2,1:T(8,128)(2,1)S(1)}, bf16[3,2,1,96,768]{4,3,0,2,1:T(8,128)(2,1)S(1)}, u32[]{:S(2)}, u32[]{:S(2)}) collective-permute-start(bf16[3,2,1,96,768]{4,3,0,2,1:T(8,128)(2,1)S(1)} %pad_maximum_fusion.7), channel_id=1, source_target_pairs={{0,8},{4,12},{8,0},{12,4},{16,24},{20,28},{24,16},{28,20},{1,9},{5... | collective-permute-start | bytes 2654216 | tf_op jit(solution)/shard_map/ppermute | solution.py:520
  72.7 21.4 %collective-permute-start.18 = (bf16[3,1,2,96,768]{4,3,0,2,1:T(8,128)(2,1)S(1)}, bf16[3,1,2,96,768]{4,3,0,2,1:T(8,128)(2,1)S(1)}, u32[]{:S(2)}, u32[]{:S(2)}) collective-permute-start(bf16[3,1,2,96,768]{4,3,0,2,1:T(8,128)(2,1)S(1)} %pad_maximum_fusion.6), channel_id=1, source_target_pairs={{0,16},{4,20},{8,24},{12,28},{16,0},{20,4},{24,8},{28,12},{1,17},{... | collective-permute-start | bytes 2654216 | tf_op jit(solution)/shard_map/ppermute | solution.py:520
  74.3 19.8 %collective-permute-start.20 = (bf16[3,40,768]{2,1,0:T(8,128)(2,1)S(1)}, bf16[3,40,768]{2,1,0:T(8,128)(2,1)S(1)}, u32[]{:S(2)}, u32[]{:S(2)}) collective-permute-start(bf16[3,40,768]{2,1,0:T(8,128)(2,1)S(1)} %get-tuple-element.232), channel_id=1, source_target_pairs={{0,1},{1,0},{2,3},{3,2},{4,5},{5,4},{6,7},{7,6},{8,9},{9,8},{10,11... | collective-permute-start | bytes 552968 | tf_op jit(solution)/shard_map/ppermute | solution.py:520
  74.4 19.7 %collective-permute-start.21 = (bf16[3,40,768]{2,1,0:T(8,128)(2,1)S(1)}, bf16[3,40,768]{2,1,0:T(8,128)(2,1)S(1)}, u32[]{:S(2)}, u32[]{:S(2)}) collective-permute-start(bf16[3,40,768]{2,1,0:T(8,128)(2,1)S(1)} %get-tuple-element.233), channel_id=1, source_target_pairs={{0,2},{1,3},{2,0},{3,1},{4,6},{5,7},{6,4},{7,5},{8,10},{9,11},{10,... | collective-permute-start | bytes 552968 | tf_op jit(solution)/shard_map/ppermute | solution.py:520
  77.0 17.0 %collective-permute-start.22 = (bf16[3,40,768]{2,1,0:T(8,128)(2,1)S(1)}, bf16[3,40,768]{2,1,0:T(8,128)(2,1)S(1)}, u32[]{:S(2)}, u32[]{:S(2)}) collective-permute-start(bf16[3,40,768]{2,1,0:T(8,128)(2,1)S(1)} %get-tuple-element.234), channel_id=1, source_target_pairs={{0,3},{1,2},{2,1},{3,0},{4,7},{5,6},{6,5},{7,4},{8,11},{9,10},{10,... | collective-permute-start | bytes 552968 | tf_op jit(solution)/shard_map/ppermute | solution.py:520
  118.9 7.8 %collective-permute-start.25 = (bf16[4,384,768]{2,1,0:T(8,128)(2,1)}, bf16[4,384,768]{2,1,0:T(8,128)(2,1)S(1)}, u32[]{:S(2)}, u32[]{:S(2)}) collective-permute-start(bf16[4,384,768]{2,1,0:T(8,128)(2,1)} %get-tuple-element.249), channel_id=1, source_target_pairs={{0,4},{4,0},{8,12},{12,8},{16,20},{20,16},{24,28},{28,24},{1,5},{5... | collective-permute-start | bytes 7077896 | tf_op jit(solution)/shard_map/ppermute | solution.py:520
  119.1 8.0 %collective-permute-start.26 = (bf16[4,384,768]{2,1,0:T(8,128)(2,1)}, bf16[4,384,768]{2,1,0:T(8,128)(2,1)S(1)}, u32[]{:S(2)}, u32[]{:S(2)}) collective-permute-start(bf16[4,384,768]{2,1,0:T(8,128)(2,1)} %get-tuple-element.250), channel_id=1, source_target_pairs={{0,4},{4,0},{8,12},{12,8},{16,20},{20,16},{24,28},{28,24},{1,5},{5... | collective-permute-start | bytes 7077896 | tf_op jit(solution)/shard_map/ppermute | solution.py:520
  129.0 28.2 %collective-permute-start.27 = (bf16[4,2,96,768]{3,2,1,0:T(8,128)(2,1)}, bf16[4,2,96,768]{3,2,1,0:T(8,128)(2,1)S(1)}, u32[]{:S(2)}, u32[]{:S(2)}) collective-permute-start(bf16[4,2,96,768]{3,2,1,0:T(8,128)(2,1)} %get-tuple-element.280), channel_id=1, source_target_pairs={{0,8},{4,12},{8,0},{12,4},{16,24},{20,28},{24,16},{28,20},{1,9},{5... | collective-permute-start | bytes 3538952 | tf_op jit(solution)/shard_map/ppermute | solution.py:520
  129.6 27.7 %collective-permute-start.28 = (bf16[4,2,96,768]{3,2,1,0:T(8,128)(2,1)S(1)}, bf16[4,2,96,768]{3,2,1,0:T(8,128)(2,1)S(1)}, u32[]{:S(2)}, u32[]{:S(2)}) collective-permute-start(bf16[4,2,96,768]{3,2,1,0:T(8,128)(2,1)S(1)} %get-tuple-element.281), channel_id=1, source_target_pairs={{0,16},{4,20},{8,24},{12,28},{16,0},{20,4},{24,8},{28,12},{1,17},{... | collective-permute-start | bytes 3538952 | tf_op jit(solution)/shard_map/ppermute | solution.py:520
  131.1 23.5 %collective-permute-start.29 = (bf16[3,40,768]{2,1,0:T(8,128)(2,1)S(1)}, bf16[3,40,768]{2,1,0:T(8,128)(2,1)S(1)}, u32[]{:S(2)}, u32[]{:S(2)}) collective-permute-start(bf16[3,40,768]{2,1,0:T(8,128)(2,1)S(1)} %copy-done.31), channel_id=1, source_target_pairs={{0,1},{1,0},{2,3},{3,2},{4,5},{5,4},{6,7},{7,6},{8,9},{9,8},{10,11... | collective-permute-start | bytes 552968 | tf_op jit(solution)/shard_map/ppermute | solution.py:520
  132.1 22.5 %collective-permute-start.30 = (bf16[3,40,768]{2,1,0:T(8,128)(2,1)S(1)}, bf16[3,40,768]{2,1,0:T(8,128)(2,1)S(1)}, u32[]{:S(2)}, u32[]{:S(2)}) collective-permute-start(bf16[3,40,768]{2,1,0:T(8,128)(2,1)S(1)} %copy-done.30), channel_id=1, source_target_pairs={{0,2},{1,3},{2,0},{3,1},{4,6},{5,7},{6,4},{7,5},{8,10},{9,11},{10,... | collective-permute-start | bytes 552968 | tf_op jit(solution)/shard_map/ppermute | solution.py:520
  133.8 20.8 %collective-permute-start.31 = (bf16[3,40,768]{2,1,0:T(8,128)(2,1)S(1)}, bf16[3,40,768]{2,1,0:T(8,128)(2,1)S(1)}, u32[]{:S(2)}, u32[]{:S(2)}) collective-permute-start(bf16[3,40,768]{2,1,0:T(8,128)(2,1)S(1)} %copy-done.29), channel_id=1, source_target_pairs={{0,3},{1,2},{2,1},{3,0},{4,7},{5,6},{6,5},{7,4},{8,11},{9,10},{10,... | collective-permute-start | bytes 552968 | tf_op jit(solution)/shard_map/ppermute | solution.py:520
  157.3 17.5 %collective-permute-start.34 = (bf16[2,4,192,768]{3,2,1,0:T(8,128)(2,1)}, bf16[2,4,192,768]{3,2,1,0:T(8,128)(2,1)S(1)}, u32[]{:S(2)}, u32[]{:S(2)}) collective-permute-start(bf16[2,4,192,768]{3,2,1,0:T(8,128)(2,1)} %get-tuple-element.296), channel_id=1, source_target_pairs={{0,4},{4,0},{8,12},{12,8},{16,20},{20,16},{24,28},{28,24},{1,5},{5... | collective-permute-start | bytes 7077896 | tf_op jit(solution)/shard_map/ppermute | solution.py:520
  157.8 15.8 %collective-permute-start.32 = (bf16[4,1,96,768]{3,2,1,0:T(8,128)(2,1)S(1)}, bf16[4,1,96,768]{3,2,1,0:T(8,128)(2,1)S(1)}, u32[]{:S(2)}, u32[]{:S(2)}) collective-permute-start(bf16[4,1,96,768]{3,2,1,0:T(8,128)(2,1)S(1)} %get-tuple-element.294), channel_id=1, source_target_pairs={{0,16},{4,20},{8,24},{12,28},{16,0},{20,4},{24,8},{28,12},{1,17},{... | collective-permute-start | bytes 1769480 | tf_op jit(solution)/shard_map/ppermute | solution.py:520
  159.4 15.5 %collective-permute-start.33 = (bf16[4,1,96,768]{3,2,1,0:T(8,128)(2,1)S(1)}, bf16[4,1,96,768]{3,2,1,0:T(8,128)(2,1)S(1)}, u32[]{:S(2)}, u32[]{:S(2)}) collective-permute-start(bf16[4,1,96,768]{3,2,1,0:T(8,128)(2,1)S(1)} %get-tuple-element.295), channel_id=1, source_target_pairs={{0,8},{4,12},{8,0},{12,4},{16,24},{20,28},{24,16},{28,20},{1,9},{5... | collective-permute-start | bytes 1769480 | tf_op jit(solution)/shard_map/ppermute | solution.py:520
  160.9 12.1 %collective-permute-start.35 = (bf16[3,40,768]{2,1,0:T(8,128)(2,1)S(1)}, bf16[3,40,768]{2,1,0:T(8,128)(2,1)S(1)}, u32[]{:S(2)}, u32[]{:S(2)}) collective-permute-start(bf16[3,40,768]{2,1,0:T(8,128)(2,1)S(1)} %copy-done.32), channel_id=1, source_target_pairs={{0,3},{1,2},{2,1},{3,0},{4,7},{5,6},{6,5},{7,4},{8,11},{9,10},{10,... | collective-permute-start | bytes 552968 | tf_op jit(solution)/shard_map/ppermute | solution.py:520
  163.0 10.0 %collective-permute-start.36 = (f32[16,768]{1,0:T(8,128)S(1)}, f32[16,768]{1,0:T(8,128)S(1)}, u32[]{:S(2)}, u32[]{:S(2)}) collective-permute-start(f32[16,768]{1,0:T(8,128)S(1)} %get-tuple-element.298), channel_id=1, source_target_pairs={{0,2},{1,3},{2,0},{3,1},{4,6},{5,7},{6,4},{7,5},{8,10},{9,11},{10,... | collective-permute-start | bytes 147464 | tf_op jit(solution)/shard_map/ppermute | solution.py:520
  175.7 18.7 %collective-permute-start.39 = (bf16[2,192,768]{2,1,0:T(8,128)(2,1)S(1)}, bf16[2,192,768]{2,1,0:T(8,128)(2,1)S(1)}, u32[]{:S(2)}, u32[]{:S(2)}) collective-permute-start(bf16[2,192,768]{2,1,0:T(8,128)(2,1)S(1)} %pad_maximum_fusion.11), channel_id=1, source_target_pairs={{0,1},{1,0},{2,3},{3,2},{4,5},{5,4},{6,7},{7,6},{8,9},{9,8},{10,11... | collective-permute-start | bytes 1769480 | tf_op jit(solution)/shard_map/ppermute | solution.py:520
  178.3 16.1 %collective-permute-start.37 = (bf16[4,2,48,768]{3,2,1,0:T(8,128)(2,1)S(1)}, bf16[4,2,48,768]{3,2,1,0:T(8,128)(2,1)S(1)}, u32[]{:S(2)}, u32[]{:S(2)}) collective-permute-start(bf16[4,2,48,768]{3,2,1,0:T(8,128)(2,1)S(1)} %get-tuple-element.304), channel_id=1, source_target_pairs={{0,8},{4,12},{8,0},{12,4},{16,24},{20,28},{24,16},{28,20},{1,9},{5... | collective-permute-start | bytes 1769480 | tf_op jit(solution)/shard_map/ppermute | solution.py:520
  179.8 14.6 %collective-permute-start.38 = (bf16[4,2,48,768]{3,2,1,0:T(8,128)(2,1)S(1)}, bf16[4,2,48,768]{3,2,1,0:T(8,128)(2,1)S(1)}, u32[]{:S(2)}, u32[]{:S(2)}) collective-permute-start(bf16[4,2,48,768]{3,2,1,0:T(8,128)(2,1)S(1)} %get-tuple-element.305), channel_id=1, source_target_pairs={{0,16},{4,20},{8,24},{12,28},{16,0},{20,4},{24,8},{28,12},{1,17},{... | collective-permute-start | bytes 1769480 | tf_op jit(solution)/shard_map/ppermute | solution.py:520
  180.3 13.7 %collective-permute-start.41 = (bf16[3,40,768]{2,1,0:T(8,128)(2,1)S(1)}, bf16[3,40,768]{2,1,0:T(8,128)(2,1)S(1)}, u32[]{:S(2)}, u32[]{:S(2)}) collective-permute-start(bf16[3,40,768]{2,1,0:T(8,128)(2,1)S(1)} %copy-done.28), channel_id=1, source_target_pairs={{0,2},{1,3},{2,0},{3,1},{4,6},{5,7},{6,4},{7,5},{8,10},{9,11},{10,... | collective-permute-start | bytes 552968 | tf_op jit(solution)/shard_map/ppermute | solution.py:520
  181.7 12.3 %collective-permute-start.40 = (f32[16,768]{1,0:T(8,128)S(1)}, f32[16,768]{1,0:T(8,128)S(1)}, u32[]{:S(2)}, u32[]{:S(2)}) collective-permute-start(f32[16,768]{1,0:T(8,128)S(1)} %add.145), channel_id=1, source_target_pairs={{0,8},{4,12},{8,0},{12,4},{16,24},{20,28},{24,16},{28,20},{1,9},{5... | collective-permute-start | bytes 147464 | tf_op jit(solution)/shard_map/ppermute | solution.py:520
  194.5 14.7 %collective-permute-start.44 = (bf16[192,768]{1,0:T(8,128)(2,1)S(1)}, bf16[192,768]{1,0:T(8,128)(2,1)S(1)}, u32[]{:S(2)}, u32[]{:S(2)}) collective-permute-start(bf16[192,768]{1,0:T(8,128)(2,1)S(1)} %fusion.1), channel_id=1, source_target_pairs={{0,2},{1,3},{2,0},{3,1},{4,6},{5,7},{6,4},{7,5},{8,10},{9,11},{10,... | collective-permute-start | bytes 884744 | tf_op jit(solution)/shard_map/ppermute | solution.py:520
  196.7 12.5 %collective-permute-start.42 = (bf16[4,1,48,768]{3,2,1,0:T(8,128)(2,1)S(1)}, bf16[4,1,48,768]{3,2,1,0:T(8,128)(2,1)S(1)}, u32[]{:S(2)}, u32[]{:S(2)}) collective-permute-start(bf16[4,1,48,768]{3,2,1,0:T(8,128)(2,1)S(1)} %get-tuple-element.325), channel_id=1, source_target_pairs={{0,16},{4,20},{8,24},{12,28},{16,0},{20,4},{24,8},{28,12},{1,17},{... | collective-permute-start | bytes 884744 | tf_op jit(solution)/shard_map/ppermute | solution.py:520
  197.3 11.8 %collective-permute-start.43 = (bf16[4,1,48,768]{3,2,1,0:T(8,128)(2,1)S(1)}, bf16[4,1,48,768]{3,2,1,0:T(8,128)(2,1)S(1)}, u32[]{:S(2)}, u32[]{:S(2)}) collective-permute-start(bf16[4,1,48,768]{3,2,1,0:T(8,128)(2,1)S(1)} %get-tuple-element.326), channel_id=1, source_target_pairs={{0,8},{4,12},{8,0},{12,4},{16,24},{20,28},{24,16},{28,20},{1,9},{5... | collective-permute-start | bytes 884744 | tf_op jit(solution)/shard_map/ppermute | solution.py:520
  198.1 7.4 %collective-permute-start.45 = (bf16[3,40,768]{2,1,0:T(8,128)(2,1)S(1)}, bf16[3,40,768]{2,1,0:T(8,128)(2,1)S(1)}, u32[]{:S(2)}, u32[]{:S(2)}) collective-permute-start(bf16[3,40,768]{2,1,0:T(8,128)(2,1)S(1)} %copy-done.27), channel_id=1, source_target_pairs={{0,1},{1,0},{2,3},{3,2},{4,5},{5,4},{6,7},{7,6},{8,9},{9,8},{10,11... | collective-permute-start | bytes 552968 | tf_op jit(solution)/shard_map/ppermute | solution.py:520
  209.7 7.8 %collective-permute-start.49 = (bf16[2,96,768]{2,1,0:T(8,128)(2,1)S(1)}, bf16[2,96,768]{2,1,0:T(8,128)(2,1)S(1)}, u32[]{:S(2)}, u32[]{:S(2)}) collective-permute-start(bf16[2,96,768]{2,1,0:T(8,128)(2,1)S(1)} %pad_maximum_fusion.18), channel_id=1, source_target_pairs={{0,1},{1,0},{2,3},{3,2},{4,5},{5,4},{6,7},{7,6},{8,9},{9,8},{10,11... | collective-permute-start | bytes 884744 | tf_op jit(solution)/shard_map/ppermute | solution.py:520
  217.7 10.5 %collective-permute-start.52 = (bf16[1,2,1,96,768]{4,3,2,1,0:T(8,128)(2,1)S(1)}, bf16[1,2,1,96,768]{4,3,2,1,0:T(8,128)(2,1)S(1)}, u32[]{:S(2)}, u32[]{:S(2)}) collective-permute-start(bf16[1,2,1,96,768]{4,3,2,1,0:T(8,128)(2,1)S(1)} %pad_maximum_fusion.21), channel_id=1, source_target_pairs={{0,8},{4,12},{8,0},{12,4},{16,24},{20,28},{24,16},{28,20},{1,9},{5... | collective-permute-start | bytes 884744 | tf_op jit(solution)/shard_map/ppermute | solution.py:520
  219.8 8.3 %collective-permute-start.51 = (bf16[1,1,2,96,768]{4,3,2,1,0:T(8,128)(2,1)S(1)}, bf16[1,1,2,96,768]{4,3,2,1,0:T(8,128)(2,1)S(1)}, u32[]{:S(2)}, u32[]{:S(2)}) collective-permute-start(bf16[1,1,2,96,768]{4,3,2,1,0:T(8,128)(2,1)S(1)} %pad_maximum_fusion.20), channel_id=1, source_target_pairs={{0,16},{4,20},{8,24},{12,28},{16,0},{20,4},{24,8},{28,12},{1,17},{... | collective-permute-start | bytes 884744 | tf_op jit(solution)/shard_map/ppermute | solution.py:520
  220.6 7.5 %collective-permute-start.53 = (bf16[96,768]{1,0:T(8,128)(2,1)S(1)}, bf16[96,768]{1,0:T(8,128)(2,1)S(1)}, u32[]{:S(2)}, u32[]{:S(2)}) collective-permute-start(bf16[96,768]{1,0:T(8,128)(2,1)S(1)} %fusion.3), channel_id=1, source_target_pairs={{0,2},{1,3},{2,0},{3,1},{4,6},{5,7},{6,4},{7,5},{8,10},{9,11},{10,... | collective-permute-start | bytes 442376 | tf_op jit(solution)/shard_map/ppermute | solution.py:520
  229.1 6.8 %collective-permute-start.55 = (bf16[96,768]{1,0:T(8,128)(2,1)S(1)}, bf16[96,768]{1,0:T(8,128)(2,1)S(1)}, u32[]{:S(2)}, u32[]{:S(2)}) collective-permute-start(bf16[96,768]{1,0:T(8,128)(2,1)S(1)} %fusion.2), channel_id=1, source_target_pairs={{0,8},{4,12},{8,0},{12,4},{16,24},{20,28},{24,16},{28,20},{1,9},{5... | collective-permute-start | bytes 442376 | tf_op jit(solution)/shard_map/ppermute | solution.py:520
  231.0 8.1 %collective-permute-start.57 = (bf16[96,768]{1,0:T(8,128)(2,1)S(1)}, bf16[96,768]{1,0:T(8,128)(2,1)S(1)}, u32[]{:S(2)}, u32[]{:S(2)}) collective-permute-start(bf16[96,768]{1,0:T(8,128)(2,1)S(1)} %fusion.2), channel_id=1, source_target_pairs={{0,24},{4,28},{8,16},{12,20},{16,8},{20,12},{24,0},{28,4},{1,25},{... | collective-permute-start | bytes 442376 | tf_op jit(solution)/shard_map/ppermute | solution.py:520
  (46 other events, 220.8 us)
where the time goes:
time: 244 us; the launch traced here: 243 us
  waiting for transfers between devices  92.1 us (38%)
  Pallas kernels  71.4 us (29%)
  starting transfers between devices  63.7 us (26%)
  local copies, waits for them, and re-layouts  9.43 us (4%)
  other arithmetic  5.07 us (2%)
    ppermute x61, waiting for transfers between devices, flip(): return lax.ppermute(array, axis, [(i, i ^ mask) for i in range(size)])  92.1 us
    pallas_call x8, Pallas kernels, call(): pl.pallas_call(kernel, grid_spec=spec, out_shape=[pltpu.HBM(a.shape, a.dt...  67 us
    ppermute x61, starting transfers between devices, flip(): return lax.ppermute(array, axis, [(i, i ^ mask) for i in range(size)])  63.7 us
  transfers between devices with their start and end apart: 61, of which 30 were waited for; matrix products, arithmetic and copies ran while one was open for 4% of the time, Pallas kernels for 19%

commit v1 on v0

--- a/solution.py
+++ b/solution.py
@@ -610,6 +610,7 @@
     bits, _ = outer_bits()
     order = list(range(1 << len(bits)))
     if len(order) <= 4:
+        order = order[:1] + order[:0:-1]
         return [piece] + [flip(piece, "dp", 2 * k) for k in order[1:]], order
     held = piece[None]
     for bit in bits:
@@ -759,7 +760,7 @@
         partial(attention_kernel, pairs),
         mp,
         "attention",
-        32,
+        24,
         [
             (whole, x),
             *head_args,
@@ -795,7 +796,7 @@
         partial(ffn_kernel, mp),
         1,
         "ffn",
-        44,
+        42,
         [
             (where_it_is, hidden_low),
             (where_it_is, normed_one),
@@ -848,7 +849,7 @@
         partial(ffn_back_kernel, mp),
         1,
         "ffn_back",
-        28,
+        18,
         [
             (where_it_is, pre_grad),
             (where_it_is, w_in),
@@ -882,7 +883,7 @@
         partial(attention_back_kernel, pairs),
         mp,
         "attention_back",
-        40,
+        28,
         [
             (whole, x),
             (whole, attn_low),
@@ -914,16 +915,6 @@
     qk_keep, vo_keep, att_send, sums = results[:4]
     row_sends = results[4:]
     got, out_got, att_send, row_sends, sums = tie(got, out_got, att_send, row_sends, sums)
-    for step in range(1, ffn.steps):
-        ffn.take(got)
-        packs = ffn.pack(step)
-        got = ffn.send(step, packs)
-        if step == 1:
-            att_got = flip(att_send, "dp", 1)
-            row_three = flip(row_sends[3], "mp", 3)
-            sums_got = flip(sums, "mp", 2)
-        got, att_got, row_three, sums_got, row_sends = tie(got, att_got, row_three, sums_got, row_sends)
-    sums = sums + sums_got
     place = lambda blocks, dtype: call(
         partial(place_kernel, pairs),
         1,
@@ -934,20 +925,30 @@
         [],
         here,
     )[0]
-    layer_out = place(out_got, BF16)
+    for step in range(1, ffn.steps):
+        ffn.take(got)
+        packs = ffn.pack(step)
+        got = ffn.send(step, packs)
+        if step == 1:
+            att_got = flip(att_send, "dp", 1)
+            row_three = flip(row_sends[3], "mp", 3)
+            sums_got = flip(sums, "mp", 2)
+            att = Reduce([qk_keep, vo_keep], [att_got[0], att_got[1]])
+            att_packs = att.pack(0)
+            layer_out = place(out_got, BF16)
+        got, att_packs, row_three, sums_got, row_sends, layer_out = tie(
+            got, att_packs, row_three, sums_got, row_sends, layer_out
+        )
+    sums = sums + sums_got
     ffn.take(got)
     ffn_parts = ffn.finish()
     ffn_odd = jnp.concatenate([p[1::2] for p in ffn_parts], axis=1)
     ffn_even = jnp.concatenate([p[0::2] for p in ffn_parts], axis=1)
-    att = Reduce([qk_keep, vo_keep], [att_got[0], att_got[1]])
-    ffn_odd, ffn_even, sums = tie(ffn_odd, ffn_even, sums)
-    got = att.send(0, att.pack(0))
+    got = att.send(0, att_packs)
     ffn_got = flip(ffn_odd, "mp", 1)
     sums_got = flip(sums, "dp", 2)
     row_two = flip(row_sends[2], "mp", 2)
-    got, ffn_got, sums_got, row_two, row_sends, layer_out = tie(
-        got, ffn_got, sums_got, row_two, row_sends, layer_out
-    )
+    got, ffn_got, sums_got, row_two, row_sends = tie(got, ffn_got, sums_got, row_two, row_sends)
     sums = sums + sums_got
     for mask in [1 << b for b in range(2, dp.bit_length() - 2)]:
         sums = sums + flip(sums, "dp", mask)

time: 244 us -> 243 us (level)
  transfers between devices with their start and end apart: 61 -> 61, of which waited for: 30 -> 32; matrix products, arithmetic and copies ran while one was open for 4% -> 4% of each run, Pallas kernels for 19% -> 19%
where the time goes in v1:
time: 243 us; the launch traced here: 242 us
  waiting for transfers between devices  91.4 us (38%)
  Pallas kernels  70.3 us (29%)
  starting transfers between devices  63.5 us (26%)
  local copies, waits for them, and re-layouts  10.5 us (4%)
  other arithmetic  5.03 us (2%)
    ppermute x61, waiting for transfers between devices, flip(): return lax.ppermute(array, axis, [(i, i ^ mask) for i in range(size)])  91.4 us
    pallas_call x8, Pallas kernels, call(): pl.pallas_call(kernel, grid_spec=spec, out_shape=[pltpu.HBM(a.shape, a.dt...  66.7 us
    ppermute x61, starting transfers between devices, flip(): return lax.ppermute(array, axis, [(i, i ^ mask) for i in range(size)])  63.5 us
  transfers between devices with their start and end apart: 61, of which 32 were waited for; matrix products, arithmetic and copies ran while one was open for 4% of the time, Pallas kernels for 19%

profile of v1, /device:TPU:0, one launch (start us, length us, event | category | flops | bytes accessed | tf_op | source)
XLA Modules:
  0.0 242.5 jit_solution(18305000995503755945)
XLA Ops:
  1.8 3.1 %collective-permute-start = (bf16[96,768]{1,0:T(8,128)(2,1)S(1)}, bf16[96,768]{1,0:T(8,128)(2,1)S(1)}, u32[]{:S(2)}, u32[]{:S(2)}) collective-permute-start(bf16[96,768]{1,0:T(8,128)(2,1)S(1)} %pad_maximum_fusion.22), channel_id=1, source_target_pairs={{0,1},{1,0},{2,3},{3,2},{4,5},{5,4},{6,7},{7,6},{8,9},{9,8},{10,11... | collective-permute-start | bytes 442376 | tf_op jit(solution)/shard_map/ppermute | solution.py:520
  4.9 2.6 %collective-permute-start.1 = (bf16[96,768]{1,0:T(8,128)(2,1)S(1)}, bf16[96,768]{1,0:T(8,128)(2,1)}, u32[]{:S(2)}, u32[]{:S(2)}) collective-permute-start(bf16[96,768]{1,0:T(8,128)(2,1)S(1)} %pad_maximum_fusion.22), channel_id=1, source_target_pairs={{0,2},{1,3},{2,0},{3,1},{4,6},{5,7},{6,4},{7,5},{8,10},{9,11},{10,... | collective-permute-start | bytes 442376 | tf_op jit(solution)/shard_map/ppermute | solution.py:520
  14.2 4.8 %collective-permute-done.1 = bf16[96,768]{1,0:T(8,128)(2,1)} collective-permute-done((bf16[96,768]{1,0:T(8,128)(2,1)S(1)}, bf16[96,768]{1,0:T(8,128)(2,1)}, u32[]{:S(2)}, u32[]{:S(2)}) %collective-permute-start.1) | collective-permute-done | bytes 147488 | tf_op jit(solution)/shard_map/ppermute | solution.py:520
  20.1 1.6 collective-permute-start.5
  21.7 3.3 %collective-permute-start.3 = (bf16[200,768]{1,0:T(8,128)(2,1)S(1)}, bf16[200,768]{1,0:T(8,128)(2,1)S(1)}, u32[]{:S(2)}, u32[]{:S(2)}) collective-permute-start(bf16[200,768]{1,0:T(8,128)(2,1)S(1)} %concatenate.71), channel_id=1, source_target_pairs={{0,2},{1,3},{2,0},{3,1},{4,6},{5,7},{6,4},{7,5},{8,10},{9,11},{10,... | collective-permute-start | bytes 921608 | tf_op jit(solution)/shard_map/ppermute | solution.py:520
  25.0 1.6 collective-permute-start.4
  26.6 7.8 %collective-permute-done.6 = bf16[3,40,768]{2,1,0:T(8,128)(2,1)S(1)} collective-permute-done((bf16[3,40,768]{2,1,0:T(8,128)(2,1)}, bf16[3,40,768]{2,1,0:T(8,128)(2,1)S(1)}, u32[]{:S(2)}, u32[]{:S(2)}) %collective-permute-start.6) | collective-permute-done | bytes 184352 | tf_op jit(solution)/shard_map/ppermute | solution.py:520
  34.4 3.2 %collective-permute-done.3 = bf16[200,768]{1,0:T(8,128)(2,1)S(1)} collective-permute-done((bf16[200,768]{1,0:T(8,128)(2,1)S(1)}, bf16[200,768]{1,0:T(8,128)(2,1)S(1)}, u32[]{:S(2)}, u32[]{:S(2)}) %collective-permute-start.3) | collective-permute-done | bytes 307232 | tf_op jit(solution)/shard_map/ppermute | solution.py:520
  37.8 1.6 collective-permute-start.8
  41.4 14.2 %collective-permute-done.10 = bf16[3,40,768]{2,1,0:T(8,128)(2,1)S(1)} collective-permute-done((bf16[3,40,768]{2,1,0:T(8,128)(2,1)S(1)}, bf16[3,40,768]{2,1,0:T(8,128)(2,1)S(1)}, u32[]{:S(2)}, u32[]{:S(2)}) %collective-permute-start.10) | collective-permute-done | bytes 184352 | tf_op jit(solution)/shard_map/ppermute | solution.py:520
  58.3 1.6 collective-permute-start.11
  59.9 10.3 %collective-permute-done.15 = bf16[3,40,768]{2,1,0:T(8,128)(2,1)S(1)} collective-permute-done((bf16[3,40,768]{2,1,0:T(8,128)(2,1)S(1)}, bf16[3,40,768]{2,1,0:T(8,128)(2,1)S(1)}, u32[]{:S(2)}, u32[]{:S(2)}) %collective-permute-start.15) | collective-permute-done | bytes 184352 | tf_op jit(solution)/shard_map/ppermute | solution.py:520
  71.2 1.5 collective-permute-start.17
  72.7 1.5 collective-permute-start.16
  74.4 2.7 %collective-permute-start.21 = (bf16[3,40,768]{2,1,0:T(8,128)(2,1)S(1)}, bf16[3,40,768]{2,1,0:T(8,128)(2,1)S(1)}, u32[]{:S(2)}, u32[]{:S(2)}) collective-permute-start(bf16[3,40,768]{2,1,0:T(8,128)(2,1)S(1)} %get-tuple-element.231), channel_id=1, source_target_pairs={{0,2},{1,3},{2,0},{3,1},{4,6},{5,7},{6,4},{7,5},{8,10},{9,11},{10,... | collective-permute-start | bytes 552968 | tf_op jit(solution)/shard_map/ppermute | solution.py:520
  77.0 1.7 collective-permute-start.22
  78.7 11.9 %attention.1 = (bf16[4,480,192]{2,1,0:T(8,128)(2,1)}, bf16[4,480,192]{2,1,0:T(8,128)(2,1)}, bf16[4,480,192]{2,1,0:T(8,128)(2,1)}, f32[4,3,480,160]{3,2,1,0:T(8,1...) custom-call(s32[3]{0:T(128)S(1)} %pad_add_fusion.here_ref, ...), custom_call_target="tpu_custom_call" | custom-call | tf_op jit(solution)/shard_map/attention/pallas_call | solution.py:448
  90.7 2.2 collective-permute-done.17
  98.7 20.1 %ffn.1 = (bf16[3,40,768]{2,1,0:T(8,128)(2,1)}, bf16[3,40,768]{2,1,0:T(8,128)(2,1)}, bf16[3,40,768]{2,1,0:T(8,128)(2,1)}, bf16[3,40,768]{2,1,0:T(8,128)(2,1)}, f3...) custom-call(s32[3]{0:T(128)S(1)} %pad_add_fusion.here_ref, ...), custom_call_target="tpu_custom_call" | custom-call | tf_op jit(solution)/shard_map/ffn/pallas_call | solution.py:448
  119.4 7.2 %ffn_back.1 = (f32[480,768]{1,0:T(8,128)}, bf16[480,768]{1,0:T(8,128)(2,1)S(1)}, f32[8,768]{1,0:T(8,128)S(1)}) custom-call(s32[3]{0:T(128)S(1)} %pad_add_fusion.here_ref, bf16[4,480,768]{2,1,0:T(8,128)(2,1)} %get-tuple-element.253.pre_grad_hbm, bf16[768,768]{1,0:T(8,128)(2,1)} %w_in_hbm.3, bf16[3,384,768]{2,1,0:T(8,128)(2,1)S(1)} %bitcast.139, ...), custom_call_target="tpu_custom_call" | custom-call | tf_op jit(solution)/shard_map/ffn_back/pallas_call | solution.py:448
  128.8 1.5 collective-permute-start.28
  131.4 1.6 collective-permute-start.30
  133.0 1.7 collective-permute-start.31
  134.8 18.9 %attention_back.1 = (bf16[4,192,768]{2,1,0:T(8,128)(2,1)}, bf16[4,192,768]{2,1,0:T(8,128)(2,1)}, bf16[2,4,192,768]{3,2,1,0:T(8,128)(2,1)}, f32[16,768]{1,0:T(8,1...) custom-call(s32[3]{0:T(128)S(1)} %pad_add_fusion.here_ref, ...), custom_call_target="tpu_custom_call" | custom-call | tf_op jit(solution)/shard_map/attention_back/pallas_call | solution.py:448
  153.7 2.6 %collective-permute-done.27.refs_3_ = bf16[4,2,96,768]{3,2,1,0:T(8,128)(2,1)S(1)} collective-permute-done((bf16[4,2,96,768]{3,2,1,0:T(8,128)(2,1)S(1)}, bf16[4,2,96,768]{3,2,1,0:T(8,128)(2,1)S(1)}, u32[]{:S(2)}, u32[]{:S(2)}) %collective-permute-start.27) | collective-permute-done | bytes 1179680 | tf_op jit(solution)/shard_map/ppermute | solution.py:520
  157.0 1.6 collective-permute-start.32
  158.6 1.5 collective-permute-start.33
  160.1 2.1 collective-permute-start.35
  162.2 1.5 place.2
  166.2 5.9 %collective-permute-done.36 = f32[16,768]{1,0:T(8,128)S(1)} collective-permute-done((f32[16,768]{1,0:T(8,128)S(1)}, f32[16,768]{1,0:T(8,128)S(1)}, u32[]{:S(2)}, u32[]{:S(2)}) %collective-permute-start.36) | collective-permute-done | bytes 49184 | tf_op jit(solution)/shard_map/ppermute | solution.py:520
  177.0 2.6 %collective-permute-start.41 = (bf16[3,40,768]{2,1,0:T(8,128)(2,1)S(1)}, bf16[3,40,768]{2,1,0:T(8,128)(2,1)S(1)}, u32[]{:S(2)}, u32[]{:S(2)}) collective-permute-start(bf16[3,40,768]{2,1,0:T(8,128)(2,1)S(1)} %copy-done.26), channel_id=1, source_target_pairs={{0,2},{1,3},{2,0},{3,1},{4,6},{5,7},{6,4},{7,5},{8,10},{9,11},{10,... | collective-permute-start | bytes 552968 | tf_op jit(solution)/shard_map/ppermute | solution.py:520
  180.1 11.2 %collective-permute-done.40 = f32[16,768]{1,0:T(8,128)S(1)} collective-permute-done((f32[16,768]{1,0:T(8,128)S(1)}, f32[16,768]{1,0:T(8,128)S(1)}, u32[]{:S(2)}, u32[]{:S(2)}) %collective-permute-start.40) | collective-permute-done | bytes 49184 | tf_op jit(solution)/shard_map/ppermute | solution.py:520
  192.0 1.5 collective-permute-done.39
  193.6 2.0 collective-permute-start.44
  197.2 1.5 collective-permute-start.45
  200.1 3.9 %collective-permute-done.46 = f32[16,768]{1,0:T(8,128)S(1)} collective-permute-done((f32[16,768]{1,0:T(8,128)S(1)}, f32[16,768]{1,0:T(8,128)S(1)}, u32[]{:S(2)}, u32[]{:S(2)}) %collective-permute-start.46) | collective-permute-done | bytes 49184 | tf_op jit(solution)/shard_map/ppermute | solution.py:520
  204.6 3.6 %collective-permute-done.44 = bf16[192,768]{1,0:T(8,128)(2,1)S(1)} collective-permute-done((bf16[192,768]{1,0:T(8,128)(2,1)S(1)}, bf16[192,768]{1,0:T(8,128)(2,1)S(1)}, u32[]{:S(2)}, u32[]{:S(2)}) %collective-permute-start.44) | collective-permute-done | bytes 294944 | tf_op jit(solution)/shard_map/ppermute | solution.py:520
  208.9 1.5 collective-permute-start.47
  212.7 1.5 collective-permute-done.47
  214.2 1.5 collective-permute-done.48
  216.8 2.0 collective-permute-start.52
  221.1 1.7 collective-permute-start.54
  222.9 1.7 place.3
  225.2 2.0 collective-permute-done.53
  230.0 1.7 collective-permute-start.57
  231.7 3.1 %unit_grads.1 = (f32[768,768]{1,0:T(8,128)}, f32[768,768]{1,0:T(8,128)}) custom-call(s32[3]{0:T(128)S(1)} %pad_add_fusion.here_ref, bf16[1,384,768]{2,1,0:T(8,128)(2,1)S(1)} %bitcast.163, bf16[1,384,768]{2,1,0:T(8,128)(2,1)S(1)} %bitcast.161, bf16[1,384,768]{2,1,0:T(8,128)(2,1)S(1)} %collective-permute-done.58.in_other, ...), custom_call_target="tpu_custom_call" | custom-call | tf_op jit(solution)/shard_map/unit_grads/pallas_call | solution.py:448
  235.9 2.2 collective-permute-done.56
  240.3 2.2 head_grads.1
  (251 shorter events, 50.0 us)
Async XLA Ops:
  1.8 12.4 %collective-permute-start = (bf16[96,768]{1,0:T(8,128)(2,1)S(1)}, bf16[96,768]{1,0:T(8,128)(2,1)S(1)}, u32[]{:S(2)}, u32[]{:S(2)}) collective-permute-start(bf16[96,768]{1,0:T(8,128)(2,1)S(1)} %pad_maximum_fusion.22), channel_id=1, source_target_pairs={{0,1},{1,0},{2,3},{3,2},{4,5},{5,4},{6,7},{7,6},{8,9},{9,8},{10,11... | collective-permute-start | bytes 442376 | tf_op jit(solution)/shard_map/ppermute | solution.py:520
  4.9 14.1 %collective-permute-start.1 = (bf16[96,768]{1,0:T(8,128)(2,1)S(1)}, bf16[96,768]{1,0:T(8,128)(2,1)}, u32[]{:S(2)}, u32[]{:S(2)}) collective-permute-start(bf16[96,768]{1,0:T(8,128)(2,1)S(1)} %pad_maximum_fusion.22), channel_id=1, source_target_pairs={{0,2},{1,3},{2,0},{3,1},{4,6},{5,7},{6,4},{7,5},{8,10},{9,11},{10,... | collective-permute-start | bytes 442376 | tf_op jit(solution)/shard_map/ppermute | solution.py:520
  7.5 11.5 %collective-permute-start.2 = (bf16[96,768]{1,0:T(8,128)(2,1)S(1)}, bf16[96,768]{1,0:T(8,128)(2,1)}, u32[]{:S(2)}, u32[]{:S(2)}) collective-permute-start(bf16[96,768]{1,0:T(8,128)(2,1)S(1)} %pad_maximum_fusion.22), channel_id=1, source_target_pairs={{0,3},{1,2},{2,1},{3,0},{4,7},{5,6},{6,5},{7,4},{8,11},{9,10},{10,... | collective-permute-start | bytes 442376 | tf_op jit(solution)/shard_map/ppermute | solution.py:520
  20.1 14.3 %collective-permute-start.5 = (bf16[3,1,1,48,768]{4,3,0,2,1:T(8,128)(2,1)S(1)}, bf16[3,1,1,48,768]{4,3,0,2,1:T(8,128)(2,1)S(1)}, u32[]{:S(2)}, u32[]{:S(2)}) collective-permute-start(bf16[3,1,1,48,768]{4,3,0,2,1:T(8,128)(2,1)S(1)} %maximum_bitcast_fusion.3), channel_id=1, source_target_pairs={{0,16},{4,20},{8,24},{12,28},{16,0},{20,4},{24,8},{28,12},{1,17},{... | collective-permute-start | bytes 663560 | tf_op jit(solution)/shard_map/ppermute | solution.py:520
  21.7 15.9 %collective-permute-start.3 = (bf16[200,768]{1,0:T(8,128)(2,1)S(1)}, bf16[200,768]{1,0:T(8,128)(2,1)S(1)}, u32[]{:S(2)}, u32[]{:S(2)}) collective-permute-start(bf16[200,768]{1,0:T(8,128)(2,1)S(1)} %concatenate.71), channel_id=1, source_target_pairs={{0,2},{1,3},{2,0},{3,1},{4,6},{5,7},{6,4},{7,5},{8,10},{9,11},{10,... | collective-permute-start | bytes 921608 | tf_op jit(solution)/shard_map/ppermute | solution.py:520
  25.0 9.4 %collective-permute-start.4 = (bf16[3,1,1,48,768]{4,3,0,2,1:T(8,128)(2,1)S(1)}, bf16[3,1,1,48,768]{4,3,0,2,1:T(8,128)(2,1)S(1)}, u32[]{:S(2)}, u32[]{:S(2)}) collective-permute-start(bf16[3,1,1,48,768]{4,3,0,2,1:T(8,128)(2,1)S(1)} %maximum_bitcast_fusion.2), channel_id=1, source_target_pairs={{0,8},{4,12},{8,0},{12,4},{16,24},{20,28},{24,16},{28,20},{1,9},{5... | collective-permute-start | bytes 663560 | tf_op jit(solution)/shard_map/ppermute | solution.py:520
  26.6 7.8 %collective-permute-start.6 = (bf16[3,40,768]{2,1,0:T(8,128)(2,1)}, bf16[3,40,768]{2,1,0:T(8,128)(2,1)S(1)}, u32[]{:S(2)}, u32[]{:S(2)}) collective-permute-start(bf16[3,40,768]{2,1,0:T(8,128)(2,1)} %get-tuple-element.193), channel_id=1, source_target_pairs={{0,1},{1,0},{2,3},{3,2},{4,5},{5,4},{6,7},{7,6},{8,9},{9,8},{10,11... | collective-permute-start | bytes 552968 | tf_op jit(solution)/shard_map/ppermute | solution.py:520
  37.7 18.8 %collective-permute-start.9 = (bf16[2,200,768]{2,1,0:T(8,128)(2,1)S(1)}, bf16[2,200,768]{2,1,0:T(8,128)(2,1)S(1)}, u32[]{:S(2)}, u32[]{:S(2)}) collective-permute-start(bf16[2,200,768]{2,1,0:T(8,128)(2,1)S(1)} %pad_maximum_fusion.9), channel_id=1, source_target_pairs={{0,1},{1,0},{2,3},{3,2},{4,5},{5,4},{6,7},{7,6},{8,9},{9,8},{10,11... | collective-permute-start | bytes 1843208 | tf_op jit(solution)/shard_map/ppermute | solution.py:520
  37.8 17.7 %collective-permute-start.8 = (bf16[3,2,1,48,768]{4,3,0,2,1:T(8,128)(2,1)S(1)}, bf16[3,2,1,48,768]{4,3,0,2,1:T(8,128)(2,1)S(1)}, u32[]{:S(2)}, u32[]{:S(2)}) collective-permute-start(bf16[3,2,1,48,768]{4,3,0,2,1:T(8,128)(2,1)S(1)} %pad_maximum_fusion.16), channel_id=1, source_target_pairs={{0,8},{4,12},{8,0},{12,4},{16,24},{20,28},{24,16},{28,20},{1,9},{5... | collective-permute-start | bytes 1327112 | tf_op jit(solution)/shard_map/ppermute | solution.py:520
  39.5 16.1 %collective-permute-start.7 = (bf16[3,1,2,48,768]{4,3,0,2,1:T(8,128)(2,1)S(1)}, bf16[3,1,2,48,768]{4,3,0,2,1:T(8,128)(2,1)S(1)}, u32[]{:S(2)}, u32[]{:S(2)}) collective-permute-start(bf16[3,1,2,48,768]{4,3,0,2,1:T(8,128)(2,1)S(1)} %pad_maximum_fusion.15), channel_id=1, source_target_pairs={{0,16},{4,20},{8,24},{12,28},{16,0},{20,4},{24,8},{28,12},{1,17},{... | collective-permute-start | bytes 1327112 | tf_op jit(solution)/shard_map/ppermute | solution.py:520
  40.2 15.4 %collective-permute-start.10 = (bf16[3,40,768]{2,1,0:T(8,128)(2,1)S(1)}, bf16[3,40,768]{2,1,0:T(8,128)(2,1)S(1)}, u32[]{:S(2)}, u32[]{:S(2)}) collective-permute-start(bf16[3,40,768]{2,1,0:T(8,128)(2,1)S(1)} %copy-done.16), channel_id=1, source_target_pairs={{0,3},{1,2},{2,1},{3,0},{4,7},{5,6},{6,5},{7,4},{8,11},{9,10},{10,... | collective-permute-start | bytes 552968 | tf_op jit(solution)/shard_map/ppermute | solution.py:520
  56.7 13.5 %collective-permute-start.14 = (bf16[3,192,768]{2,1,0:T(8,128)(2,1)S(1)}, bf16[3,192,768]{2,1,0:T(8,128)(2,1)S(1)}, u32[]{:S(2)}, u32[]{:S(2)}) collective-permute-start(bf16[3,192,768]{2,1,0:T(8,128)(2,1)S(1)} %bitcast.148), channel_id=1, source_target_pairs={{0,4},{4,0},{8,12},{12,8},{16,20},{20,16},{24,28},{28,24},{1,5},{5... | collective-permute-start | bytes 2654216 | tf_op jit(solution)/shard_map/ppermute | solution.py:520
  57.1 13.2 %collective-permute-start.13 = (bf16[3,192,768]{2,1,0:T(8,128)(2,1)S(1)}, bf16[3,192,768]{2,1,0:T(8,128)(2,1)S(1)}, u32[]{:S(2)}, u32[]{:S(2)}) collective-permute-start(bf16[3,192,768]{2,1,0:T(8,128)(2,1)S(1)} %bitcast.151), channel_id=1, source_target_pairs={{0,4},{4,0},{8,12},{12,8},{16,20},{20,16},{24,28},{28,24},{1,5},{5... | collective-permute-start | bytes 2654216 | tf_op jit(solution)/shard_map/ppermute | solution.py:520
  57.7 12.5 %collective-permute-start.12 = (bf16[3,1,1,96,768]{4,3,0,2,1:T(8,128)(2,1)S(1)}, bf16[3,1,1,96,768]{4,3,0,2,1:T(8,128)(2,1)S(1)}, u32[]{:S(2)}, u32[]{:S(2)}) collective-permute-start(bf16[3,1,1,96,768]{4,3,0,2,1:T(8,128)(2,1)S(1)} %maximum_bitcast_fusion.1), channel_id=1, source_target_pairs={{0,16},{4,20},{8,24},{12,28},{16,0},{20,4},{24,8},{28,12},{1,17},{... | collective-permute-start | bytes 1327112 | tf_op jit(solution)/shard_map/ppermute | solution.py:520
  58.3 11.9 %collective-permute-start.11 = (bf16[3,1,1,96,768]{4,3,0,2,1:T(8,128)(2,1)S(1)}, bf16[3,1,1,96,768]{4,3,0,2,1:T(8,128)(2,1)S(1)}, u32[]{:S(2)}, u32[]{:S(2)}) collective-permute-start(bf16[3,1,1,96,768]{4,3,0,2,1:T(8,128)(2,1)S(1)} %maximum_bitcast_fusion), channel_id=1, source_target_pairs={{0,8},{4,12},{8,0},{12,4},{16,24},{20,28},{24,16},{28,20},{1,9},{5... | collective-permute-start | bytes 1327112 | tf_op jit(solution)/shard_map/ppermute | solution.py:520
  59.9 10.3 %collective-permute-start.15 = (bf16[3,40,768]{2,1,0:T(8,128)(2,1)S(1)}, bf16[3,40,768]{2,1,0:T(8,128)(2,1)S(1)}, u32[]{:S(2)}, u32[]{:S(2)}) collective-permute-start(bf16[3,40,768]{2,1,0:T(8,128)(2,1)S(1)} %copy-done.15), channel_id=1, source_target_pairs={{0,2},{1,3},{2,0},{3,1},{4,6},{5,7},{6,4},{7,5},{8,10},{9,11},{10,... | collective-permute-start | bytes 552968 | tf_op jit(solution)/shard_map/ppermute | solution.py:520
  71.2 21.6 %collective-permute-start.17 = (bf16[3,2,1,96,768]{4,3,0,2,1:T(8,128)(2,1)S(1)}, bf16[3,2,1,96,768]{4,3,0,2,1:T(8,128)(2,1)S(1)}, u32[]{:S(2)}, u32[]{:S(2)}) collective-permute-start(bf16[3,2,1,96,768]{4,3,0,2,1:T(8,128)(2,1)S(1)} %pad_maximum_fusion.7), channel_id=1, source_target_pairs={{0,8},{4,12},{8,0},{12,4},{16,24},{20,28},{24,16},{28,20},{1,9},{5... | collective-permute-start | bytes 2654216 | tf_op jit(solution)/shard_map/ppermute | solution.py:520
  72.7 21.4 %collective-permute-start.16 = (bf16[3,1,2,96,768]{4,3,0,2,1:T(8,128)(2,1)S(1)}, bf16[3,1,2,96,768]{4,3,0,2,1:T(8,128)(2,1)S(1)}, u32[]{:S(2)}, u32[]{:S(2)}) collective-permute-start(bf16[3,1,2,96,768]{4,3,0,2,1:T(8,128)(2,1)S(1)} %pad_maximum_fusion.6), channel_id=1, source_target_pairs={{0,16},{4,20},{8,24},{12,28},{16,0},{20,4},{24,8},{28,12},{1,17},{... | collective-permute-start | bytes 2654216 | tf_op jit(solution)/shard_map/ppermute | solution.py:520
  74.3 19.8 %collective-permute-start.20 = (bf16[3,40,768]{2,1,0:T(8,128)(2,1)S(1)}, bf16[3,40,768]{2,1,0:T(8,128)(2,1)S(1)}, u32[]{:S(2)}, u32[]{:S(2)}) collective-permute-start(bf16[3,40,768]{2,1,0:T(8,128)(2,1)S(1)} %get-tuple-element.230), channel_id=1, source_target_pairs={{0,1},{1,0},{2,3},{3,2},{4,5},{5,4},{6,7},{7,6},{8,9},{9,8},{10,11... | collective-permute-start | bytes 552968 | tf_op jit(solution)/shard_map/ppermute | solution.py:520
  74.4 19.7 %collective-permute-start.21 = (bf16[3,40,768]{2,1,0:T(8,128)(2,1)S(1)}, bf16[3,40,768]{2,1,0:T(8,128)(2,1)S(1)}, u32[]{:S(2)}, u32[]{:S(2)}) collective-permute-start(bf16[3,40,768]{2,1,0:T(8,128)(2,1)S(1)} %get-tuple-element.231), channel_id=1, source_target_pairs={{0,2},{1,3},{2,0},{3,1},{4,6},{5,7},{6,4},{7,5},{8,10},{9,11},{10,... | collective-permute-start | bytes 552968 | tf_op jit(solution)/shard_map/ppermute | solution.py:520
  77.0 17.0 %collective-permute-start.22 = (bf16[3,40,768]{2,1,0:T(8,128)(2,1)S(1)}, bf16[3,40,768]{2,1,0:T(8,128)(2,1)S(1)}, u32[]{:S(2)}, u32[]{:S(2)}) collective-permute-start(bf16[3,40,768]{2,1,0:T(8,128)(2,1)S(1)} %get-tuple-element.232), channel_id=1, source_target_pairs={{0,3},{1,2},{2,1},{3,0},{4,7},{5,6},{6,5},{7,4},{8,11},{9,10},{10,... | collective-permute-start | bytes 552968 | tf_op jit(solution)/shard_map/ppermute | solution.py:520
  118.8 7.8 %collective-permute-start.25 = (bf16[4,384,768]{2,1,0:T(8,128)(2,1)}, bf16[4,384,768]{2,1,0:T(8,128)(2,1)S(1)}, u32[]{:S(2)}, u32[]{:S(2)}) collective-permute-start(bf16[4,384,768]{2,1,0:T(8,128)(2,1)} %get-tuple-element.247), channel_id=1, source_target_pairs={{0,4},{4,0},{8,12},{12,8},{16,20},{20,16},{24,28},{28,24},{1,5},{5... | collective-permute-start | bytes 7077896 | tf_op jit(solution)/shard_map/ppermute | solution.py:520
  119.0 8.0 %collective-permute-start.26 = (bf16[4,384,768]{2,1,0:T(8,128)(2,1)}, bf16[4,384,768]{2,1,0:T(8,128)(2,1)S(1)}, u32[]{:S(2)}, u32[]{:S(2)}) collective-permute-start(bf16[4,384,768]{2,1,0:T(8,128)(2,1)} %get-tuple-element.248), channel_id=1, source_target_pairs={{0,4},{4,0},{8,12},{12,8},{16,20},{20,16},{24,28},{28,24},{1,5},{5... | collective-permute-start | bytes 7077896 | tf_op jit(solution)/shard_map/ppermute | solution.py:520
  128.2 28.1 %collective-permute-start.27 = (bf16[4,2,96,768]{3,2,1,0:T(8,128)(2,1)S(1)}, bf16[4,2,96,768]{3,2,1,0:T(8,128)(2,1)S(1)}, u32[]{:S(2)}, u32[]{:S(2)}) collective-permute-start(bf16[4,2,96,768]{3,2,1,0:T(8,128)(2,1)S(1)} %get-tuple-element.267), channel_id=1, source_target_pairs={{0,8},{4,12},{8,0},{12,4},{16,24},{20,28},{24,16},{28,20},{1,9},{5... | collective-permute-start | bytes 3538952 | tf_op jit(solution)/shard_map/ppermute | solution.py:520
  128.8 27.7 %collective-permute-start.28 = (bf16[4,2,96,768]{3,2,1,0:T(8,128)(2,1)S(1)}, bf16[4,2,96,768]{3,2,1,0:T(8,128)(2,1)S(1)}, u32[]{:S(2)}, u32[]{:S(2)}) collective-permute-start(bf16[4,2,96,768]{3,2,1,0:T(8,128)(2,1)S(1)} %get-tuple-element.268), channel_id=1, source_target_pairs={{0,16},{4,20},{8,24},{12,28},{16,0},{20,4},{24,8},{28,12},{1,17},{... | collective-permute-start | bytes 3538952 | tf_op jit(solution)/shard_map/ppermute | solution.py:520
  130.4 23.3 %collective-permute-start.29 = (bf16[3,40,768]{2,1,0:T(8,128)(2,1)S(1)}, bf16[3,40,768]{2,1,0:T(8,128)(2,1)S(1)}, u32[]{:S(2)}, u32[]{:S(2)}) collective-permute-start(bf16[3,40,768]{2,1,0:T(8,128)(2,1)S(1)} %copy-done.29), channel_id=1, source_target_pairs={{0,1},{1,0},{2,3},{3,2},{4,5},{5,4},{6,7},{7,6},{8,9},{9,8},{10,11... | collective-permute-start | bytes 552968 | tf_op jit(solution)/shard_map/ppermute | solution.py:520
  131.4 22.3 %collective-permute-start.30 = (bf16[3,40,768]{2,1,0:T(8,128)(2,1)S(1)}, bf16[3,40,768]{2,1,0:T(8,128)(2,1)S(1)}, u32[]{:S(2)}, u32[]{:S(2)}) collective-permute-start(bf16[3,40,768]{2,1,0:T(8,128)(2,1)S(1)} %copy-done.28), channel_id=1, source_target_pairs={{0,2},{1,3},{2,0},{3,1},{4,6},{5,7},{6,4},{7,5},{8,10},{9,11},{10,... | collective-permute-start | bytes 552968 | tf_op jit(solution)/shard_map/ppermute | solution.py:520
  133.0 20.7 %collective-permute-start.31 = (bf16[3,40,768]{2,1,0:T(8,128)(2,1)S(1)}, bf16[3,40,768]{2,1,0:T(8,128)(2,1)S(1)}, u32[]{:S(2)}, u32[]{:S(2)}) collective-permute-start(bf16[3,40,768]{2,1,0:T(8,128)(2,1)S(1)} %copy-done.27), channel_id=1, source_target_pairs={{0,3},{1,2},{2,1},{3,0},{4,7},{5,6},{6,5},{7,4},{8,11},{9,10},{10,... | collective-permute-start | bytes 552968 | tf_op jit(solution)/shard_map/ppermute | solution.py:520
  157.0 15.8 %collective-permute-start.32 = (bf16[4,1,96,768]{3,2,1,0:T(8,128)(2,1)S(1)}, bf16[4,1,96,768]{3,2,1,0:T(8,128)(2,1)S(1)}, u32[]{:S(2)}, u32[]{:S(2)}) collective-permute-start(bf16[4,1,96,768]{3,2,1,0:T(8,128)(2,1)S(1)} %get-tuple-element.291), channel_id=1, source_target_pairs={{0,16},{4,20},{8,24},{12,28},{16,0},{20,4},{24,8},{28,12},{1,17},{... | collective-permute-start | bytes 1769480 | tf_op jit(solution)/shard_map/ppermute | solution.py:520
  158.6 15.5 %collective-permute-start.33 = (bf16[4,1,96,768]{3,2,1,0:T(8,128)(2,1)S(1)}, bf16[4,1,96,768]{3,2,1,0:T(8,128)(2,1)S(1)}, u32[]{:S(2)}, u32[]{:S(2)}) collective-permute-start(bf16[4,1,96,768]{3,2,1,0:T(8,128)(2,1)S(1)} %get-tuple-element.292), channel_id=1, source_target_pairs={{0,8},{4,12},{8,0},{12,4},{16,24},{20,28},{24,16},{28,20},{1,9},{5... | collective-permute-start | bytes 1769480 | tf_op jit(solution)/shard_map/ppermute | solution.py:520
  160.1 12.1 %collective-permute-start.35 = (bf16[3,40,768]{2,1,0:T(8,128)(2,1)S(1)}, bf16[3,40,768]{2,1,0:T(8,128)(2,1)S(1)}, u32[]{:S(2)}, u32[]{:S(2)}) collective-permute-start(bf16[3,40,768]{2,1,0:T(8,128)(2,1)S(1)} %copy-done.30), channel_id=1, source_target_pairs={{0,3},{1,2},{2,1},{3,0},{4,7},{5,6},{6,5},{7,4},{8,11},{9,10},{10,... | collective-permute-start | bytes 552968 | tf_op jit(solution)/shard_map/ppermute | solution.py:520
  162.2 10.0 %collective-permute-start.36 = (f32[16,768]{1,0:T(8,128)S(1)}, f32[16,768]{1,0:T(8,128)S(1)}, u32[]{:S(2)}, u32[]{:S(2)}) collective-permute-start(f32[16,768]{1,0:T(8,128)S(1)} %get-tuple-element.299), channel_id=1, source_target_pairs={{0,2},{1,3},{2,0},{3,1},{4,6},{5,7},{6,4},{7,5},{8,10},{9,11},{10,... | collective-permute-start | bytes 147464 | tf_op jit(solution)/shard_map/ppermute | solution.py:520
  174.8 18.7 %collective-permute-start.39 = (bf16[2,192,768]{2,1,0:T(8,128)(2,1)S(1)}, bf16[2,192,768]{2,1,0:T(8,128)(2,1)S(1)}, u32[]{:S(2)}, u32[]{:S(2)}) collective-permute-start(bf16[2,192,768]{2,1,0:T(8,128)(2,1)S(1)} %pad_maximum_fusion.11), channel_id=1, source_target_pairs={{0,1},{1,0},{2,3},{3,2},{4,5},{5,4},{6,7},{7,6},{8,9},{9,8},{10,11... | collective-permute-start | bytes 1769480 | tf_op jit(solution)/shard_map/ppermute | solution.py:520
  175.9 17.6 %collective-permute-start.37 = (bf16[4,2,48,768]{3,2,1,0:T(8,128)(2,1)S(1)}, bf16[4,2,48,768]{3,2,1,0:T(8,128)(2,1)S(1)}, u32[]{:S(2)}, u32[]{:S(2)}) collective-permute-start(bf16[4,2,48,768]{3,2,1,0:T(8,128)(2,1)S(1)} %get-tuple-element.312), channel_id=1, source_target_pairs={{0,8},{4,12},{8,0},{12,4},{16,24},{20,28},{24,16},{28,20},{1,9},{5... | collective-permute-start | bytes 1769480 | tf_op jit(solution)/shard_map/ppermute | solution.py:520
  176.5 17.0 %collective-permute-start.38 = (bf16[4,2,48,768]{3,2,1,0:T(8,128)(2,1)S(1)}, bf16[4,2,48,768]{3,2,1,0:T(8,128)(2,1)S(1)}, u32[]{:S(2)}, u32[]{:S(2)}) collective-permute-start(bf16[4,2,48,768]{3,2,1,0:T(8,128)(2,1)S(1)} %get-tuple-element.313), channel_id=1, source_target_pairs={{0,16},{4,20},{8,24},{12,28},{16,0},{20,4},{24,8},{28,12},{1,17},{... | collective-permute-start | bytes 1769480 | tf_op jit(solution)/shard_map/ppermute | solution.py:520
  177.0 15.0 %collective-permute-start.41 = (bf16[3,40,768]{2,1,0:T(8,128)(2,1)S(1)}, bf16[3,40,768]{2,1,0:T(8,128)(2,1)S(1)}, u32[]{:S(2)}, u32[]{:S(2)}) collective-permute-start(bf16[3,40,768]{2,1,0:T(8,128)(2,1)S(1)} %copy-done.26), channel_id=1, source_target_pairs={{0,2},{1,3},{2,0},{3,1},{4,6},{5,7},{6,4},{7,5},{8,10},{9,11},{10,... | collective-permute-start | bytes 552968 | tf_op jit(solution)/shard_map/ppermute | solution.py:520
  179.6 11.8 %collective-permute-start.40 = (f32[16,768]{1,0:T(8,128)S(1)}, f32[16,768]{1,0:T(8,128)S(1)}, u32[]{:S(2)}, u32[]{:S(2)}) collective-permute-start(f32[16,768]{1,0:T(8,128)S(1)} %add.145), channel_id=1, source_target_pairs={{0,8},{4,12},{8,0},{12,4},{16,24},{20,28},{24,16},{28,20},{1,9},{5... | collective-permute-start | bytes 147464 | tf_op jit(solution)/shard_map/ppermute | solution.py:520
  193.6 14.7 %collective-permute-start.44 = (bf16[192,768]{1,0:T(8,128)(2,1)S(1)}, bf16[192,768]{1,0:T(8,128)(2,1)S(1)}, u32[]{:S(2)}, u32[]{:S(2)}) collective-permute-start(bf16[192,768]{1,0:T(8,128)(2,1)S(1)} %fusion.1), channel_id=1, source_target_pairs={{0,2},{1,3},{2,0},{3,1},{4,6},{5,7},{6,4},{7,5},{8,10},{9,11},{10,... | collective-permute-start | bytes 884744 | tf_op jit(solution)/shard_map/ppermute | solution.py:520
  195.8 12.5 %collective-permute-start.42 = (bf16[4,1,48,768]{3,2,1,0:T(8,128)(2,1)S(1)}, bf16[4,1,48,768]{3,2,1,0:T(8,128)(2,1)S(1)}, u32[]{:S(2)}, u32[]{:S(2)}) collective-permute-start(bf16[4,1,48,768]{3,2,1,0:T(8,128)(2,1)S(1)} %get-tuple-element.321), channel_id=1, source_target_pairs={{0,16},{4,20},{8,24},{12,28},{16,0},{20,4},{24,8},{28,12},{1,17},{... | collective-permute-start | bytes 884744 | tf_op jit(solution)/shard_map/ppermute | solution.py:520
  196.5 11.8 %collective-permute-start.43 = (bf16[4,1,48,768]{3,2,1,0:T(8,128)(2,1)S(1)}, bf16[4,1,48,768]{3,2,1,0:T(8,128)(2,1)S(1)}, u32[]{:S(2)}, u32[]{:S(2)}) collective-permute-start(bf16[4,1,48,768]{3,2,1,0:T(8,128)(2,1)S(1)} %get-tuple-element.322), channel_id=1, source_target_pairs={{0,8},{4,12},{8,0},{12,4},{16,24},{20,28},{24,16},{28,20},{1,9},{5... | collective-permute-start | bytes 884744 | tf_op jit(solution)/shard_map/ppermute | solution.py:520
  197.2 7.4 %collective-permute-start.45 = (bf16[3,40,768]{2,1,0:T(8,128)(2,1)S(1)}, bf16[3,40,768]{2,1,0:T(8,128)(2,1)S(1)}, u32[]{:S(2)}, u32[]{:S(2)}) collective-permute-start(bf16[3,40,768]{2,1,0:T(8,128)(2,1)S(1)} %copy-done.25), channel_id=1, source_target_pairs={{0,1},{1,0},{2,3},{3,2},{4,5},{5,4},{6,7},{7,6},{8,9},{9,8},{10,11... | collective-permute-start | bytes 552968 | tf_op jit(solution)/shard_map/ppermute | solution.py:520
  208.9 7.8 %collective-permute-start.49 = (bf16[2,96,768]{2,1,0:T(8,128)(2,1)S(1)}, bf16[2,96,768]{2,1,0:T(8,128)(2,1)S(1)}, u32[]{:S(2)}, u32[]{:S(2)}) collective-permute-start(bf16[2,96,768]{2,1,0:T(8,128)(2,1)S(1)} %pad_maximum_fusion.18), channel_id=1, source_target_pairs={{0,1},{1,0},{2,3},{3,2},{4,5},{5,4},{6,7},{7,6},{8,9},{9,8},{10,11... | collective-permute-start | bytes 884744 | tf_op jit(solution)/shard_map/ppermute | solution.py:520
  216.8 10.4 %collective-permute-start.52 = (bf16[1,2,1,96,768]{4,3,2,1,0:T(8,128)(2,1)S(1)}, bf16[1,2,1,96,768]{4,3,2,1,0:T(8,128)(2,1)S(1)}, u32[]{:S(2)}, u32[]{:S(2)}) collective-permute-start(bf16[1,2,1,96,768]{4,3,2,1,0:T(8,128)(2,1)S(1)} %pad_maximum_fusion.21), channel_id=1, source_target_pairs={{0,8},{4,12},{8,0},{12,4},{16,24},{20,28},{24,16},{28,20},{1,9},{5... | collective-permute-start | bytes 884744 | tf_op jit(solution)/shard_map/ppermute | solution.py:520
  218.9 8.3 %collective-permute-start.51 = (bf16[1,1,2,96,768]{4,3,2,1,0:T(8,128)(2,1)S(1)}, bf16[1,1,2,96,768]{4,3,2,1,0:T(8,128)(2,1)S(1)}, u32[]{:S(2)}, u32[]{:S(2)}) collective-permute-start(bf16[1,1,2,96,768]{4,3,2,1,0:T(8,128)(2,1)S(1)} %pad_maximum_fusion.20), channel_id=1, source_target_pairs={{0,16},{4,20},{8,24},{12,28},{16,0},{20,4},{24,8},{28,12},{1,17},{... | collective-permute-start | bytes 884744 | tf_op jit(solution)/shard_map/ppermute | solution.py:520
  219.7 7.5 %collective-permute-start.53 = (bf16[96,768]{1,0:T(8,128)(2,1)S(1)}, bf16[96,768]{1,0:T(8,128)(2,1)S(1)}, u32[]{:S(2)}, u32[]{:S(2)}) collective-permute-start(bf16[96,768]{1,0:T(8,128)(2,1)S(1)} %fusion.4), channel_id=1, source_target_pairs={{0,2},{1,3},{2,0},{3,1},{4,6},{5,7},{6,4},{7,5},{8,10},{9,11},{10,... | collective-permute-start | bytes 442376 | tf_op jit(solution)/shard_map/ppermute | solution.py:520
  228.1 7.7 %collective-permute-start.55 = (bf16[96,768]{1,0:T(8,128)(2,1)S(1)}, bf16[96,768]{1,0:T(8,128)(2,1)S(1)}, u32[]{:S(2)}, u32[]{:S(2)}) collective-permute-start(bf16[96,768]{1,0:T(8,128)(2,1)S(1)} %fusion.3), channel_id=1, source_target_pairs={{0,24},{4,28},{8,16},{12,20},{16,8},{20,12},{24,0},{28,4},{1,25},{... | collective-permute-start | bytes 442376 | tf_op jit(solution)/shard_map/ppermute | solution.py:520
  229.5 8.5 %collective-permute-start.56 = (bf16[96,768]{1,0:T(8,128)(2,1)S(1)}, bf16[96,768]{1,0:T(8,128)(2,1)S(1)}, u32[]{:S(2)}, u32[]{:S(2)}) collective-permute-start(bf16[96,768]{1,0:T(8,128)(2,1)S(1)} %fusion.3), channel_id=1, source_target_pairs={{0,16},{4,20},{8,24},{12,28},{16,0},{20,4},{24,8},{28,12},{1,17},{... | collective-permute-start | bytes 442376 | tf_op jit(solution)/shard_map/ppermute | solution.py:520
  230.0 8.2 %collective-permute-start.57 = (bf16[96,768]{1,0:T(8,128)(2,1)S(1)}, bf16[96,768]{1,0:T(8,128)(2,1)S(1)}, u32[]{:S(2)}, u32[]{:S(2)}) collective-permute-start(bf16[96,768]{1,0:T(8,128)(2,1)S(1)} %fusion.3), channel_id=1, source_target_pairs={{0,8},{4,12},{8,0},{12,4},{16,24},{20,28},{24,16},{28,20},{1,9},{5... | collective-permute-start | bytes 442376 | tf_op jit(solution)/shard_map/ppermute | solution.py:520
  (44 other events, 199.8 us)

commit v2 on v1

--- a/solution.py
+++ b/solution.py
@@ -536,6 +536,12 @@
 def share_of():
     me = lax.axis_index("dp")
     return (me & 1) * (lax.axis_size("dp") // 2) + (me >> 1)
+
+
+def flip_core(arrays):
+    form = (arrays[0].shape[0], -1, arrays[0].shape[-1])
+    got = flip(jnp.stack([a.reshape(form) for a in arrays]), "dp", 1)
+    return [got[i].reshape(a.shape) for i, a in enumerate(arrays)]
 
 
 class Gather:
@@ -744,7 +750,7 @@
         got = ffn.send(step)
         if step < ffn.steps - 1:
             got = tie(*got)
-    early = [flip(h, "dp", 1) for h in ffn.held]
+    early = flip_core(ffn.held)
     early, cot, x = tie(early, cot, join([tok[0], tok_one, tok_two, tok_three]))
     cot_blocks = [cot[0]] + [flip(cot[k], "mp", k) for k in range(1, mp)]
     later = lambda a: pl.BlockSpec((1,) + a.shape[1:], lambda s, h: (jnp.clip(s - 1, 0, mp - 2), 0, 0))
@@ -988,7 +994,7 @@
     sums = sums + sums_got
     att_sum = add_parts(att_even[0], att_got[0], att_last)
     ffn_halves = ffn.halves()
-    core_got = [flip(h, "dp", 1) for h in ffn_halves]
+    core_got = flip_core(ffn_halves)
     att_mine, att_order = gather_stack(att_sum)
     grad_in, grad_down = call(
         unit_grads_kernel,

time: 243 us -> 243 us (level)
    ppermute x61 -> x59, starting transfers between devices: 63.5 us -> 63 us  [flip(): return lax.ppermute(array, axis, [(i, i ^ mask) for i in range(size)])]
    ppermute x61 -> x59, waiting for transfers between devices: 91.4 us -> 91.3 us  [flip(): return lax.ppermute(array, axis, [(i, i ^ mask) for i in range(size)])]
  transfers between devices with their start and end apart: 61 -> 59, of which waited for: 32 -> 33; matrix products, arithmetic and copies ran while one was open for 4% -> 4% of each run, Pallas kernels for 19% -> 19%
where the time goes in v2:
time: 243 us; the launch traced here: 242 us
  waiting for transfers between devices  91.3 us (38%)
  Pallas kernels  70.3 us (29%)
  starting transfers between devices  63 us (26%)
  local copies, waits for them, and re-layouts  10.8 us (4%)
  other arithmetic  5.33 us (2%)
    ppermute x59, waiting for transfers between devices, flip(): return lax.ppermute(array, axis, [(i, i ^ mask) for i in range(size)])  91.3 us
    pallas_call x8, Pallas kernels, call(): pl.pallas_call(kernel, grid_spec=spec, out_shape=[pltpu.HBM(a.shape, a.dt...  66.7 us
    ppermute x59, starting transfers between devices, flip(): return lax.ppermute(array, axis, [(i, i ^ mask) for i in range(size)])  63 us
  transfers between devices with their start and end apart: 59, of which 33 were waited for; matrix products, arithmetic and copies ran while one was open for 4% of the time, Pallas kernels for 19%

profile of v2, /device:TPU:0, one launch (start us, length us, event | category | flops | bytes accessed | tf_op | source)
XLA Modules:
  0.0 242.5 jit_solution(17336964431374726035)
XLA Ops:
  1.8 3.1 %collective-permute-start = (bf16[96,768]{1,0:T(8,128)(2,1)S(1)}, bf16[96,768]{1,0:T(8,128)(2,1)S(1)}, u32[]{:S(2)}, u32[]{:S(2)}) collective-permute-start(bf16[96,768]{1,0:T(8,128)(2,1)S(1)} %pad_maximum_fusion.24), channel_id=1, source_target_pairs={{0,1},{1,0},{2,3},{3,2},{4,5},{5,4},{6,7},{7,6},{8,9},{9,8},{10,11... | collective-permute-start | bytes 442376 | tf_op jit(solution)/shard_map/ppermute | solution.py:520
  4.9 2.6 %collective-permute-start.1 = (bf16[96,768]{1,0:T(8,128)(2,1)S(1)}, bf16[96,768]{1,0:T(8,128)(2,1)}, u32[]{:S(2)}, u32[]{:S(2)}) collective-permute-start(bf16[96,768]{1,0:T(8,128)(2,1)S(1)} %pad_maximum_fusion.24), channel_id=1, source_target_pairs={{0,2},{1,3},{2,0},{3,1},{4,6},{5,7},{6,4},{7,5},{8,10},{9,11},{10,... | collective-permute-start | bytes 442376 | tf_op jit(solution)/shard_map/ppermute | solution.py:520
  14.2 4.8 %collective-permute-done.1 = bf16[96,768]{1,0:T(8,128)(2,1)} collective-permute-done((bf16[96,768]{1,0:T(8,128)(2,1)S(1)}, bf16[96,768]{1,0:T(8,128)(2,1)}, u32[]{:S(2)}, u32[]{:S(2)}) %collective-permute-start.1) | collective-permute-done | bytes 147488 | tf_op jit(solution)/shard_map/ppermute | solution.py:520
  20.1 1.6 collective-permute-start.5
  21.7 3.3 %collective-permute-start.3 = (bf16[200,768]{1,0:T(8,128)(2,1)S(1)}, bf16[200,768]{1,0:T(8,128)(2,1)S(1)}, u32[]{:S(2)}, u32[]{:S(2)}) collective-permute-start(bf16[200,768]{1,0:T(8,128)(2,1)S(1)} %concatenate.71), channel_id=1, source_target_pairs={{0,2},{1,3},{2,0},{3,1},{4,6},{5,7},{6,4},{7,5},{8,10},{9,11},{10,... | collective-permute-start | bytes 921608 | tf_op jit(solution)/shard_map/ppermute | solution.py:520
  25.0 1.6 collective-permute-start.4
  26.6 7.8 %collective-permute-done.6 = bf16[3,40,768]{2,1,0:T(8,128)(2,1)S(1)} collective-permute-done((bf16[3,40,768]{2,1,0:T(8,128)(2,1)}, bf16[3,40,768]{2,1,0:T(8,128)(2,1)S(1)}, u32[]{:S(2)}, u32[]{:S(2)}) %collective-permute-start.6) | collective-permute-done | bytes 184352 | tf_op jit(solution)/shard_map/ppermute | solution.py:520
  34.4 3.2 %collective-permute-done.3 = bf16[200,768]{1,0:T(8,128)(2,1)S(1)} collective-permute-done((bf16[200,768]{1,0:T(8,128)(2,1)S(1)}, bf16[200,768]{1,0:T(8,128)(2,1)S(1)}, u32[]{:S(2)}, u32[]{:S(2)}) %collective-permute-start.3) | collective-permute-done | bytes 307232 | tf_op jit(solution)/shard_map/ppermute | solution.py:520
  37.8 1.6 collective-permute-start.8
  41.4 14.2 %collective-permute-done.10 = bf16[3,40,768]{2,1,0:T(8,128)(2,1)S(1)} collective-permute-done((bf16[3,40,768]{2,1,0:T(8,128)(2,1)S(1)}, bf16[3,40,768]{2,1,0:T(8,128)(2,1)S(1)}, u32[]{:S(2)}, u32[]{:S(2)}) %collective-permute-start.10) | collective-permute-done | bytes 184352 | tf_op jit(solution)/shard_map/ppermute | solution.py:520
  58.3 1.6 collective-permute-start.11
  59.9 10.3 %collective-permute-done.15 = bf16[3,40,768]{2,1,0:T(8,128)(2,1)S(1)} collective-permute-done((bf16[3,40,768]{2,1,0:T(8,128)(2,1)S(1)}, bf16[3,40,768]{2,1,0:T(8,128)(2,1)S(1)}, u32[]{:S(2)}, u32[]{:S(2)}) %collective-permute-start.15) | collective-permute-done | bytes 184352 | tf_op jit(solution)/shard_map/ppermute | solution.py:520
  71.0 1.5 collective-permute-start.17
  72.5 1.5 collective-permute-start.16
  74.9 2.6 %collective-permute-start.20 = (bf16[3,40,768]{2,1,0:T(8,128)(2,1)S(1)}, bf16[3,40,768]{2,1,0:T(8,128)(2,1)S(1)}, u32[]{:S(2)}, u32[]{:S(2)}) collective-permute-start(bf16[3,40,768]{2,1,0:T(8,128)(2,1)S(1)} %get-tuple-element.231), channel_id=1, source_target_pairs={{0,2},{1,3},{2,0},{3,1},{4,6},{5,7},{6,4},{7,5},{8,10},{9,11},{10,... | collective-permute-start | bytes 552968 | tf_op jit(solution)/shard_map/ppermute | solution.py:520
  77.5 1.7 collective-permute-start.21
  79.2 11.9 %attention.1 = (bf16[4,480,192]{2,1,0:T(8,128)(2,1)}, bf16[4,480,192]{2,1,0:T(8,128)(2,1)}, bf16[4,480,192]{2,1,0:T(8,128)(2,1)}, f32[4,3,480,160]{3,2,1,0:T(8,1...) custom-call(s32[3]{0:T(128)S(1)} %pad_add_fusion.here_ref, ...), custom_call_target="tpu_custom_call" | custom-call | tf_op jit(solution)/shard_map/attention/pallas_call | solution.py:448
  91.2 1.9 collective-permute-done.17
  98.9 20.1 %ffn.1 = (bf16[3,40,768]{2,1,0:T(8,128)(2,1)}, bf16[3,40,768]{2,1,0:T(8,128)(2,1)}, bf16[3,40,768]{2,1,0:T(8,128)(2,1)}, bf16[3,40,768]{2,1,0:T(8,128)(2,1)}, f3...) custom-call(s32[3]{0:T(128)S(1)} %pad_add_fusion.here_ref, ...), custom_call_target="tpu_custom_call" | custom-call | tf_op jit(solution)/shard_map/ffn/pallas_call | solution.py:448
  119.5 7.2 %ffn_back.1 = (f32[480,768]{1,0:T(8,128)}, bf16[480,768]{1,0:T(8,128)(2,1)S(1)}, f32[8,768]{1,0:T(8,128)S(1)}) custom-call(s32[3]{0:T(128)S(1)} %pad_add_fusion.here_ref, bf16[4,480,768]{2,1,0:T(8,128)(2,1)} %get-tuple-element.253.pre_grad_hbm, bf16[768,768]{1,0:T(8,128)(2,1)} %w_in_hbm.3, bf16[3,384,768]{2,1,0:T(8,128)(2,1)S(1)} %bitcast.149, ...), custom_call_target="tpu_custom_call" | custom-call | tf_op jit(solution)/shard_map/ffn_back/pallas_call | solution.py:448
  129.0 1.5 collective-permute-start.27
  130.6 1.6 collective-permute-start.28
  133.2 1.7 collective-permute-start.30
  135.0 18.9 %attention_back.1 = (bf16[4,192,768]{2,1,0:T(8,128)(2,1)}, bf16[4,192,768]{2,1,0:T(8,128)(2,1)}, bf16[2,4,192,768]{3,2,1,0:T(8,128)(2,1)}, f32[16,768]{1,0:T(8,1...) custom-call(s32[3]{0:T(128)S(1)} %pad_add_fusion.here_ref, ...), custom_call_target="tpu_custom_call" | custom-call | tf_op jit(solution)/shard_map/attention_back/pallas_call | solution.py:448
  153.9 2.6 %collective-permute-done.26.refs_3_ = bf16[4,2,96,768]{3,2,1,0:T(8,128)(2,1)S(1)} collective-permute-done((bf16[4,2,96,768]{3,2,1,0:T(8,128)(2,1)S(1)}, bf16[4,2,96,768]{3,2,1,0:T(8,128)(2,1)S(1)}, u32[]{:S(2)}, u32[]{:S(2)}) %collective-permute-start.26) | collective-permute-done | bytes 1179680 | tf_op jit(solution)/shard_map/ppermute | solution.py:520
  157.2 1.6 collective-permute-start.31
  158.8 1.5 collective-permute-start.32
  160.3 2.1 collective-permute-start.34
  162.4 1.5 place.2
  166.4 6.5 %collective-permute-done.35 = f32[16,768]{1,0:T(8,128)S(1)} collective-permute-done((f32[16,768]{1,0:T(8,128)S(1)}, f32[16,768]{1,0:T(8,128)S(1)}, u32[]{:S(2)}, u32[]{:S(2)}) %collective-permute-start.35) | collective-permute-done | bytes 49184 | tf_op jit(solution)/shard_map/ppermute | solution.py:520
  175.0 1.6 collective-permute-start.38
  177.7 2.0 collective-permute-start.40
  180.3 11.8 %collective-permute-done.39 = f32[16,768]{1,0:T(8,128)S(1)} collective-permute-done((f32[16,768]{1,0:T(8,128)S(1)}, f32[16,768]{1,0:T(8,128)S(1)}, u32[]{:S(2)}, u32[]{:S(2)}) %collective-permute-start.39) | collective-permute-done | bytes 49184 | tf_op jit(solution)/shard_map/ppermute | solution.py:520
  193.8 2.5 %collective-permute-start.43 = (bf16[192,768]{1,0:T(8,128)(2,1)S(1)}, bf16[192,768]{1,0:T(8,128)(2,1)S(1)}, u32[]{:S(2)}, u32[]{:S(2)}) collective-permute-start(bf16[192,768]{1,0:T(8,128)(2,1)S(1)} %fusion.1), channel_id=1, source_target_pairs={{0,2},{1,3},{2,0},{3,1},{4,6},{5,7},{6,4},{7,5},{8,10},{9,11},{10,... | collective-permute-start | bytes 884744 | tf_op jit(solution)/shard_map/ppermute | solution.py:520
  198.9 1.4 collective-permute-start.45
  200.3 4.5 %collective-permute-done.45 = f32[16,768]{1,0:T(8,128)S(1)} collective-permute-done((f32[16,768]{1,0:T(8,128)S(1)}, f32[16,768]{1,0:T(8,128)S(1)}, u32[]{:S(2)}, u32[]{:S(2)}) %collective-permute-start.45) | collective-permute-done | bytes 49184 | tf_op jit(solution)/shard_map/ppermute | solution.py:520
  205.2 3.2 %collective-permute-done.43 = bf16[192,768]{1,0:T(8,128)(2,1)S(1)} collective-permute-done((bf16[192,768]{1,0:T(8,128)(2,1)S(1)}, bf16[192,768]{1,0:T(8,128)(2,1)S(1)}, u32[]{:S(2)}, u32[]{:S(2)}) %collective-permute-start.43) | collective-permute-done | bytes 294944 | tf_op jit(solution)/shard_map/ppermute | solution.py:520
  209.1 1.5 collective-permute-start.46
  213.0 1.4 collective-permute-done.46
  214.3 1.5 collective-permute-done.47
  216.4 2.5 %collective-permute-start.51 = (bf16[1,2,1,96,768]{4,3,2,1,0:T(8,128)(2,1)S(1)}, bf16[1,2,1,96,768]{4,3,2,1,0:T(8,128)(2,1)S(1)}, u32[]{:S(2)}, u32[]{:S(2)}) collective-permute-start(bf16[1,2,1,96,768]{4,3,2,1,0:T(8,128)(2,1)S(1)} %pad_maximum_fusion.23), channel_id=1, source_target_pairs={{0,8},{4,12},{8,0},{12,4},{16,24},{20,28},{24,16},{28,20},{1,9},{5... | collective-permute-start | bytes 884744 | tf_op jit(solution)/shard_map/ppermute | solution.py:520
  221.1 1.7 collective-permute-start.53
  222.9 1.7 place.3
  225.3 1.9 collective-permute-done.52
  229.5 1.7 collective-permute-start.56
  231.4 3.1 %unit_grads.1 = (f32[768,768]{1,0:T(8,128)}, f32[768,768]{1,0:T(8,128)}) custom-call(s32[3]{0:T(128)S(1)} %pad_add_fusion.here_ref, bf16[1,384,768]{2,1,0:T(8,128)(2,1)S(1)} %bitcast.173, bf16[1,384,768]{2,1,0:T(8,128)(2,1)S(1)} %bitcast.171, bf16[1,384,768]{2,1,0:T(8,128)(2,1)S(1)} %get-tuple-element.382.in_other, ...), custom_call_target="tpu_custom_call" | custom-call | tf_op jit(solution)/shard_map/unit_grads/pallas_call | solution.py:448
  235.4 2.7 %collective-permute-done.55 = bf16[96,768]{1,0:T(8,128)(2,1)S(1)} collective-permute-done((bf16[96,768]{1,0:T(8,128)(2,1)S(1)}, bf16[96,768]{1,0:T(8,128)(2,1)S(1)}, u32[]{:S(2)}, u32[]{:S(2)}) %collective-permute-start.55) | collective-permute-done | bytes 147488 | tf_op jit(solution)/shard_map/ppermute | solution.py:520
  240.3 2.2 head_grads.1
  (253 shorter events, 48.2 us)
Async XLA Ops:
  1.8 12.4 %collective-permute-start = (bf16[96,768]{1,0:T(8,128)(2,1)S(1)}, bf16[96,768]{1,0:T(8,128)(2,1)S(1)}, u32[]{:S(2)}, u32[]{:S(2)}) collective-permute-start(bf16[96,768]{1,0:T(8,128)(2,1)S(1)} %pad_maximum_fusion.24), channel_id=1, source_target_pairs={{0,1},{1,0},{2,3},{3,2},{4,5},{5,4},{6,7},{7,6},{8,9},{9,8},{10,11... | collective-permute-start | bytes 442376 | tf_op jit(solution)/shard_map/ppermute | solution.py:520
  4.9 14.1 %collective-permute-start.1 = (bf16[96,768]{1,0:T(8,128)(2,1)S(1)}, bf16[96,768]{1,0:T(8,128)(2,1)}, u32[]{:S(2)}, u32[]{:S(2)}) collective-permute-start(bf16[96,768]{1,0:T(8,128)(2,1)S(1)} %pad_maximum_fusion.24), channel_id=1, source_target_pairs={{0,2},{1,3},{2,0},{3,1},{4,6},{5,7},{6,4},{7,5},{8,10},{9,11},{10,... | collective-permute-start | bytes 442376 | tf_op jit(solution)/shard_map/ppermute | solution.py:520
  7.5 11.5 %collective-permute-start.2 = (bf16[96,768]{1,0:T(8,128)(2,1)S(1)}, bf16[96,768]{1,0:T(8,128)(2,1)}, u32[]{:S(2)}, u32[]{:S(2)}) collective-permute-start(bf16[96,768]{1,0:T(8,128)(2,1)S(1)} %pad_maximum_fusion.24), channel_id=1, source_target_pairs={{0,3},{1,2},{2,1},{3,0},{4,7},{5,6},{6,5},{7,4},{8,11},{9,10},{10,... | collective-permute-start | bytes 442376 | tf_op jit(solution)/shard_map/ppermute | solution.py:520
  20.1 14.3 %collective-permute-start.5 = (bf16[3,1,1,48,768]{4,3,0,2,1:T(8,128)(2,1)S(1)}, bf16[3,1,1,48,768]{4,3,0,2,1:T(8,128)(2,1)S(1)}, u32[]{:S(2)}, u32[]{:S(2)}) collective-permute-start(bf16[3,1,1,48,768]{4,3,0,2,1:T(8,128)(2,1)S(1)} %maximum_bitcast_fusion.3), channel_id=1, source_target_pairs={{0,16},{4,20},{8,24},{12,28},{16,0},{20,4},{24,8},{28,12},{1,17},{... | collective-permute-start | bytes 663560 | tf_op jit(solution)/shard_map/ppermute | solution.py:520
  21.7 15.9 %collective-permute-start.3 = (bf16[200,768]{1,0:T(8,128)(2,1)S(1)}, bf16[200,768]{1,0:T(8,128)(2,1)S(1)}, u32[]{:S(2)}, u32[]{:S(2)}) collective-permute-start(bf16[200,768]{1,0:T(8,128)(2,1)S(1)} %concatenate.71), channel_id=1, source_target_pairs={{0,2},{1,3},{2,0},{3,1},{4,6},{5,7},{6,4},{7,5},{8,10},{9,11},{10,... | collective-permute-start | bytes 921608 | tf_op jit(solution)/shard_map/ppermute | solution.py:520
  25.0 9.4 %collective-permute-start.4 = (bf16[3,1,1,48,768]{4,3,0,2,1:T(8,128)(2,1)S(1)}, bf16[3,1,1,48,768]{4,3,0,2,1:T(8,128)(2,1)S(1)}, u32[]{:S(2)}, u32[]{:S(2)}) collective-permute-start(bf16[3,1,1,48,768]{4,3,0,2,1:T(8,128)(2,1)S(1)} %maximum_bitcast_fusion.2), channel_id=1, source_target_pairs={{0,8},{4,12},{8,0},{12,4},{16,24},{20,28},{24,16},{28,20},{1,9},{5... | collective-permute-start | bytes 663560 | tf_op jit(solution)/shard_map/ppermute | solution.py:520
  26.6 7.8 %collective-permute-start.6 = (bf16[3,40,768]{2,1,0:T(8,128)(2,1)}, bf16[3,40,768]{2,1,0:T(8,128)(2,1)S(1)}, u32[]{:S(2)}, u32[]{:S(2)}) collective-permute-start(bf16[3,40,768]{2,1,0:T(8,128)(2,1)} %get-tuple-element.193), channel_id=1, source_target_pairs={{0,1},{1,0},{2,3},{3,2},{4,5},{5,4},{6,7},{7,6},{8,9},{9,8},{10,11... | collective-permute-start | bytes 552968 | tf_op jit(solution)/shard_map/ppermute | solution.py:520
  37.7 18.8 %collective-permute-start.9 = (bf16[2,200,768]{2,1,0:T(8,128)(2,1)S(1)}, bf16[2,200,768]{2,1,0:T(8,128)(2,1)S(1)}, u32[]{:S(2)}, u32[]{:S(2)}) collective-permute-start(bf16[2,200,768]{2,1,0:T(8,128)(2,1)S(1)} %pad_maximum_fusion.11), channel_id=1, source_target_pairs={{0,1},{1,0},{2,3},{3,2},{4,5},{5,4},{6,7},{7,6},{8,9},{9,8},{10,11... | collective-permute-start | bytes 1843208 | tf_op jit(solution)/shard_map/ppermute | solution.py:520
  37.8 17.7 %collective-permute-start.8 = (bf16[3,2,1,48,768]{4,3,0,2,1:T(8,128)(2,1)S(1)}, bf16[3,2,1,48,768]{4,3,0,2,1:T(8,128)(2,1)S(1)}, u32[]{:S(2)}, u32[]{:S(2)}) collective-permute-start(bf16[3,2,1,48,768]{4,3,0,2,1:T(8,128)(2,1)S(1)} %pad_maximum_fusion.18), channel_id=1, source_target_pairs={{0,8},{4,12},{8,0},{12,4},{16,24},{20,28},{24,16},{28,20},{1,9},{5... | collective-permute-start | bytes 1327112 | tf_op jit(solution)/shard_map/ppermute | solution.py:520
  39.5 16.1 %collective-permute-start.7 = (bf16[3,1,2,48,768]{4,3,0,2,1:T(8,128)(2,1)S(1)}, bf16[3,1,2,48,768]{4,3,0,2,1:T(8,128)(2,1)S(1)}, u32[]{:S(2)}, u32[]{:S(2)}) collective-permute-start(bf16[3,1,2,48,768]{4,3,0,2,1:T(8,128)(2,1)S(1)} %pad_maximum_fusion.17), channel_id=1, source_target_pairs={{0,16},{4,20},{8,24},{12,28},{16,0},{20,4},{24,8},{28,12},{1,17},{... | collective-permute-start | bytes 1327112 | tf_op jit(solution)/shard_map/ppermute | solution.py:520
  40.2 15.4 %collective-permute-start.10 = (bf16[3,40,768]{2,1,0:T(8,128)(2,1)S(1)}, bf16[3,40,768]{2,1,0:T(8,128)(2,1)S(1)}, u32[]{:S(2)}, u32[]{:S(2)}) collective-permute-start(bf16[3,40,768]{2,1,0:T(8,128)(2,1)S(1)} %copy-done.16), channel_id=1, source_target_pairs={{0,3},{1,2},{2,1},{3,0},{4,7},{5,6},{6,5},{7,4},{8,11},{9,10},{10,... | collective-permute-start | bytes 552968 | tf_op jit(solution)/shard_map/ppermute | solution.py:520
  56.7 13.5 %collective-permute-start.14 = (bf16[3,192,768]{2,1,0:T(8,128)(2,1)S(1)}, bf16[3,192,768]{2,1,0:T(8,128)(2,1)S(1)}, u32[]{:S(2)}, u32[]{:S(2)}) collective-permute-start(bf16[3,192,768]{2,1,0:T(8,128)(2,1)S(1)} %bitcast.158), channel_id=1, source_target_pairs={{0,4},{4,0},{8,12},{12,8},{16,20},{20,16},{24,28},{28,24},{1,5},{5... | collective-permute-start | bytes 2654216 | tf_op jit(solution)/shard_map/ppermute | solution.py:520
  57.1 13.2 %collective-permute-start.13 = (bf16[3,192,768]{2,1,0:T(8,128)(2,1)S(1)}, bf16[3,192,768]{2,1,0:T(8,128)(2,1)S(1)}, u32[]{:S(2)}, u32[]{:S(2)}) collective-permute-start(bf16[3,192,768]{2,1,0:T(8,128)(2,1)S(1)} %bitcast.161), channel_id=1, source_target_pairs={{0,4},{4,0},{8,12},{12,8},{16,20},{20,16},{24,28},{28,24},{1,5},{5... | collective-permute-start | bytes 2654216 | tf_op jit(solution)/shard_map/ppermute | solution.py:520
  57.7 12.5 %collective-permute-start.12 = (bf16[3,1,1,96,768]{4,3,0,2,1:T(8,128)(2,1)S(1)}, bf16[3,1,1,96,768]{4,3,0,2,1:T(8,128)(2,1)S(1)}, u32[]{:S(2)}, u32[]{:S(2)}) collective-permute-start(bf16[3,1,1,96,768]{4,3,0,2,1:T(8,128)(2,1)S(1)} %maximum_bitcast_fusion.1), channel_id=1, source_target_pairs={{0,16},{4,20},{8,24},{12,28},{16,0},{20,4},{24,8},{28,12},{1,17},{... | collective-permute-start | bytes 1327112 | tf_op jit(solution)/shard_map/ppermute | solution.py:520
  58.3 11.9 %collective-permute-start.11 = (bf16[3,1,1,96,768]{4,3,0,2,1:T(8,128)(2,1)S(1)}, bf16[3,1,1,96,768]{4,3,0,2,1:T(8,128)(2,1)S(1)}, u32[]{:S(2)}, u32[]{:S(2)}) collective-permute-start(bf16[3,1,1,96,768]{4,3,0,2,1:T(8,128)(2,1)S(1)} %maximum_bitcast_fusion), channel_id=1, source_target_pairs={{0,8},{4,12},{8,0},{12,4},{16,24},{20,28},{24,16},{28,20},{1,9},{5... | collective-permute-start | bytes 1327112 | tf_op jit(solution)/shard_map/ppermute | solution.py:520
  59.9 10.3 %collective-permute-start.15 = (bf16[3,40,768]{2,1,0:T(8,128)(2,1)S(1)}, bf16[3,40,768]{2,1,0:T(8,128)(2,1)S(1)}, u32[]{:S(2)}, u32[]{:S(2)}) collective-permute-start(bf16[3,40,768]{2,1,0:T(8,128)(2,1)S(1)} %copy-done.15), channel_id=1, source_target_pairs={{0,2},{1,3},{2,0},{3,1},{4,6},{5,7},{6,4},{7,5},{8,10},{9,11},{10,... | collective-permute-start | bytes 552968 | tf_op jit(solution)/shard_map/ppermute | solution.py:520
  71.0 22.1 %collective-permute-start.17 = (bf16[3,2,1,96,768]{4,3,0,2,1:T(8,128)(2,1)S(1)}, bf16[3,2,1,96,768]{4,3,0,2,1:T(8,128)(2,1)S(1)}, u32[]{:S(2)}, u32[]{:S(2)}) collective-permute-start(bf16[3,2,1,96,768]{4,3,0,2,1:T(8,128)(2,1)S(1)} %pad_maximum_fusion.9), channel_id=1, source_target_pairs={{0,8},{4,12},{8,0},{12,4},{16,24},{20,28},{24,16},{28,20},{1,9},{5... | collective-permute-start | bytes 2654216 | tf_op jit(solution)/shard_map/ppermute | solution.py:520
  72.5 21.7 %collective-permute-start.16 = (bf16[3,1,2,96,768]{4,3,0,2,1:T(8,128)(2,1)S(1)}, bf16[3,1,2,96,768]{4,3,0,2,1:T(8,128)(2,1)S(1)}, u32[]{:S(2)}, u32[]{:S(2)}) collective-permute-start(bf16[3,1,2,96,768]{4,3,0,2,1:T(8,128)(2,1)S(1)} %pad_maximum_fusion.8), channel_id=1, source_target_pairs={{0,16},{4,20},{8,24},{12,28},{16,0},{20,4},{24,8},{28,12},{1,17},{... | collective-permute-start | bytes 2654216 | tf_op jit(solution)/shard_map/ppermute | solution.py:520
  74.8 19.5 %collective-permute-start.19 = (bf16[3,40,768]{2,1,0:T(8,128)(2,1)S(1)}, bf16[3,40,768]{2,1,0:T(8,128)(2,1)S(1)}, u32[]{:S(2)}, u32[]{:S(2)}) collective-permute-start(bf16[3,40,768]{2,1,0:T(8,128)(2,1)S(1)} %get-tuple-element.230), channel_id=1, source_target_pairs={{0,1},{1,0},{2,3},{3,2},{4,5},{5,4},{6,7},{7,6},{8,9},{9,8},{10,11... | collective-permute-start | bytes 552968 | tf_op jit(solution)/shard_map/ppermute | solution.py:520
  74.9 19.4 %collective-permute-start.20 = (bf16[3,40,768]{2,1,0:T(8,128)(2,1)S(1)}, bf16[3,40,768]{2,1,0:T(8,128)(2,1)S(1)}, u32[]{:S(2)}, u32[]{:S(2)}) collective-permute-start(bf16[3,40,768]{2,1,0:T(8,128)(2,1)S(1)} %get-tuple-element.231), channel_id=1, source_target_pairs={{0,2},{1,3},{2,0},{3,1},{4,6},{5,7},{6,4},{7,5},{8,10},{9,11},{10,... | collective-permute-start | bytes 552968 | tf_op jit(solution)/shard_map/ppermute | solution.py:520
  77.5 16.8 %collective-permute-start.21 = (bf16[3,40,768]{2,1,0:T(8,128)(2,1)S(1)}, bf16[3,40,768]{2,1,0:T(8,128)(2,1)S(1)}, u32[]{:S(2)}, u32[]{:S(2)}) collective-permute-start(bf16[3,40,768]{2,1,0:T(8,128)(2,1)S(1)} %get-tuple-element.232), channel_id=1, source_target_pairs={{0,3},{1,2},{2,1},{3,0},{4,7},{5,6},{6,5},{7,4},{8,11},{9,10},{10,... | collective-permute-start | bytes 552968 | tf_op jit(solution)/shard_map/ppermute | solution.py:520
  119.0 7.8 %collective-permute-start.24 = (bf16[4,384,768]{2,1,0:T(8,128)(2,1)}, bf16[4,384,768]{2,1,0:T(8,128)(2,1)S(1)}, u32[]{:S(2)}, u32[]{:S(2)}) collective-permute-start(bf16[4,384,768]{2,1,0:T(8,128)(2,1)} %get-tuple-element.247), channel_id=1, source_target_pairs={{0,4},{4,0},{8,12},{12,8},{16,20},{20,16},{24,28},{28,24},{1,5},{5... | collective-permute-start | bytes 7077896 | tf_op jit(solution)/shard_map/ppermute | solution.py:520
  119.2 8.0 %collective-permute-start.25 = (bf16[4,384,768]{2,1,0:T(8,128)(2,1)}, bf16[4,384,768]{2,1,0:T(8,128)(2,1)S(1)}, u32[]{:S(2)}, u32[]{:S(2)}) collective-permute-start(bf16[4,384,768]{2,1,0:T(8,128)(2,1)} %get-tuple-element.248), channel_id=1, source_target_pairs={{0,4},{4,0},{8,12},{12,8},{16,20},{20,16},{24,28},{28,24},{1,5},{5... | collective-permute-start | bytes 7077896 | tf_op jit(solution)/shard_map/ppermute | solution.py:520
  128.4 28.1 %collective-permute-start.26 = (bf16[4,2,96,768]{3,2,1,0:T(8,128)(2,1)S(1)}, bf16[4,2,96,768]{3,2,1,0:T(8,128)(2,1)S(1)}, u32[]{:S(2)}, u32[]{:S(2)}) collective-permute-start(bf16[4,2,96,768]{3,2,1,0:T(8,128)(2,1)S(1)} %get-tuple-element.267), channel_id=1, source_target_pairs={{0,8},{4,12},{8,0},{12,4},{16,24},{20,28},{24,16},{28,20},{1,9},{5... | collective-permute-start | bytes 3538952 | tf_op jit(solution)/shard_map/ppermute | solution.py:520
  129.0 27.7 %collective-permute-start.27 = (bf16[4,2,96,768]{3,2,1,0:T(8,128)(2,1)S(1)}, bf16[4,2,96,768]{3,2,1,0:T(8,128)(2,1)S(1)}, u32[]{:S(2)}, u32[]{:S(2)}) collective-permute-start(bf16[4,2,96,768]{3,2,1,0:T(8,128)(2,1)S(1)} %get-tuple-element.268), channel_id=1, source_target_pairs={{0,16},{4,20},{8,24},{12,28},{16,0},{20,4},{24,8},{28,12},{1,17},{... | collective-permute-start | bytes 3538952 | tf_op jit(solution)/shard_map/ppermute | solution.py:520
  130.6 23.3 %collective-permute-start.28 = (bf16[3,40,768]{2,1,0:T(8,128)(2,1)S(1)}, bf16[3,40,768]{2,1,0:T(8,128)(2,1)S(1)}, u32[]{:S(2)}, u32[]{:S(2)}) collective-permute-start(bf16[3,40,768]{2,1,0:T(8,128)(2,1)S(1)} %copy-done.29), channel_id=1, source_target_pairs={{0,1},{1,0},{2,3},{3,2},{4,5},{5,4},{6,7},{7,6},{8,9},{9,8},{10,11... | collective-permute-start | bytes 552968 | tf_op jit(solution)/shard_map/ppermute | solution.py:520
  132.1 21.8 %collective-permute-start.29 = (bf16[3,40,768]{2,1,0:T(8,128)(2,1)S(1)}, bf16[3,40,768]{2,1,0:T(8,128)(2,1)S(1)}, u32[]{:S(2)}, u32[]{:S(2)}) collective-permute-start(bf16[3,40,768]{2,1,0:T(8,128)(2,1)S(1)} %copy-done.28), channel_id=1, source_target_pairs={{0,2},{1,3},{2,0},{3,1},{4,6},{5,7},{6,4},{7,5},{8,10},{9,11},{10,... | collective-permute-start | bytes 552968 | tf_op jit(solution)/shard_map/ppermute | solution.py:520
  133.2 20.7 %collective-permute-start.30 = (bf16[3,40,768]{2,1,0:T(8,128)(2,1)S(1)}, bf16[3,40,768]{2,1,0:T(8,128)(2,1)S(1)}, u32[]{:S(2)}, u32[]{:S(2)}) collective-permute-start(bf16[3,40,768]{2,1,0:T(8,128)(2,1)S(1)} %copy-done.27), channel_id=1, source_target_pairs={{0,3},{1,2},{2,1},{3,0},{4,7},{5,6},{6,5},{7,4},{8,11},{9,10},{10,... | collective-permute-start | bytes 552968 | tf_op jit(solution)/shard_map/ppermute | solution.py:520
  157.2 15.8 %collective-permute-start.31 = (bf16[4,1,96,768]{3,2,1,0:T(8,128)(2,1)S(1)}, bf16[4,1,96,768]{3,2,1,0:T(8,128)(2,1)S(1)}, u32[]{:S(2)}, u32[]{:S(2)}) collective-permute-start(bf16[4,1,96,768]{3,2,1,0:T(8,128)(2,1)S(1)} %get-tuple-element.291), channel_id=1, source_target_pairs={{0,16},{4,20},{8,24},{12,28},{16,0},{20,4},{24,8},{28,12},{1,17},{... | collective-permute-start | bytes 1769480 | tf_op jit(solution)/shard_map/ppermute | solution.py:520
  158.8 15.5 %collective-permute-start.32 = (bf16[4,1,96,768]{3,2,1,0:T(8,128)(2,1)S(1)}, bf16[4,1,96,768]{3,2,1,0:T(8,128)(2,1)S(1)}, u32[]{:S(2)}, u32[]{:S(2)}) collective-permute-start(bf16[4,1,96,768]{3,2,1,0:T(8,128)(2,1)S(1)} %get-tuple-element.292), channel_id=1, source_target_pairs={{0,8},{4,12},{8,0},{12,4},{16,24},{20,28},{24,16},{28,20},{1,9},{5... | collective-permute-start | bytes 1769480 | tf_op jit(solution)/shard_map/ppermute | solution.py:520
  160.3 12.6 %collective-permute-start.34 = (bf16[3,40,768]{2,1,0:T(8,128)(2,1)S(1)}, bf16[3,40,768]{2,1,0:T(8,128)(2,1)S(1)}, u32[]{:S(2)}, u32[]{:S(2)}) collective-permute-start(bf16[3,40,768]{2,1,0:T(8,128)(2,1)S(1)} %copy-done.30), channel_id=1, source_target_pairs={{0,3},{1,2},{2,1},{3,0},{4,7},{5,6},{6,5},{7,4},{8,11},{9,10},{10,... | collective-permute-start | bytes 552968 | tf_op jit(solution)/shard_map/ppermute | solution.py:520
  162.4 10.5 %collective-permute-start.35 = (f32[16,768]{1,0:T(8,128)S(1)}, f32[16,768]{1,0:T(8,128)S(1)}, u32[]{:S(2)}, u32[]{:S(2)}) collective-permute-start(f32[16,768]{1,0:T(8,128)S(1)} %get-tuple-element.299), channel_id=1, source_target_pairs={{0,2},{1,3},{2,0},{3,1},{4,6},{5,7},{6,4},{7,5},{8,10},{9,11},{10,... | collective-permute-start | bytes 147464 | tf_op jit(solution)/shard_map/ppermute | solution.py:520
  175.0 18.7 %collective-permute-start.38 = (bf16[2,192,768]{2,1,0:T(8,128)(2,1)S(1)}, bf16[2,192,768]{2,1,0:T(8,128)(2,1)S(1)}, u32[]{:S(2)}, u32[]{:S(2)}) collective-permute-start(bf16[2,192,768]{2,1,0:T(8,128)(2,1)S(1)} %pad_maximum_fusion.13), channel_id=1, source_target_pairs={{0,1},{1,0},{2,3},{3,2},{4,5},{5,4},{6,7},{7,6},{8,9},{9,8},{10,11... | collective-permute-start | bytes 1769480 | tf_op jit(solution)/shard_map/ppermute | solution.py:520
  176.7 17.0 %collective-permute-start.36 = (bf16[4,2,48,768]{3,2,1,0:T(8,128)(2,1)S(1)}, bf16[4,2,48,768]{3,2,1,0:T(8,128)(2,1)S(1)}, u32[]{:S(2)}, u32[]{:S(2)}) collective-permute-start(bf16[4,2,48,768]{3,2,1,0:T(8,128)(2,1)S(1)} %get-tuple-element.312), channel_id=1, source_target_pairs={{0,8},{4,12},{8,0},{12,4},{16,24},{20,28},{24,16},{28,20},{1,9},{5... | collective-permute-start | bytes 1769480 | tf_op jit(solution)/shard_map/ppermute | solution.py:520
  177.2 16.5 %collective-permute-start.37 = (bf16[4,2,48,768]{3,2,1,0:T(8,128)(2,1)S(1)}, bf16[4,2,48,768]{3,2,1,0:T(8,128)(2,1)S(1)}, u32[]{:S(2)}, u32[]{:S(2)}) collective-permute-start(bf16[4,2,48,768]{3,2,1,0:T(8,128)(2,1)S(1)} %get-tuple-element.313), channel_id=1, source_target_pairs={{0,16},{4,20},{8,24},{12,28},{16,0},{20,4},{24,8},{28,12},{1,17},{... | collective-permute-start | bytes 1769480 | tf_op jit(solution)/shard_map/ppermute | solution.py:520
  177.7 15.0 %collective-permute-start.40 = (bf16[3,40,768]{2,1,0:T(8,128)(2,1)S(1)}, bf16[3,40,768]{2,1,0:T(8,128)(2,1)S(1)}, u32[]{:S(2)}, u32[]{:S(2)}) collective-permute-start(bf16[3,40,768]{2,1,0:T(8,128)(2,1)S(1)} %copy-done.26), channel_id=1, source_target_pairs={{0,2},{1,3},{2,0},{3,1},{4,6},{5,7},{6,4},{7,5},{8,10},{9,11},{10,... | collective-permute-start | bytes 552968 | tf_op jit(solution)/shard_map/ppermute | solution.py:520
  179.8 12.3 %collective-permute-start.39 = (f32[16,768]{1,0:T(8,128)S(1)}, f32[16,768]{1,0:T(8,128)S(1)}, u32[]{:S(2)}, u32[]{:S(2)}) collective-permute-start(f32[16,768]{1,0:T(8,128)S(1)} %add.145), channel_id=1, source_target_pairs={{0,8},{4,12},{8,0},{12,4},{16,24},{20,28},{24,16},{28,20},{1,9},{5... | collective-permute-start | bytes 147464 | tf_op jit(solution)/shard_map/ppermute | solution.py:520
  193.8 14.7 %collective-permute-start.43 = (bf16[192,768]{1,0:T(8,128)(2,1)S(1)}, bf16[192,768]{1,0:T(8,128)(2,1)S(1)}, u32[]{:S(2)}, u32[]{:S(2)}) collective-permute-start(bf16[192,768]{1,0:T(8,128)(2,1)S(1)} %fusion.1), channel_id=1, source_target_pairs={{0,2},{1,3},{2,0},{3,1},{4,6},{5,7},{6,4},{7,5},{8,10},{9,11},{10,... | collective-permute-start | bytes 884744 | tf_op jit(solution)/shard_map/ppermute | solution.py:520
  196.5 11.9 %collective-permute-start.41 = (bf16[4,1,48,768]{3,2,1,0:T(8,128)(2,1)S(1)}, bf16[4,1,48,768]{3,2,1,0:T(8,128)(2,1)S(1)}, u32[]{:S(2)}, u32[]{:S(2)}) collective-permute-start(bf16[4,1,48,768]{3,2,1,0:T(8,128)(2,1)S(1)} %get-tuple-element.321), channel_id=1, source_target_pairs={{0,16},{4,20},{8,24},{12,28},{16,0},{20,4},{24,8},{28,12},{1,17},{... | collective-permute-start | bytes 884744 | tf_op jit(solution)/shard_map/ppermute | solution.py:520
  197.2 11.3 %collective-permute-start.42 = (bf16[4,1,48,768]{3,2,1,0:T(8,128)(2,1)S(1)}, bf16[4,1,48,768]{3,2,1,0:T(8,128)(2,1)S(1)}, u32[]{:S(2)}, u32[]{:S(2)}) collective-permute-start(bf16[4,1,48,768]{3,2,1,0:T(8,128)(2,1)S(1)} %get-tuple-element.322), channel_id=1, source_target_pairs={{0,8},{4,12},{8,0},{12,4},{16,24},{20,28},{24,16},{28,20},{1,9},{5... | collective-permute-start | bytes 884744 | tf_op jit(solution)/shard_map/ppermute | solution.py:520
  197.8 7.5 %collective-permute-start.44 = (bf16[3,40,768]{2,1,0:T(8,128)(2,1)S(1)}, bf16[3,40,768]{2,1,0:T(8,128)(2,1)S(1)}, u32[]{:S(2)}, u32[]{:S(2)}) collective-permute-start(bf16[3,40,768]{2,1,0:T(8,128)(2,1)S(1)} %copy-done.25), channel_id=1, source_target_pairs={{0,1},{1,0},{2,3},{3,2},{4,5},{5,4},{6,7},{7,6},{8,9},{9,8},{10,11... | collective-permute-start | bytes 552968 | tf_op jit(solution)/shard_map/ppermute | solution.py:520
  209.1 7.3 %collective-permute-start.48 = (bf16[2,96,768]{2,1,0:T(8,128)(2,1)S(1)}, bf16[2,96,768]{2,1,0:T(8,128)(2,1)S(1)}, u32[]{:S(2)}, u32[]{:S(2)}) collective-permute-start(bf16[2,96,768]{2,1,0:T(8,128)(2,1)S(1)} %pad_maximum_fusion.20), channel_id=1, source_target_pairs={{0,1},{1,0},{2,3},{3,2},{4,5},{5,4},{6,7},{7,6},{8,9},{9,8},{10,11... | collective-permute-start | bytes 884744 | tf_op jit(solution)/shard_map/ppermute | solution.py:520
  216.4 10.8 %collective-permute-start.51 = (bf16[1,2,1,96,768]{4,3,2,1,0:T(8,128)(2,1)S(1)}, bf16[1,2,1,96,768]{4,3,2,1,0:T(8,128)(2,1)S(1)}, u32[]{:S(2)}, u32[]{:S(2)}) collective-permute-start(bf16[1,2,1,96,768]{4,3,2,1,0:T(8,128)(2,1)S(1)} %pad_maximum_fusion.23), channel_id=1, source_target_pairs={{0,8},{4,12},{8,0},{12,4},{16,24},{20,28},{24,16},{28,20},{1,9},{5... | collective-permute-start | bytes 884744 | tf_op jit(solution)/shard_map/ppermute | solution.py:520
  219.0 8.3 %collective-permute-start.50 = (bf16[1,1,2,96,768]{4,3,2,1,0:T(8,128)(2,1)S(1)}, bf16[1,1,2,96,768]{4,3,2,1,0:T(8,128)(2,1)S(1)}, u32[]{:S(2)}, u32[]{:S(2)}) collective-permute-start(bf16[1,1,2,96,768]{4,3,2,1,0:T(8,128)(2,1)S(1)} %pad_maximum_fusion.22), channel_id=1, source_target_pairs={{0,16},{4,20},{8,24},{12,28},{16,0},{20,4},{24,8},{28,12},{1,17},{... | collective-permute-start | bytes 884744 | tf_op jit(solution)/shard_map/ppermute | solution.py:520
  219.8 7.4 %collective-permute-start.52 = (bf16[96,768]{1,0:T(8,128)(2,1)S(1)}, bf16[96,768]{1,0:T(8,128)(2,1)S(1)}, u32[]{:S(2)}, u32[]{:S(2)}) collective-permute-start(bf16[96,768]{1,0:T(8,128)(2,1)S(1)} %fusion.4), channel_id=1, source_target_pairs={{0,2},{1,3},{2,0},{3,1},{4,6},{5,7},{6,4},{7,5},{8,10},{9,11},{10,... | collective-permute-start | bytes 442376 | tf_op jit(solution)/shard_map/ppermute | solution.py:520
  227.7 7.7 %collective-permute-start.54 = (bf16[96,768]{1,0:T(8,128)(2,1)S(1)}, bf16[96,768]{1,0:T(8,128)(2,1)S(1)}, u32[]{:S(2)}, u32[]{:S(2)}) collective-permute-start(bf16[96,768]{1,0:T(8,128)(2,1)S(1)} %fusion.3), channel_id=1, source_target_pairs={{0,24},{4,28},{8,16},{12,20},{16,8},{20,12},{24,0},{28,4},{1,25},{... | collective-permute-start | bytes 442376 | tf_op jit(solution)/shard_map/ppermute | solution.py:520
  229.0 9.1 %collective-permute-start.55 = (bf16[96,768]{1,0:T(8,128)(2,1)S(1)}, bf16[96,768]{1,0:T(8,128)(2,1)S(1)}, u32[]{:S(2)}, u32[]{:S(2)}) collective-permute-start(bf16[96,768]{1,0:T(8,128)(2,1)S(1)} %fusion.3), channel_id=1, source_target_pairs={{0,16},{4,20},{8,24},{12,28},{16,0},{20,4},{24,8},{28,12},{1,17},{... | collective-permute-start | bytes 442376 | tf_op jit(solution)/shard_map/ppermute | solution.py:520
  229.5 8.6 %collective-permute-start.56 = (bf16[96,768]{1,0:T(8,128)(2,1)S(1)}, bf16[96,768]{1,0:T(8,128)(2,1)S(1)}, u32[]{:S(2)}, u32[]{:S(2)}) collective-permute-start(bf16[96,768]{1,0:T(8,128)(2,1)S(1)} %fusion.3), channel_id=1, source_target_pairs={{0,8},{4,12},{8,0},{12,4},{16,24},{20,28},{24,16},{28,20},{1,9},{5... | collective-permute-start | bytes 442376 | tf_op jit(solution)/shard_map/ppermute | solution.py:520
  (42 other events, 193.0 us)

commit v3 on v2

--- a/solution.py
+++ b/solution.py
@@ -938,12 +938,13 @@
         if step == 1:
             att_got = flip(att_send, "dp", 1)
             row_three = flip(row_sends[3], "mp", 3)
+            row_one = flip(row_sends[1], "mp", 1)
             sums_got = flip(sums, "mp", 2)
             att = Reduce([qk_keep, vo_keep], [att_got[0], att_got[1]])
             att_packs = att.pack(0)
             layer_out = place(out_got, BF16)
-        got, att_packs, row_three, sums_got, row_sends, layer_out = tie(
-            got, att_packs, row_three, sums_got, row_sends, layer_out
+        got, att_packs, row_one, row_three, sums_got, row_sends, layer_out = tie(
+            got, att_packs, row_one, row_three, sums_got, row_sends, layer_out
         )
     sums = sums + sums_got
     ffn.take(got)
@@ -965,9 +966,8 @@
         got = att.send(step, packs)
         if step == 1:
             ffn_last = flip(ffn_two, "mp", 2)
-            row_one = flip(row_sends[1], "mp", 1)
             sums_got = flip(sums, "dp", dp // 2)
-        got, ffn_last, row_one, sums_got, row_sends = tie(got, ffn_last, row_one, sums_got, row_sends)
+        got, ffn_last, sums_got, row_sends = tie(got, ffn_last, sums_got, row_sends)
     att.take(got)
     sums = sums + sums_got
     att_parts = att.finish()

time: 243 us -> 243 us (level)
  transfers between devices with their start and end apart: 59 -> 59, of which waited for: 33 -> 30; matrix products, arithmetic and copies ran while one was open for 4% -> 4% of each run, Pallas kernels for 19% -> 19%
where the time goes in v3:
time: 243 us; the launch traced here: 242 us
  waiting for transfers between devices  92.1 us (38%)
  Pallas kernels  70.4 us (29%)
  starting transfers between devices  62.8 us (26%)
  local copies, waits for them, and re-layouts  10.1 us (4%)
  other arithmetic  5.33 us (2%)
    ppermute x59, waiting for transfers between devices, flip(): return lax.ppermute(array, axis, [(i, i ^ mask) for i in range(size)])  92.1 us
    pallas_call x8, Pallas kernels, call(): pl.pallas_call(kernel, grid_spec=spec, out_shape=[pltpu.HBM(a.shape, a.dt...  66.7 us
    ppermute x59, starting transfers between devices, flip(): return lax.ppermute(array, axis, [(i, i ^ mask) for i in range(size)])  62.8 us
  transfers between devices with their start and end apart: 59, of which 30 were waited for; matrix products, arithmetic and copies ran while one was open for 4% of the time, Pallas kernels for 19%

profile of v3, /device:TPU:0, one launch (start us, length us, event | category | flops | bytes accessed | tf_op | source)
XLA Modules:
  0.0 242.5 jit_solution(7420902251863138192)
XLA Ops:
  1.8 3.1 %collective-permute-start = (bf16[96,768]{1,0:T(8,128)(2,1)S(1)}, bf16[96,768]{1,0:T(8,128)(2,1)S(1)}, u32[]{:S(2)}, u32[]{:S(2)}) collective-permute-start(bf16[96,768]{1,0:T(8,128)(2,1)S(1)} %pad_maximum_fusion.24), channel_id=1, source_target_pairs={{0,1},{1,0},{2,3},{3,2},{4,5},{5,4},{6,7},{7,6},{8,9},{9,8},{10,11... | collective-permute-start | bytes 442376 | tf_op jit(solution)/shard_map/ppermute | solution.py:520
  4.9 2.6 %collective-permute-start.1 = (bf16[96,768]{1,0:T(8,128)(2,1)S(1)}, bf16[96,768]{1,0:T(8,128)(2,1)}, u32[]{:S(2)}, u32[]{:S(2)}) collective-permute-start(bf16[96,768]{1,0:T(8,128)(2,1)S(1)} %pad_maximum_fusion.24), channel_id=1, source_target_pairs={{0,2},{1,3},{2,0},{3,1},{4,6},{5,7},{6,4},{7,5},{8,10},{9,11},{10,... | collective-permute-start | bytes 442376 | tf_op jit(solution)/shard_map/ppermute | solution.py:520
  14.2 4.8 %collective-permute-done.1 = bf16[96,768]{1,0:T(8,128)(2,1)} collective-permute-done((bf16[96,768]{1,0:T(8,128)(2,1)S(1)}, bf16[96,768]{1,0:T(8,128)(2,1)}, u32[]{:S(2)}, u32[]{:S(2)}) %collective-permute-start.1) | collective-permute-done | bytes 147488 | tf_op jit(solution)/shard_map/ppermute | solution.py:520
  20.1 1.6 collective-permute-start.5
  21.7 3.3 %collective-permute-start.3 = (bf16[200,768]{1,0:T(8,128)(2,1)S(1)}, bf16[200,768]{1,0:T(8,128)(2,1)S(1)}, u32[]{:S(2)}, u32[]{:S(2)}) collective-permute-start(bf16[200,768]{1,0:T(8,128)(2,1)S(1)} %concatenate.71), channel_id=1, source_target_pairs={{0,2},{1,3},{2,0},{3,1},{4,6},{5,7},{6,4},{7,5},{8,10},{9,11},{10,... | collective-permute-start | bytes 921608 | tf_op jit(solution)/shard_map/ppermute | solution.py:520
  25.0 1.6 collective-permute-start.4
  26.6 7.8 %collective-permute-done.6 = bf16[3,40,768]{2,1,0:T(8,128)(2,1)S(1)} collective-permute-done((bf16[3,40,768]{2,1,0:T(8,128)(2,1)}, bf16[3,40,768]{2,1,0:T(8,128)(2,1)S(1)}, u32[]{:S(2)}, u32[]{:S(2)}) %collective-permute-start.6) | collective-permute-done | bytes 184352 | tf_op jit(solution)/shard_map/ppermute | solution.py:520
  34.4 3.2 %collective-permute-done.3 = bf16[200,768]{1,0:T(8,128)(2,1)S(1)} collective-permute-done((bf16[200,768]{1,0:T(8,128)(2,1)S(1)}, bf16[200,768]{1,0:T(8,128)(2,1)S(1)}, u32[]{:S(2)}, u32[]{:S(2)}) %collective-permute-start.3) | collective-permute-done | bytes 307232 | tf_op jit(solution)/shard_map/ppermute | solution.py:520
  37.8 1.6 collective-permute-start.8
  41.4 14.2 %collective-permute-done.10 = bf16[3,40,768]{2,1,0:T(8,128)(2,1)S(1)} collective-permute-done((bf16[3,40,768]{2,1,0:T(8,128)(2,1)S(1)}, bf16[3,40,768]{2,1,0:T(8,128)(2,1)S(1)}, u32[]{:S(2)}, u32[]{:S(2)}) %collective-permute-start.10) | collective-permute-done | bytes 184352 | tf_op jit(solution)/shard_map/ppermute | solution.py:520
  58.3 1.6 collective-permute-start.11
  59.9 10.3 %collective-permute-done.15 = bf16[3,40,768]{2,1,0:T(8,128)(2,1)S(1)} collective-permute-done((bf16[3,40,768]{2,1,0:T(8,128)(2,1)S(1)}, bf16[3,40,768]{2,1,0:T(8,128)(2,1)S(1)}, u32[]{:S(2)}, u32[]{:S(2)}) %collective-permute-start.15) | collective-permute-done | bytes 184352 | tf_op jit(solution)/shard_map/ppermute | solution.py:520
  71.0 1.5 collective-permute-start.17
  72.5 1.5 collective-permute-start.16
  74.9 2.6 %collective-permute-start.20 = (bf16[3,40,768]{2,1,0:T(8,128)(2,1)S(1)}, bf16[3,40,768]{2,1,0:T(8,128)(2,1)S(1)}, u32[]{:S(2)}, u32[]{:S(2)}) collective-permute-start(bf16[3,40,768]{2,1,0:T(8,128)(2,1)S(1)} %get-tuple-element.229), channel_id=1, source_target_pairs={{0,2},{1,3},{2,0},{3,1},{4,6},{5,7},{6,4},{7,5},{8,10},{9,11},{10,... | collective-permute-start | bytes 552968 | tf_op jit(solution)/shard_map/ppermute | solution.py:520
  77.5 1.7 collective-permute-start.21
  79.2 11.9 %attention.1 = (bf16[4,480,192]{2,1,0:T(8,128)(2,1)}, bf16[4,480,192]{2,1,0:T(8,128)(2,1)}, bf16[4,480,192]{2,1,0:T(8,128)(2,1)}, f32[4,3,480,160]{3,2,1,0:T(8,1...) custom-call(s32[3]{0:T(128)S(1)} %pad_add_fusion.here_ref, ...), custom_call_target="tpu_custom_call" | custom-call | tf_op jit(solution)/shard_map/attention/pallas_call | solution.py:448
  91.2 1.9 collective-permute-done.17
  98.9 20.1 %ffn.1 = (bf16[3,40,768]{2,1,0:T(8,128)(2,1)}, bf16[3,40,768]{2,1,0:T(8,128)(2,1)}, bf16[3,40,768]{2,1,0:T(8,128)(2,1)}, bf16[3,40,768]{2,1,0:T(8,128)(2,1)}, f3...) custom-call(s32[3]{0:T(128)S(1)} %pad_add_fusion.here_ref, ...), custom_call_target="tpu_custom_call" | custom-call | tf_op jit(solution)/shard_map/ffn/pallas_call | solution.py:448
  119.5 7.2 %ffn_back.1 = (f32[480,768]{1,0:T(8,128)}, bf16[480,768]{1,0:T(8,128)(2,1)S(1)}, f32[8,768]{1,0:T(8,128)S(1)}) custom-call(s32[3]{0:T(128)S(1)} %pad_add_fusion.here_ref, bf16[4,480,768]{2,1,0:T(8,128)(2,1)} %get-tuple-element.251.pre_grad_hbm, bf16[768,768]{1,0:T(8,128)(2,1)} %w_in_hbm.3, bf16[3,384,768]{2,1,0:T(8,128)(2,1)S(1)} %bitcast.149, ...), custom_call_target="tpu_custom_call" | custom-call | tf_op jit(solution)/shard_map/ffn_back/pallas_call | solution.py:448
  129.0 1.5 collective-permute-start.27
  130.6 1.6 collective-permute-start.28
  133.2 1.7 collective-permute-start.30
  135.0 18.9 %attention_back.1 = (bf16[4,192,768]{2,1,0:T(8,128)(2,1)}, bf16[4,192,768]{2,1,0:T(8,128)(2,1)}, bf16[2,4,192,768]{3,2,1,0:T(8,128)(2,1)}, f32[16,768]{1,0:T(8,1...) custom-call(s32[3]{0:T(128)S(1)} %pad_add_fusion.here_ref, ...), custom_call_target="tpu_custom_call" | custom-call | tf_op jit(solution)/shard_map/attention_back/pallas_call | solution.py:448
  153.9 2.6 %collective-permute-done.26.refs_3_ = bf16[4,2,96,768]{3,2,1,0:T(8,128)(2,1)S(1)} collective-permute-done((bf16[4,2,96,768]{3,2,1,0:T(8,128)(2,1)S(1)}, bf16[4,2,96,768]{3,2,1,0:T(8,128)(2,1)S(1)}, u32[]{:S(2)}, u32[]{:S(2)}) %collective-permute-start.26) | collective-permute-done | bytes 1179680 | tf_op jit(solution)/shard_map/ppermute | solution.py:520
  157.2 1.6 collective-permute-start.31
  158.8 1.5 collective-permute-start.32
  160.9 2.1 collective-permute-start.35
  163.0 1.5 place.2
  167.0 7.0 %collective-permute-done.36 = f32[16,768]{1,0:T(8,128)S(1)} collective-permute-done((f32[16,768]{1,0:T(8,128)S(1)}, f32[16,768]{1,0:T(8,128)S(1)}, u32[]{:S(2)}, u32[]{:S(2)}) %collective-permute-start.36) | collective-permute-done | bytes 49184 | tf_op jit(solution)/shard_map/ppermute | solution.py:520
  175.0 1.6 collective-permute-start.39
  177.7 2.0 collective-permute-start.41
  180.3 11.8 %collective-permute-done.40 = f32[16,768]{1,0:T(8,128)S(1)} collective-permute-done((f32[16,768]{1,0:T(8,128)S(1)}, f32[16,768]{1,0:T(8,128)S(1)}, u32[]{:S(2)}, u32[]{:S(2)}) %collective-permute-start.40) | collective-permute-done | bytes 49184 | tf_op jit(solution)/shard_map/ppermute | solution.py:520
  193.8 2.5 %collective-permute-start.44 = (bf16[192,768]{1,0:T(8,128)(2,1)S(1)}, bf16[192,768]{1,0:T(8,128)(2,1)S(1)}, u32[]{:S(2)}, u32[]{:S(2)}) collective-permute-start(bf16[192,768]{1,0:T(8,128)(2,1)S(1)} %fusion.1), channel_id=1, source_target_pairs={{0,2},{1,3},{2,0},{3,1},{4,6},{5,7},{6,4},{7,5},{8,10},{9,11},{10,... | collective-permute-start | bytes 884744 | tf_op jit(solution)/shard_map/ppermute | solution.py:520
  197.8 1.4 collective-permute-start.45
  199.2 5.6 %collective-permute-done.45 = f32[16,768]{1,0:T(8,128)S(1)} collective-permute-done((f32[16,768]{1,0:T(8,128)S(1)}, f32[16,768]{1,0:T(8,128)S(1)}, u32[]{:S(2)}, u32[]{:S(2)}) %collective-permute-start.45) | collective-permute-done | bytes 49184 | tf_op jit(solution)/shard_map/ppermute | solution.py:520
  204.7 3.7 %collective-permute-done.44 = bf16[192,768]{1,0:T(8,128)(2,1)S(1)} collective-permute-done((bf16[192,768]{1,0:T(8,128)(2,1)S(1)}, bf16[192,768]{1,0:T(8,128)(2,1)S(1)}, u32[]{:S(2)}, u32[]{:S(2)}) %collective-permute-start.44) | collective-permute-done | bytes 294944 | tf_op jit(solution)/shard_map/ppermute | solution.py:520
  209.1 1.5 collective-permute-start.46
  212.6 1.7 collective-permute-done.46
  214.3 1.5 collective-permute-done.47
  216.4 2.5 %collective-permute-start.51 = (bf16[1,2,1,96,768]{4,3,2,1,0:T(8,128)(2,1)S(1)}, bf16[1,2,1,96,768]{4,3,2,1,0:T(8,128)(2,1)S(1)}, u32[]{:S(2)}, u32[]{:S(2)}) collective-permute-start(bf16[1,2,1,96,768]{4,3,2,1,0:T(8,128)(2,1)S(1)} %pad_maximum_fusion.23), channel_id=1, source_target_pairs={{0,8},{4,12},{8,0},{12,4},{16,24},{20,28},{24,16},{28,20},{1,9},{5... | collective-permute-start | bytes 884744 | tf_op jit(solution)/shard_map/ppermute | solution.py:520
  221.1 1.7 collective-permute-start.53
  222.8 1.7 place.3
  225.2 2.2 collective-permute-done.52
  229.7 1.7 collective-permute-start.56
  231.5 3.1 %unit_grads.1 = (f32[768,768]{1,0:T(8,128)}, f32[768,768]{1,0:T(8,128)}) custom-call(s32[3]{0:T(128)S(1)} %pad_add_fusion.here_ref, bf16[1,384,768]{2,1,0:T(8,128)(2,1)S(1)} %bitcast.173, bf16[1,384,768]{2,1,0:T(8,128)(2,1)S(1)} %bitcast.171, bf16[1,384,768]{2,1,0:T(8,128)(2,1)S(1)} %get-tuple-element.378.in_other, ...), custom_call_target="tpu_custom_call" | custom-call | tf_op jit(solution)/shard_map/unit_grads/pallas_call | solution.py:448
  235.5 2.6 %collective-permute-done.55 = bf16[96,768]{1,0:T(8,128)(2,1)S(1)} collective-permute-done((bf16[96,768]{1,0:T(8,128)(2,1)S(1)}, bf16[96,768]{1,0:T(8,128)(2,1)S(1)}, u32[]{:S(2)}, u32[]{:S(2)}) %collective-permute-start.55) | collective-permute-done | bytes 147488 | tf_op jit(solution)/shard_map/ppermute | solution.py:520
  240.3 2.2 head_grads.1
  (253 shorter events, 45.6 us)
Async XLA Ops:
  1.8 12.4 %collective-permute-start = (bf16[96,768]{1,0:T(8,128)(2,1)S(1)}, bf16[96,768]{1,0:T(8,128)(2,1)S(1)}, u32[]{:S(2)}, u32[]{:S(2)}) collective-permute-start(bf16[96,768]{1,0:T(8,128)(2,1)S(1)} %pad_maximum_fusion.24), channel_id=1, source_target_pairs={{0,1},{1,0},{2,3},{3,2},{4,5},{5,4},{6,7},{7,6},{8,9},{9,8},{10,11... | collective-permute-start | bytes 442376 | tf_op jit(solution)/shard_map/ppermute | solution.py:520
  4.9 14.1 %collective-permute-start.1 = (bf16[96,768]{1,0:T(8,128)(2,1)S(1)}, bf16[96,768]{1,0:T(8,128)(2,1)}, u32[]{:S(2)}, u32[]{:S(2)}) collective-permute-start(bf16[96,768]{1,0:T(8,128)(2,1)S(1)} %pad_maximum_fusion.24), channel_id=1, source_target_pairs={{0,2},{1,3},{2,0},{3,1},{4,6},{5,7},{6,4},{7,5},{8,10},{9,11},{10,... | collective-permute-start | bytes 442376 | tf_op jit(solution)/shard_map/ppermute | solution.py:520
  7.5 11.5 %collective-permute-start.2 = (bf16[96,768]{1,0:T(8,128)(2,1)S(1)}, bf16[96,768]{1,0:T(8,128)(2,1)}, u32[]{:S(2)}, u32[]{:S(2)}) collective-permute-start(bf16[96,768]{1,0:T(8,128)(2,1)S(1)} %pad_maximum_fusion.24), channel_id=1, source_target_pairs={{0,3},{1,2},{2,1},{3,0},{4,7},{5,6},{6,5},{7,4},{8,11},{9,10},{10,... | collective-permute-start | bytes 442376 | tf_op jit(solution)/shard_map/ppermute | solution.py:520
  20.1 14.3 %collective-permute-start.5 = (bf16[3,1,1,48,768]{4,3,0,2,1:T(8,128)(2,1)S(1)}, bf16[3,1,1,48,768]{4,3,0,2,1:T(8,128)(2,1)S(1)}, u32[]{:S(2)}, u32[]{:S(2)}) collective-permute-start(bf16[3,1,1,48,768]{4,3,0,2,1:T(8,128)(2,1)S(1)} %maximum_bitcast_fusion.3), channel_id=1, source_target_pairs={{0,16},{4,20},{8,24},{12,28},{16,0},{20,4},{24,8},{28,12},{1,17},{... | collective-permute-start | bytes 663560 | tf_op jit(solution)/shard_map/ppermute | solution.py:520
  21.7 15.9 %collective-permute-start.3 = (bf16[200,768]{1,0:T(8,128)(2,1)S(1)}, bf16[200,768]{1,0:T(8,128)(2,1)S(1)}, u32[]{:S(2)}, u32[]{:S(2)}) collective-permute-start(bf16[200,768]{1,0:T(8,128)(2,1)S(1)} %concatenate.71), channel_id=1, source_target_pairs={{0,2},{1,3},{2,0},{3,1},{4,6},{5,7},{6,4},{7,5},{8,10},{9,11},{10,... | collective-permute-start | bytes 921608 | tf_op jit(solution)/shard_map/ppermute | solution.py:520
  25.0 9.4 %collective-permute-start.4 = (bf16[3,1,1,48,768]{4,3,0,2,1:T(8,128)(2,1)S(1)}, bf16[3,1,1,48,768]{4,3,0,2,1:T(8,128)(2,1)S(1)}, u32[]{:S(2)}, u32[]{:S(2)}) collective-permute-start(bf16[3,1,1,48,768]{4,3,0,2,1:T(8,128)(2,1)S(1)} %maximum_bitcast_fusion.2), channel_id=1, source_target_pairs={{0,8},{4,12},{8,0},{12,4},{16,24},{20,28},{24,16},{28,20},{1,9},{5... | collective-permute-start | bytes 663560 | tf_op jit(solution)/shard_map/ppermute | solution.py:520
  26.6 7.8 %collective-permute-start.6 = (bf16[3,40,768]{2,1,0:T(8,128)(2,1)}, bf16[3,40,768]{2,1,0:T(8,128)(2,1)S(1)}, u32[]{:S(2)}, u32[]{:S(2)}) collective-permute-start(bf16[3,40,768]{2,1,0:T(8,128)(2,1)} %get-tuple-element.191), channel_id=1, source_target_pairs={{0,1},{1,0},{2,3},{3,2},{4,5},{5,4},{6,7},{7,6},{8,9},{9,8},{10,11... | collective-permute-start | bytes 552968 | tf_op jit(solution)/shard_map/ppermute | solution.py:520
  37.7 18.8 %collective-permute-start.9 = (bf16[2,200,768]{2,1,0:T(8,128)(2,1)S(1)}, bf16[2,200,768]{2,1,0:T(8,128)(2,1)S(1)}, u32[]{:S(2)}, u32[]{:S(2)}) collective-permute-start(bf16[2,200,768]{2,1,0:T(8,128)(2,1)S(1)} %pad_maximum_fusion.11), channel_id=1, source_target_pairs={{0,1},{1,0},{2,3},{3,2},{4,5},{5,4},{6,7},{7,6},{8,9},{9,8},{10,11... | collective-permute-start | bytes 1843208 | tf_op jit(solution)/shard_map/ppermute | solution.py:520
  37.8 17.7 %collective-permute-start.8 = (bf16[3,2,1,48,768]{4,3,0,2,1:T(8,128)(2,1)S(1)}, bf16[3,2,1,48,768]{4,3,0,2,1:T(8,128)(2,1)S(1)}, u32[]{:S(2)}, u32[]{:S(2)}) collective-permute-start(bf16[3,2,1,48,768]{4,3,0,2,1:T(8,128)(2,1)S(1)} %pad_maximum_fusion.18), channel_id=1, source_target_pairs={{0,8},{4,12},{8,0},{12,4},{16,24},{20,28},{24,16},{28,20},{1,9},{5... | collective-permute-start | bytes 1327112 | tf_op jit(solution)/shard_map/ppermute | solution.py:520
  39.5 16.1 %collective-permute-start.7 = (bf16[3,1,2,48,768]{4,3,0,2,1:T(8,128)(2,1)S(1)}, bf16[3,1,2,48,768]{4,3,0,2,1:T(8,128)(2,1)S(1)}, u32[]{:S(2)}, u32[]{:S(2)}) collective-permute-start(bf16[3,1,2,48,768]{4,3,0,2,1:T(8,128)(2,1)S(1)} %pad_maximum_fusion.17), channel_id=1, source_target_pairs={{0,16},{4,20},{8,24},{12,28},{16,0},{20,4},{24,8},{28,12},{1,17},{... | collective-permute-start | bytes 1327112 | tf_op jit(solution)/shard_map/ppermute | solution.py:520
  40.2 15.4 %collective-permute-start.10 = (bf16[3,40,768]{2,1,0:T(8,128)(2,1)S(1)}, bf16[3,40,768]{2,1,0:T(8,128)(2,1)S(1)}, u32[]{:S(2)}, u32[]{:S(2)}) collective-permute-start(bf16[3,40,768]{2,1,0:T(8,128)(2,1)S(1)} %copy-done.16), channel_id=1, source_target_pairs={{0,3},{1,2},{2,1},{3,0},{4,7},{5,6},{6,5},{7,4},{8,11},{9,10},{10,... | collective-permute-start | bytes 552968 | tf_op jit(solution)/shard_map/ppermute | solution.py:520
  56.7 13.5 %collective-permute-start.14 = (bf16[3,192,768]{2,1,0:T(8,128)(2,1)S(1)}, bf16[3,192,768]{2,1,0:T(8,128)(2,1)S(1)}, u32[]{:S(2)}, u32[]{:S(2)}) collective-permute-start(bf16[3,192,768]{2,1,0:T(8,128)(2,1)S(1)} %bitcast.158), channel_id=1, source_target_pairs={{0,4},{4,0},{8,12},{12,8},{16,20},{20,16},{24,28},{28,24},{1,5},{5... | collective-permute-start | bytes 2654216 | tf_op jit(solution)/shard_map/ppermute | solution.py:520
  57.1 13.2 %collective-permute-start.13 = (bf16[3,192,768]{2,1,0:T(8,128)(2,1)S(1)}, bf16[3,192,768]{2,1,0:T(8,128)(2,1)S(1)}, u32[]{:S(2)}, u32[]{:S(2)}) collective-permute-start(bf16[3,192,768]{2,1,0:T(8,128)(2,1)S(1)} %bitcast.161), channel_id=1, source_target_pairs={{0,4},{4,0},{8,12},{12,8},{16,20},{20,16},{24,28},{28,24},{1,5},{5... | collective-permute-start | bytes 2654216 | tf_op jit(solution)/shard_map/ppermute | solution.py:520
  57.7 12.5 %collective-permute-start.12 = (bf16[3,1,1,96,768]{4,3,0,2,1:T(8,128)(2,1)S(1)}, bf16[3,1,1,96,768]{4,3,0,2,1:T(8,128)(2,1)S(1)}, u32[]{:S(2)}, u32[]{:S(2)}) collective-permute-start(bf16[3,1,1,96,768]{4,3,0,2,1:T(8,128)(2,1)S(1)} %maximum_bitcast_fusion.1), channel_id=1, source_target_pairs={{0,16},{4,20},{8,24},{12,28},{16,0},{20,4},{24,8},{28,12},{1,17},{... | collective-permute-start | bytes 1327112 | tf_op jit(solution)/shard_map/ppermute | solution.py:520
  58.3 11.9 %collective-permute-start.11 = (bf16[3,1,1,96,768]{4,3,0,2,1:T(8,128)(2,1)S(1)}, bf16[3,1,1,96,768]{4,3,0,2,1:T(8,128)(2,1)S(1)}, u32[]{:S(2)}, u32[]{:S(2)}) collective-permute-start(bf16[3,1,1,96,768]{4,3,0,2,1:T(8,128)(2,1)S(1)} %maximum_bitcast_fusion), channel_id=1, source_target_pairs={{0,8},{4,12},{8,0},{12,4},{16,24},{20,28},{24,16},{28,20},{1,9},{5... | collective-permute-start | bytes 1327112 | tf_op jit(solution)/shard_map/ppermute | solution.py:520
  59.9 10.3 %collective-permute-start.15 = (bf16[3,40,768]{2,1,0:T(8,128)(2,1)S(1)}, bf16[3,40,768]{2,1,0:T(8,128)(2,1)S(1)}, u32[]{:S(2)}, u32[]{:S(2)}) collective-permute-start(bf16[3,40,768]{2,1,0:T(8,128)(2,1)S(1)} %copy-done.15), channel_id=1, source_target_pairs={{0,2},{1,3},{2,0},{3,1},{4,6},{5,7},{6,4},{7,5},{8,10},{9,11},{10,... | collective-permute-start | bytes 552968 | tf_op jit(solution)/shard_map/ppermute | solution.py:520
  71.0 22.1 %collective-permute-start.17 = (bf16[3,2,1,96,768]{4,3,0,2,1:T(8,128)(2,1)S(1)}, bf16[3,2,1,96,768]{4,3,0,2,1:T(8,128)(2,1)S(1)}, u32[]{:S(2)}, u32[]{:S(2)}) collective-permute-start(bf16[3,2,1,96,768]{4,3,0,2,1:T(8,128)(2,1)S(1)} %pad_maximum_fusion.9), channel_id=1, source_target_pairs={{0,8},{4,12},{8,0},{12,4},{16,24},{20,28},{24,16},{28,20},{1,9},{5... | collective-permute-start | bytes 2654216 | tf_op jit(solution)/shard_map/ppermute | solution.py:520
  72.5 21.7 %collective-permute-start.16 = (bf16[3,1,2,96,768]{4,3,0,2,1:T(8,128)(2,1)S(1)}, bf16[3,1,2,96,768]{4,3,0,2,1:T(8,128)(2,1)S(1)}, u32[]{:S(2)}, u32[]{:S(2)}) collective-permute-start(bf16[3,1,2,96,768]{4,3,0,2,1:T(8,128)(2,1)S(1)} %pad_maximum_fusion.8), channel_id=1, source_target_pairs={{0,16},{4,20},{8,24},{12,28},{16,0},{20,4},{24,8},{28,12},{1,17},{... | collective-permute-start | bytes 2654216 | tf_op jit(solution)/shard_map/ppermute | solution.py:520
  74.8 19.5 %collective-permute-start.19 = (bf16[3,40,768]{2,1,0:T(8,128)(2,1)S(1)}, bf16[3,40,768]{2,1,0:T(8,128)(2,1)S(1)}, u32[]{:S(2)}, u32[]{:S(2)}) collective-permute-start(bf16[3,40,768]{2,1,0:T(8,128)(2,1)S(1)} %get-tuple-element.228), channel_id=1, source_target_pairs={{0,1},{1,0},{2,3},{3,2},{4,5},{5,4},{6,7},{7,6},{8,9},{9,8},{10,11... | collective-permute-start | bytes 552968 | tf_op jit(solution)/shard_map/ppermute | solution.py:520
  74.9 19.4 %collective-permute-start.20 = (bf16[3,40,768]{2,1,0:T(8,128)(2,1)S(1)}, bf16[3,40,768]{2,1,0:T(8,128)(2,1)S(1)}, u32[]{:S(2)}, u32[]{:S(2)}) collective-permute-start(bf16[3,40,768]{2,1,0:T(8,128)(2,1)S(1)} %get-tuple-element.229), channel_id=1, source_target_pairs={{0,2},{1,3},{2,0},{3,1},{4,6},{5,7},{6,4},{7,5},{8,10},{9,11},{10,... | collective-permute-start | bytes 552968 | tf_op jit(solution)/shard_map/ppermute | solution.py:520
  77.5 16.8 %collective-permute-start.21 = (bf16[3,40,768]{2,1,0:T(8,128)(2,1)S(1)}, bf16[3,40,768]{2,1,0:T(8,128)(2,1)S(1)}, u32[]{:S(2)}, u32[]{:S(2)}) collective-permute-start(bf16[3,40,768]{2,1,0:T(8,128)(2,1)S(1)} %get-tuple-element.230), channel_id=1, source_target_pairs={{0,3},{1,2},{2,1},{3,0},{4,7},{5,6},{6,5},{7,4},{8,11},{9,10},{10,... | collective-permute-start | bytes 552968 | tf_op jit(solution)/shard_map/ppermute | solution.py:520
  119.0 7.8 %collective-permute-start.24 = (bf16[4,384,768]{2,1,0:T(8,128)(2,1)}, bf16[4,384,768]{2,1,0:T(8,128)(2,1)S(1)}, u32[]{:S(2)}, u32[]{:S(2)}) collective-permute-start(bf16[4,384,768]{2,1,0:T(8,128)(2,1)} %get-tuple-element.245), channel_id=1, source_target_pairs={{0,4},{4,0},{8,12},{12,8},{16,20},{20,16},{24,28},{28,24},{1,5},{5... | collective-permute-start | bytes 7077896 | tf_op jit(solution)/shard_map/ppermute | solution.py:520
  119.2 8.0 %collective-permute-start.25 = (bf16[4,384,768]{2,1,0:T(8,128)(2,1)}, bf16[4,384,768]{2,1,0:T(8,128)(2,1)S(1)}, u32[]{:S(2)}, u32[]{:S(2)}) collective-permute-start(bf16[4,384,768]{2,1,0:T(8,128)(2,1)} %get-tuple-element.246), channel_id=1, source_target_pairs={{0,4},{4,0},{8,12},{12,8},{16,20},{20,16},{24,28},{28,24},{1,5},{5... | collective-permute-start | bytes 7077896 | tf_op jit(solution)/shard_map/ppermute | solution.py:520
  128.4 28.1 %collective-permute-start.26 = (bf16[4,2,96,768]{3,2,1,0:T(8,128)(2,1)S(1)}, bf16[4,2,96,768]{3,2,1,0:T(8,128)(2,1)S(1)}, u32[]{:S(2)}, u32[]{:S(2)}) collective-permute-start(bf16[4,2,96,768]{3,2,1,0:T(8,128)(2,1)S(1)} %get-tuple-element.265), channel_id=1, source_target_pairs={{0,8},{4,12},{8,0},{12,4},{16,24},{20,28},{24,16},{28,20},{1,9},{5... | collective-permute-start | bytes 3538952 | tf_op jit(solution)/shard_map/ppermute | solution.py:520
  129.0 27.7 %collective-permute-start.27 = (bf16[4,2,96,768]{3,2,1,0:T(8,128)(2,1)S(1)}, bf16[4,2,96,768]{3,2,1,0:T(8,128)(2,1)S(1)}, u32[]{:S(2)}, u32[]{:S(2)}) collective-permute-start(bf16[4,2,96,768]{3,2,1,0:T(8,128)(2,1)S(1)} %get-tuple-element.266), channel_id=1, source_target_pairs={{0,16},{4,20},{8,24},{12,28},{16,0},{20,4},{24,8},{28,12},{1,17},{... | collective-permute-start | bytes 3538952 | tf_op jit(solution)/shard_map/ppermute | solution.py:520
  130.6 23.3 %collective-permute-start.28 = (bf16[3,40,768]{2,1,0:T(8,128)(2,1)S(1)}, bf16[3,40,768]{2,1,0:T(8,128)(2,1)S(1)}, u32[]{:S(2)}, u32[]{:S(2)}) collective-permute-start(bf16[3,40,768]{2,1,0:T(8,128)(2,1)S(1)} %copy-done.29), channel_id=1, source_target_pairs={{0,1},{1,0},{2,3},{3,2},{4,5},{5,4},{6,7},{7,6},{8,9},{9,8},{10,11... | collective-permute-start | bytes 552968 | tf_op jit(solution)/shard_map/ppermute | solution.py:520
  132.1 21.8 %collective-permute-start.29 = (bf16[3,40,768]{2,1,0:T(8,128)(2,1)S(1)}, bf16[3,40,768]{2,1,0:T(8,128)(2,1)S(1)}, u32[]{:S(2)}, u32[]{:S(2)}) collective-permute-start(bf16[3,40,768]{2,1,0:T(8,128)(2,1)S(1)} %copy-done.27), channel_id=1, source_target_pairs={{0,2},{1,3},{2,0},{3,1},{4,6},{5,7},{6,4},{7,5},{8,10},{9,11},{10,... | collective-permute-start | bytes 552968 | tf_op jit(solution)/shard_map/ppermute | solution.py:520
  133.2 20.7 %collective-permute-start.30 = (bf16[3,40,768]{2,1,0:T(8,128)(2,1)S(1)}, bf16[3,40,768]{2,1,0:T(8,128)(2,1)S(1)}, u32[]{:S(2)}, u32[]{:S(2)}) collective-permute-start(bf16[3,40,768]{2,1,0:T(8,128)(2,1)S(1)} %copy-done.26), channel_id=1, source_target_pairs={{0,3},{1,2},{2,1},{3,0},{4,7},{5,6},{6,5},{7,4},{8,11},{9,10},{10,... | collective-permute-start | bytes 552968 | tf_op jit(solution)/shard_map/ppermute | solution.py:520
  156.8 7.7 %collective-permute-start.33 = (bf16[2,4,192,768]{3,2,1,0:T(8,128)(2,1)}, bf16[2,4,192,768]{3,2,1,0:T(8,128)(2,1)S(1)}, u32[]{:S(2)}, u32[]{:S(2)}) collective-permute-start(bf16[2,4,192,768]{3,2,1,0:T(8,128)(2,1)} %get-tuple-element.292), channel_id=1, source_target_pairs={{0,4},{4,0},{8,12},{12,8},{16,20},{20,16},{24,28},{28,24},{1,5},{5... | collective-permute-start | bytes 7077896 | tf_op jit(solution)/shard_map/ppermute | solution.py:520
  157.2 16.8 %collective-permute-start.31 = (bf16[4,1,96,768]{3,2,1,0:T(8,128)(2,1)S(1)}, bf16[4,1,96,768]{3,2,1,0:T(8,128)(2,1)S(1)}, u32[]{:S(2)}, u32[]{:S(2)}) collective-permute-start(bf16[4,1,96,768]{3,2,1,0:T(8,128)(2,1)S(1)} %get-tuple-element.289), channel_id=1, source_target_pairs={{0,16},{4,20},{8,24},{12,28},{16,0},{20,4},{24,8},{28,12},{1,17},{... | collective-permute-start | bytes 1769480 | tf_op jit(solution)/shard_map/ppermute | solution.py:520
  158.8 15.4 %collective-permute-start.32 = (bf16[4,1,96,768]{3,2,1,0:T(8,128)(2,1)S(1)}, bf16[4,1,96,768]{3,2,1,0:T(8,128)(2,1)S(1)}, u32[]{:S(2)}, u32[]{:S(2)}) collective-permute-start(bf16[4,1,96,768]{3,2,1,0:T(8,128)(2,1)S(1)} %get-tuple-element.290), channel_id=1, source_target_pairs={{0,8},{4,12},{8,0},{12,4},{16,24},{20,28},{24,16},{28,20},{1,9},{5... | collective-permute-start | bytes 1769480 | tf_op jit(solution)/shard_map/ppermute | solution.py:520
  160.3 13.7 %collective-permute-start.34 = (bf16[3,40,768]{2,1,0:T(8,128)(2,1)S(1)}, bf16[3,40,768]{2,1,0:T(8,128)(2,1)S(1)}, u32[]{:S(2)}, u32[]{:S(2)}) collective-permute-start(bf16[3,40,768]{2,1,0:T(8,128)(2,1)S(1)} %copy-done.30), channel_id=1, source_target_pairs={{0,1},{1,0},{2,3},{3,2},{4,5},{5,4},{6,7},{7,6},{8,9},{9,8},{10,11... | collective-permute-start | bytes 552968 | tf_op jit(solution)/shard_map/ppermute | solution.py:520
  160.9 13.1 %collective-permute-start.35 = (bf16[3,40,768]{2,1,0:T(8,128)(2,1)S(1)}, bf16[3,40,768]{2,1,0:T(8,128)(2,1)S(1)}, u32[]{:S(2)}, u32[]{:S(2)}) collective-permute-start(bf16[3,40,768]{2,1,0:T(8,128)(2,1)S(1)} %copy-done.28), channel_id=1, source_target_pairs={{0,3},{1,2},{2,1},{3,0},{4,7},{5,6},{6,5},{7,4},{8,11},{9,10},{10,... | collective-permute-start | bytes 552968 | tf_op jit(solution)/shard_map/ppermute | solution.py:520
  164.5 9.5 %collective-permute-start.36 = (f32[16,768]{1,0:T(8,128)S(1)}, f32[16,768]{1,0:T(8,128)S(1)}, u32[]{:S(2)}, u32[]{:S(2)}) collective-permute-start(f32[16,768]{1,0:T(8,128)S(1)} %get-tuple-element.298), channel_id=1, source_target_pairs={{0,2},{1,3},{2,0},{3,1},{4,6},{5,7},{6,4},{7,5},{8,10},{9,11},{10,... | collective-permute-start | bytes 147464 | tf_op jit(solution)/shard_map/ppermute | solution.py:520
  175.0 18.6 %collective-permute-start.39 = (bf16[2,192,768]{2,1,0:T(8,128)(2,1)S(1)}, bf16[2,192,768]{2,1,0:T(8,128)(2,1)S(1)}, u32[]{:S(2)}, u32[]{:S(2)}) collective-permute-start(bf16[2,192,768]{2,1,0:T(8,128)(2,1)S(1)} %pad_maximum_fusion.13), channel_id=1, source_target_pairs={{0,1},{1,0},{2,3},{3,2},{4,5},{5,4},{6,7},{7,6},{8,9},{9,8},{10,11... | collective-permute-start | bytes 1769480 | tf_op jit(solution)/shard_map/ppermute | solution.py:520
  176.7 17.0 %collective-permute-start.37 = (bf16[4,2,48,768]{3,2,1,0:T(8,128)(2,1)S(1)}, bf16[4,2,48,768]{3,2,1,0:T(8,128)(2,1)S(1)}, u32[]{:S(2)}, u32[]{:S(2)}) collective-permute-start(bf16[4,2,48,768]{3,2,1,0:T(8,128)(2,1)S(1)} %get-tuple-element.310), channel_id=1, source_target_pairs={{0,8},{4,12},{8,0},{12,4},{16,24},{20,28},{24,16},{28,20},{1,9},{5... | collective-permute-start | bytes 1769480 | tf_op jit(solution)/shard_map/ppermute | solution.py:520
  177.2 16.5 %collective-permute-start.38 = (bf16[4,2,48,768]{3,2,1,0:T(8,128)(2,1)S(1)}, bf16[4,2,48,768]{3,2,1,0:T(8,128)(2,1)S(1)}, u32[]{:S(2)}, u32[]{:S(2)}) collective-permute-start(bf16[4,2,48,768]{3,2,1,0:T(8,128)(2,1)S(1)} %get-tuple-element.311), channel_id=1, source_target_pairs={{0,16},{4,20},{8,24},{12,28},{16,0},{20,4},{24,8},{28,12},{1,17},{... | collective-permute-start | bytes 1769480 | tf_op jit(solution)/shard_map/ppermute | solution.py:520
  177.7 15.0 %collective-permute-start.41 = (bf16[3,40,768]{2,1,0:T(8,128)(2,1)S(1)}, bf16[3,40,768]{2,1,0:T(8,128)(2,1)S(1)}, u32[]{:S(2)}, u32[]{:S(2)}) collective-permute-start(bf16[3,40,768]{2,1,0:T(8,128)(2,1)S(1)} %copy-done.25), channel_id=1, source_target_pairs={{0,2},{1,3},{2,0},{3,1},{4,6},{5,7},{6,4},{7,5},{8,10},{9,11},{10,... | collective-permute-start | bytes 552968 | tf_op jit(solution)/shard_map/ppermute | solution.py:520
  179.8 12.3 %collective-permute-start.40 = (f32[16,768]{1,0:T(8,128)S(1)}, f32[16,768]{1,0:T(8,128)S(1)}, u32[]{:S(2)}, u32[]{:S(2)}) collective-permute-start(f32[16,768]{1,0:T(8,128)S(1)} %add.145), channel_id=1, source_target_pairs={{0,8},{4,12},{8,0},{12,4},{16,24},{20,28},{24,16},{28,20},{1,9},{5... | collective-permute-start | bytes 147464 | tf_op jit(solution)/shard_map/ppermute | solution.py:520
  193.8 14.7 %collective-permute-start.44 = (bf16[192,768]{1,0:T(8,128)(2,1)S(1)}, bf16[192,768]{1,0:T(8,128)(2,1)S(1)}, u32[]{:S(2)}, u32[]{:S(2)}) collective-permute-start(bf16[192,768]{1,0:T(8,128)(2,1)S(1)} %fusion.1), channel_id=1, source_target_pairs={{0,2},{1,3},{2,0},{3,1},{4,6},{5,7},{6,4},{7,5},{8,10},{9,11},{10,... | collective-permute-start | bytes 884744 | tf_op jit(solution)/shard_map/ppermute | solution.py:520
  196.5 11.9 %collective-permute-start.42 = (bf16[4,1,48,768]{3,2,1,0:T(8,128)(2,1)S(1)}, bf16[4,1,48,768]{3,2,1,0:T(8,128)(2,1)S(1)}, u32[]{:S(2)}, u32[]{:S(2)}) collective-permute-start(bf16[4,1,48,768]{3,2,1,0:T(8,128)(2,1)S(1)} %get-tuple-element.318), channel_id=1, source_target_pairs={{0,16},{4,20},{8,24},{12,28},{16,0},{20,4},{24,8},{28,12},{1,17},{... | collective-permute-start | bytes 884744 | tf_op jit(solution)/shard_map/ppermute | solution.py:520
  197.2 11.2 %collective-permute-start.43 = (bf16[4,1,48,768]{3,2,1,0:T(8,128)(2,1)S(1)}, bf16[4,1,48,768]{3,2,1,0:T(8,128)(2,1)S(1)}, u32[]{:S(2)}, u32[]{:S(2)}) collective-permute-start(bf16[4,1,48,768]{3,2,1,0:T(8,128)(2,1)S(1)} %get-tuple-element.319), channel_id=1, source_target_pairs={{0,8},{4,12},{8,0},{12,4},{16,24},{20,28},{24,16},{28,20},{1,9},{5... | collective-permute-start | bytes 884744 | tf_op jit(solution)/shard_map/ppermute | solution.py:520
  216.4 11.0 %collective-permute-start.51 = (bf16[1,2,1,96,768]{4,3,2,1,0:T(8,128)(2,1)S(1)}, bf16[1,2,1,96,768]{4,3,2,1,0:T(8,128)(2,1)S(1)}, u32[]{:S(2)}, u32[]{:S(2)}) collective-permute-start(bf16[1,2,1,96,768]{4,3,2,1,0:T(8,128)(2,1)S(1)} %pad_maximum_fusion.23), channel_id=1, source_target_pairs={{0,8},{4,12},{8,0},{12,4},{16,24},{20,28},{24,16},{28,20},{1,9},{5... | collective-permute-start | bytes 884744 | tf_op jit(solution)/shard_map/ppermute | solution.py:520
  218.9 8.4 %collective-permute-start.50 = (bf16[1,1,2,96,768]{4,3,2,1,0:T(8,128)(2,1)S(1)}, bf16[1,1,2,96,768]{4,3,2,1,0:T(8,128)(2,1)S(1)}, u32[]{:S(2)}, u32[]{:S(2)}) collective-permute-start(bf16[1,1,2,96,768]{4,3,2,1,0:T(8,128)(2,1)S(1)} %pad_maximum_fusion.22), channel_id=1, source_target_pairs={{0,16},{4,20},{8,24},{12,28},{16,0},{20,4},{24,8},{28,12},{1,17},{... | collective-permute-start | bytes 884744 | tf_op jit(solution)/shard_map/ppermute | solution.py:520
  219.7 7.6 %collective-permute-start.52 = (bf16[96,768]{1,0:T(8,128)(2,1)S(1)}, bf16[96,768]{1,0:T(8,128)(2,1)S(1)}, u32[]{:S(2)}, u32[]{:S(2)}) collective-permute-start(bf16[96,768]{1,0:T(8,128)(2,1)S(1)} %fusion.4), channel_id=1, source_target_pairs={{0,2},{1,3},{2,0},{3,1},{4,6},{5,7},{6,4},{7,5},{8,10},{9,11},{10,... | collective-permute-start | bytes 442376 | tf_op jit(solution)/shard_map/ppermute | solution.py:520
  227.9 7.7 %collective-permute-start.54 = (bf16[96,768]{1,0:T(8,128)(2,1)S(1)}, bf16[96,768]{1,0:T(8,128)(2,1)S(1)}, u32[]{:S(2)}, u32[]{:S(2)}) collective-permute-start(bf16[96,768]{1,0:T(8,128)(2,1)S(1)} %fusion.3), channel_id=1, source_target_pairs={{0,24},{4,28},{8,16},{12,20},{16,8},{20,12},{24,0},{28,4},{1,25},{... | collective-permute-start | bytes 442376 | tf_op jit(solution)/shard_map/ppermute | solution.py:520
  229.0 9.1 %collective-permute-start.55 = (bf16[96,768]{1,0:T(8,128)(2,1)S(1)}, bf16[96,768]{1,0:T(8,128)(2,1)S(1)}, u32[]{:S(2)}, u32[]{:S(2)}) collective-permute-start(bf16[96,768]{1,0:T(8,128)(2,1)S(1)} %fusion.3), channel_id=1, source_target_pairs={{0,16},{4,20},{8,24},{12,28},{16,0},{20,4},{24,8},{28,12},{1,17},{... | collective-permute-start | bytes 442376 | tf_op jit(solution)/shard_map/ppermute | solution.py:520
  229.7 8.5 %collective-permute-start.56 = (bf16[96,768]{1,0:T(8,128)(2,1)S(1)}, bf16[96,768]{1,0:T(8,128)(2,1)S(1)}, u32[]{:S(2)}, u32[]{:S(2)}) collective-permute-start(bf16[96,768]{1,0:T(8,128)(2,1)S(1)} %fusion.3), channel_id=1, source_target_pairs={{0,8},{4,12},{8,0},{12,4},{16,24},{20,28},{24,16},{28,20},{1,9},{5... | collective-permute-start | bytes 442376 | tf_op jit(solution)/shard_map/ppermute | solution.py:520
  (42 other events, 195.0 us)
